TPU v7x, 512 devices: a whole 4x4x16 slice. The times are simulated.
512 devices in a mesh: gy: 32 (over y_hi, z), gz: 16 (over y_lo, x, core).
Axes of the slice: x: 4, y: 4 (y_hi: 2, y_lo: 2; y = y_hi * 2 + y_lo), z: 16, core: 2. Of those that a mesh axis runs over, the one named last changes fastest.
Arguments:
- tokens: bfloat16 [2, 64, 32, 32, 1024], P(None, None, 'gy', 'gz'), may hold values from -64 to 64
- w_qkv: bfloat16 [1024, 3072], P('gy'), may hold values from -2 to 2
- w_out: bfloat16 [1024, 1024], P('gy'), may hold values from -0.1875 to 0.1875
- bias_x: float32 [16, 127], replicated, may hold values from -4 to 4
- bias_y: float32 [16, 63], replicated, may hold values from -4 to 4
- bias_z: float32 [16, 63], replicated, may hold values from -4 to 4
Outputs:
- mixed: bfloat16 [2, 64, 32, 32, 1024], P(None, None, 'gy', 'gz')
All inputs are finite; a program needn't handle non-finite values.
Results may differ from a plain program's by a relative error of at most 0.0083.
Values may be sent and summed in bfloat16 or wider, within the bound.
No kernel may reach another device: no remote copies, remote signals or barrier semaphores. Data moves between devices by JAX's collectives and lax.ppermute only.
A program may use at most 64 MiB of HBM per device.

v0:
```python
import jax
import jax.numpy as jnp
from jax import lax
from jax.sharding import Mesh
from jax.sharding import PartitionSpec as P

HEADS = 16
HEAD = 64
GY = ("gy_0", "gy_1")


einsum_forms = {
    1: ("bxyzhs,bwyzhs->byzhxw", "byzhxw,bwyzhs->bxyzhs"),
    2: ("bxyzhs,bxwzhs->bxzhyw", "bxzhyw,bxwzhs->bxyzhs"),
    3: ("bxyzhs,bxywhs->bxyhzw", "bxyhzw,bxywhs->bxyzhs"),
}


def laid_out(tiles, dim):
    tiles = jnp.moveaxis(tiles, 0, dim)
    shape = tiles.shape
    return tiles.reshape(*shape[:dim], shape[dim] * shape[dim + 1], *shape[dim + 2 :])


def stacked_from(shard, axes, sequence):
    tiles = shard[None]
    for k in sequence:
        tiles = lax.all_gather(tiles, axes[k], axis=0, tiled=True)
    held = [lax.axis_size(axes[k]) for k in reversed(sequence)]
    tiles = tiles.reshape(*held, *shard.shape)
    turned = sorted(range(len(sequence)), key=lambda place: sequence[len(sequence) - 1 - place])
    return tiles.transpose(*turned, *range(len(sequence), tiles.ndim)).reshape(-1, *shard.shape)


def gathered_by_axis(shard, axes, sequence, dim):
    return laid_out(stacked_from(shard, axes, sequence), dim)


def grouped_exchange(shard, axis, split_dim, concat_dim, work, item_dim, out_dim):

    def moved(group):
        return lax.all_to_all(group, axis, split_axis=split_dim, concat_axis=concat_dim, tiled=True)

    items = jax.tree.leaves(shard)[0].shape[item_dim]
    ends = [items * k // 2 for k in range(2 + 1)] if items % 2 == 0 else [0, items]
    groups = [
        jax.tree.map(lambda a: lax.slice_in_dim(a, low, high, axis=item_dim), shard)
        for low, high in zip(ends, ends[1:])
    ]
    arrived = [moved(group) for group in groups]
    made = [work(group) for group in arrived]
    return jax.tree.map(lambda *parts: jnp.concatenate(parts, axis=out_dim), *made)


def norm_rows(tokens):
    values = tokens.astype(jnp.float32)
    center = jnp.mean(values, axis=-1, keepdims=True)
    spread = jnp.mean((values - center) ** 2, axis=-1, keepdims=True)
    return ((values - center) * lax.rsqrt(spread + 1e-05)).astype(jnp.bfloat16)


def rel_bias(table):
    length = (table.shape[1] + 1) // 2
    offsets = (
        lax.broadcasted_iota(jnp.int32, (length, length), 0)
        - lax.broadcasted_iota(jnp.int32, (length, length), 1)
        + length
        - 1
    )
    lookup = (
        offsets[:, :, None] == lax.broadcasted_iota(jnp.int32, (1, 1, 2 * length - 1), 2)
    ).astype(jnp.float32)
    return jnp.einsum("hr,ijr->hij", table, lookup, precision=lax.Precision.HIGHEST)


def attend(qkv, table, axis):
    dims = qkv.shape
    features = dims[-1] // 3
    parts = qkv.reshape(dims[:-1] + (3, HEADS, HEAD))
    query = parts[..., 0, :, :]
    keys = parts[..., 1, :, :]
    values = parts[..., 2, :, :]
    score_form, mix_form = einsum_forms[axis]
    scores = jnp.einsum(score_form, query, keys, preferred_element_type=jnp.float32) * HEAD ** (
        -0.5
    ) + rel_bias(table)
    scores = scores - jnp.max(scores, axis=-1, keepdims=True)
    expo = jnp.exp(scores)
    weights = (expo / jnp.sum(expo, axis=-1, keepdims=True)).astype(jnp.bfloat16)
    mixed = jnp.einsum(mix_form, weights, values, preferred_element_type=jnp.float32)
    return mixed.reshape(dims[:-1] + (features,)).astype(jnp.bfloat16)


def return_y(result):
    return lax.all_to_all(result, GY, split_axis=2, concat_axis=1, tiled=True)


def return_z(result):
    return lax.all_to_all(result, "gz", split_axis=3, concat_axis=1, tiled=True)


def shards(tokens, w_qkv, w_out, bias_x, bias_y, bias_z):
    samples, depth, rows_y, rows_z, features = tokens.shape
    normed = norm_rows(tokens)
    gathered = gathered_by_axis(w_qkv, GY, (0, 1), 0)

    def project(inputs):
        product = jnp.dot(
            inputs.reshape(-1, features), gathered, preferred_element_type=jnp.float32
        )
        return product.astype(jnp.bfloat16).reshape(inputs.shape[:-1] + (3 * features,))

    def z_attention_inputs(lines):
        return return_z(attend(project(lines), bias_z, 3))

    along_x = attend(project(normed), bias_x, 1)
    along_y = return_y(
        attend(
            project(lax.all_to_all(normed, GY, split_axis=1, concat_axis=2, tiled=True)), bias_y, 2
        )
    )
    along_z = grouped_exchange(normed, "gz", 1, 3, z_attention_inputs, 0, 0)
    summed = along_x.astype(jnp.float32) + along_y.astype(jnp.float32) + along_z.astype(jnp.float32)
    summed = summed.astype(jnp.bfloat16).reshape(-1, features)
    residual = tokens.reshape(-1, features).astype(jnp.float32)
    result = residual + jnp.dot(
        summed, gathered_by_axis(w_out, GY, (0, 1), 0), preferred_element_type=jnp.float32
    )
    return result.astype(jnp.bfloat16).reshape(tokens.shape)


def solution(mesh):
    torus = Mesh(mesh.devices.reshape(2, 16, mesh.shape["gz"]), ("gy_0", "gy_1", "gz"))
    in_specs = (P(None, None, GY, "gz", None), P(GY, None), P(GY, None), P(), P(), P())
    out_specs = P(None, None, GY, "gz", None)
    return jax.shard_map(
        shards, mesh=torus, in_specs=in_specs, out_specs=out_specs, check_vma=False
    )
```

profile of v0, /device:TPU:1, one launch (start us, length us, event | category | flops | bytes accessed | tf_op | source)
XLA Modules:
  0.0 258.1 jit_solution(5049971114567313379)
XLA Ops:
  6.5 9.5 %all-gather = bf16[64,3072]{1,0:T(8,128)(2,1)} all-gather(bf16[32,3072]{1,0:T(8,128)(2,1)} %param.7), channel_id=2, replica_groups=mesh['gy_0'=2,'gy_1'=16,'gz'=16] {'gy_0'}, dimensions={0}, use_global_device_ids=true | all-gather | bytes 589824 | tf_op jit(solution)/shard_map/all_gather | solution.py:28
  16.1 1.6 convert_reduce_fusion
  17.7 1.9 multiply_reduce_fusion
  19.7 1.4 multiply_convert_fusion
  21.1 1.4 fusion.45
  22.5 15.3 %all_to_all.84 = bf16[1,64,1,2,1024]{4,3,2,0,1:T(2,128)(2,1)S(1)} all-to-all(bf16[1,64,1,2,1024]{4,3,2,0,1:T(2,128)(2,1)S(1)} %get-tuple-element.17), channel_id=1, replica_groups=mesh['gy_0'=2,'gy_1'=16,'gz'=16] {'gz'}, dimensions={1} | all-to-all | bytes 524288 | tf_op jit(solution)/shard_map/all_to_all | solution.py:42
  37.9 10.5 %all_to_all.85 = bf16[1,64,1,2,1024]{4,3,2,0,1:T(2,128)(2,1)S(1)} all-to-all(bf16[1,64,1,2,1024]{4,3,2,0,1:T(2,128)(2,1)S(1)} %get-tuple-element.18), channel_id=1, replica_groups=mesh['gy_0'=2,'gy_1'=16,'gz'=16] {'gz'}, dimensions={1} | all-to-all | bytes 524288 | tf_op jit(solution)/shard_map/all_to_all | solution.py:42
  48.3 15.8 %all-to-all-start = ((bf16[2,64,1,2,1024]{4,3,2,0,1:T(2,128)(2,1)}), bf16[2,64,1,2,1024]{4,3,2,0,1:T(2,128)(2,1)S(1)}, u32[]{:S(2)}, u32[]{:S(2)}) async-start(bf16[2,64,1,2,1024]{4,3,2,0,1:T(2,128)(2,1)} %multiply_convert_fusion), calls=%async_computation | async-start | bytes 1048576 | tf_op jit(solution)/shard_map/all_to_all | solution.py:119
  64.1 5.4 %all-gather.1 = bf16[64,1024]{1,0:T(8,128)(2,1)} all-gather(bf16[32,1024]{1,0:T(8,128)(2,1)S(1)} %copy-done.12), channel_id=3, replica_groups=mesh['gy_0'=2,'gy_1'=16,'gz'=16] {'gy_0'}, dimensions={0}, use_global_device_ids=true | all-gather | bytes 196608 | tf_op jit(solution)/shard_map/all_gather | solution.py:28
  69.6 1.2 convolution_bitcast_fusion
  71.0 1.2 convolution_bitcast_fusion.1
  72.2 0.9 copy.152
  73.6 28.8 %all-to-all-done = bf16[2,64,1,2,1024]{4,3,2,0,1:T(2,128)(2,1)S(1)} async-done(((bf16[2,64,1,2,1024]{4,3,2,0,1:T(2,128)(2,1)}), bf16[2,64,1,2,1024]{4,3,2,0,1:T(2,128)(2,1)S(1)}, u32[]{:S(2)}, u32[]{:S(2)}) %all-to-all-start) | async-done | bytes 524320 | tf_op jit(solution)/shard_map/all_to_all | solution.py:119
  102.5 0.4 copy.271
  103.0 24.8 %all-gather.5.cloned.1.call-done = bf16[32,32,3072]{2,1,0:T(8,128)(2,1)} async-done(((bf16[2,32,3072]{2,1,0:T(8,128)(2,1)}), bf16[32,32,3072]{2,1,0:T(8,128)(2,1)}) %all-gather.5.cloned.1.call-update) | async-done | bytes 6291472 | tf_op jit(solution)/shard_map/all_gather | solution.py:28
  127.9 3.2 %copy.142 = bf16[2,16,32,3072]{3,2,1,0:T(8,128)(2,1)S(1)} copy(bf16[2,16,32,3072]{3,2,0,1:T(8,128)(2,1)} %bitcast.195) | data formatting | bytes 12582912 | tf_op jit(solution)/shard_map/transpose | solution.py:32
  131.1 2.7 %copy-done.1 = bf16[2,16,32,3072]{3,2,1,0:T(8,128)(2,1)} copy-done((bf16[2,16,32,3072]{3,2,1,0:T(8,128)(2,1)}, bf16[2,16,32,3072]{3,2,1,0:T(8,128)(2,1)S(1)}, u32[]{:S(2)}) %copy-start.1) | copy-done | bytes 6291480
  133.8 1.0 convolution_convert_fusion.3
  134.8 1.0 reshape_reshape.21
  135.8 1.3 fusion.43
  137.1 2.8 %fusion.48 = (f32[4,16,32]{2,1,0:T(8,128)S(1)}, f32[4,16,32,32]{2,3,1,0:T(8,128)}) fusion(bf16[1,4,1,32,1,16,64]{6,5,4,3,1,2,0:T(8,128)(2,1)} %get-tuple-element.13, bf16[1,4,1,32,1,16,64]{6,5,4,3,1,2,0:T(8,128)(2,1)} %get-tuple-element.12, f32[16,32,32]{1,2,0:T(8,128)S(1)} %copy.162), kind=kOutput, calls=%fused_computation.95 | convolution fusion | flops 8650783 | bytes 860160 | tf_op jit(solution)/shard_map/sub | solution.py:87
  140.0 1.6 fusion.20
  141.8 1.0 reshape.299
  142.8 8.2 %all-to-all-start.3 = ((bf16[1,4,1,32,1024]{4,1,2,0,3:T(4,128)(2,1)}), bf16[1,4,1,32,1024]{4,1,2,0,3:T(4,128)(2,1)S(1)}, u32[]{:S(2)}, u32[]{:S(2)}) async-start(bf16[1,4,1,32,1024]{4,1,2,0,3:T(4,128)(2,1)} %reshape.299), calls=%async_computation.3 | async-start | bytes 524288 | tf_op jit(solution)/shard_map/all_to_all | solution.py:99
  151.0 3.8 %convolution_convert_fusion.2 = bf16[128,3072]{1,0:T(8,128)(2,1)S(1)} fusion(bf16[128,1024]{1,0:T(8,128)(2,1)S(1)} %reshape.283, bf16[1024,3072]{1,0:T(8,128)(2,1)} %bitcast.191), kind=kOutput, calls=%fused_computation.6 | convolution fusion | flops 805699584 | bytes 7340032 | tf_op jit(solution)/shard_map/dot_general | solution.py:108
  154.8 1.0 reshape_reshape.22
  155.9 1.2 fusion.44
  157.0 2.8 %fusion.47 = (f32[4,16,32]{2,1,0:T(8,128)S(1)}, f32[4,16,32,32]{2,3,1,0:T(8,128)}) fusion(bf16[1,4,1,32,1,16,64]{6,5,4,3,1,2,0:T(8,128)(2,1)} %get-tuple-element.16, bf16[1,4,1,32,1,16,64]{6,5,4,3,1,2,0:T(8,128)(2,1)S(1)} %get-tuple-element.15, f32[16,32,32]{1,2,0:T(8,128)} %copy-done.11), kind=kOutput, calls=%fused_computation.94 | convolution fusion | flops 8650783 | bytes 860160 | tf_op jit(solution)/shard_map/sub | solution.py:87
  159.8 1.6 fusion.21
  161.6 1.0 reshape.300
  162.6 5.8 %convolution_convert_fusion = bf16[256,3072]{1,0:T(8,128)(2,1)} fusion(bf16[256,1024]{1,0:T(8,128)(2,1)S(1)} %reshape.278, bf16[1024,3072]{1,0:T(8,128)(2,1)} %bitcast.192), kind=kOutput, calls=%fused_computation.4 | convolution fusion | flops 1611399168 | bytes 8388608 | tf_op jit(solution)/shard_map/dot_general | solution.py:108
  168.4 3.6 %reshape_reshape.20 = bf16[2,2,32,2,3,16,64]{6,5,4,3,2,1,0:T(8,128)(2,1)S(1)} reshape(bf16[256,3072]{1,0:T(8,128)(2,1)} %convolution_convert_fusion) | data formatting | bytes 3145728 | tf_op jit(solution)/shard_map/reshape;reshape | solution.py:79
  172.1 2.0 fusion.42
  174.0 4.3 %fusion.46 = (f32[2,2,2,16,32]{4,3,2,1,0:T(8,128)S(1)}, f32[2,2,2,16,32,32]{4,5,3,2,1,0:T(8,128)}) fusion(f32[16,32,32]{1,2,0:T(8,128)} %copy.152, bf16[2,2,32,2,1,16,64]{6,5,4,3,2,1,0:T(8,128)(2,1)} %get-tuple-element.10, bf16[2,2,32,2,1,16,64]{6,5,4,3,2,1,0:T(8,128)(2,1)} %get-tuple-element.9), kind=kOutput, calls=%fused_computation.93 | convolution fusion | flops 17301536 | bytes 1654784 | tf_op jit(solution)/shard_map/sub | solution.py:87
  178.3 5.7 %all-to-all-start.5 = ((bf16[1,4,1,32,1024]{4,1,2,0,3:T(4,128)(2,1)}), bf16[1,4,1,32,1024]{4,1,2,0,3:T(4,128)(2,1)S(1)}, u32[]{:S(2)}, u32[]{:S(2)}) async-start(bf16[1,4,1,32,1024]{4,1,2,0,3:T(4,128)(2,1)} %reshape.300), calls=%async_computation.5 | async-start | bytes 524288 | tf_op jit(solution)/shard_map/all_to_all | solution.py:99
  184.0 2.3 fusion.13
  186.3 0.4 copy.184
  186.8 1.4 reshape.298
  188.1 3.1 %all-to-all-done.5 = bf16[1,4,1,32,1024]{4,1,2,0,3:T(4,128)(2,1)S(1)} async-done(((bf16[1,4,1,32,1024]{4,1,2,0,3:T(4,128)(2,1)}), bf16[1,4,1,32,1024]{4,1,2,0,3:T(4,128)(2,1)S(1)}, u32[]{:S(2)}, u32[]{:S(2)}) %all-to-all-start.5) | async-done | bytes 262176 | tf_op jit(solution)/shard_map/all_to_all | solution.py:99
  191.2 9.9 %all-to-all-start.1 = ((bf16[2,2,32,2,1024]{4,3,1,0,2:T(2,128)(2,1)}), bf16[2,2,32,2,1024]{4,3,1,0,2:T(2,128)(2,1)}, u32[]{:S(2)}, u32[]{:S(2)}) async-start(bf16[2,2,32,2,1024]{4,3,1,0,2:T(2,128)(2,1)} %reshape.298), calls=%async_computation.1 | async-start | bytes 1048576 | tf_op jit(solution)/shard_map/all_to_all | solution.py:95
  201.1 1.5 copy.141
  202.8 3.2 %fusion.19 = f32[16,64,64]{2,0,1:T(8,128)S(1)} fusion(s32[64,64]{1,0:T(8,128)S(1)} %subtract_add_fusion, f32[16,127]{1,0:T(8,128)S(1)} %copy-done), kind=kOutput, calls=%fused_computation.38 | convolution fusion | flops 100397056 | bytes 286656 | tf_op jit(solution)/shard_map/hr,ijr->hij/dot_general | solution.py:73
  206.0 1.1 copy.146
  207.0 0.6 copy_convert_fusion
  207.7 1.7 reshape.289
  209.4 3.2 %copy.178 = bf16[2,16,32,1024]{3,2,1,0:T(8,128)(2,1)} copy(bf16[2,16,32,1024]{3,2,0,1:T(8,128)(2,1)} %bitcast.196) | data formatting | bytes 4194304 | tf_op jit(solution)/shard_map/transpose | solution.py:32
  212.7 5.7 %convolution_convert_fusion.1 = bf16[256,3072]{1,0:T(8,128)(2,1)} fusion(bf16[256,1024]{1,0:T(8,128)(2,1)S(1)} %reshape.273, bf16[1024,3072]{1,0:T(8,128)(2,1)} %bitcast.193), kind=kOutput, calls=%fused_computation.5 | convolution fusion | flops 1611399168 | bytes 8388608 | tf_op jit(solution)/shard_map/dot_general | solution.py:108
  218.4 3.6 %reshape_reshape.19 = bf16[2,64,1,2,3,16,64]{6,5,4,3,1,0,2:T(8,128)(2,1)S(1)} reshape(bf16[256,3072]{1,0:T(8,128)(2,1)} %convolution_convert_fusion.1) | data formatting | bytes 3145728 | tf_op jit(solution)/shard_map/reshape;reshape | solution.py:79
  222.1 2.0 fusion.41
  224.1 3.1 %copy.190 = bf16[2,64,1,2,1,16,64]{1,6,5,3,0,4,2:T(8,128)(2,1)} copy(bf16[2,64,1,2,1,16,64]{6,5,4,3,1,0,2:T(8,128)(2,1)} %get-tuple-element.5) | data formatting | bytes 1048576
  227.1 3.7 %fusion.49 = (f32[2,2,16,64]{3,2,1,0:T(8,128)S(1)}, f32[2,2,16,64,64]{3,4,2,1,0:T(8,128)}) fusion(f32[16,64,64]{1,2,0:T(8,128)} %copy.146, bf16[2,64,1,2,1,16,64]{6,5,4,3,1,0,2:T(8,128)(2,1)S(1)} %copy-done.9, bf16[2,64,1,2,1,16,64]{6,5,4,3,1,0,2:T(8,128)(2,1)S(1)} %copy-done.10), kind=kOutput, calls=%fused_computation.96 | convolution fusion | flops 34603072 | bytes 2375680 | tf_op jit(solution)/shard_map/sub | solution.py:87
  231.1 0.3 concatenate.15
  231.4 1.4 copy.175
  232.8 0.2 copy.174
  233.1 0.3 concatenate.16
  233.4 1.4 copy.176
  234.8 1.6 convert_bitcast_fusion.1
  236.5 1.1 reshape.290
  237.6 2.2 copy.157
  239.9 4.0 %fusion.6 = bf16[2,64,1,2,16,64]{1,5,4,3,0,2:T(8,128)(2,1)} fusion(f32[2,64,1,2,16,64]{1,5,4,3,0,2:T(8,128)} %copy.157, f32[2,2,16,64,64]{3,4,2,1,0:T(8,128)} %get-tuple-element.26, bf16[1,64,1,2,16,64]{1,5,4,3,0,2:T(8,128)(2,1)} %copy.176, bf16[1,64,1,2,16,64]{1,5,4,3,0,2:T(8,128)(2,1)} %copy.175, bf16[2,64,1,2,1,16,64]{1,6,5,3,0,4,2:T(8,128)(2,1)S(1)} %copy-done.5, ...), kind=kOutput, calls=%fused_computation.11 | convolution fusion | flops 35913728 | bytes 3686400 | tf_op jit(solution)/shard_map/byzhxw,bwyzhs->bxyzhs/dot_general | solution.py:90
  243.9 2.7 %copy.177 = bf16[2,64,1,2,16,64]{5,4,3,1,0,2:T(8,128)(2,1)S(1)} copy(bf16[2,64,1,2,16,64]{1,5,4,3,0,2:T(8,128)(2,1)} %fusion.6) | data formatting | bytes 1048576 | tf_op jit(solution)/shard_map/convert_element_type | solution.py:124
  246.6 1.5 convert_element_type.194
  248.1 2.1 fusion.18
  250.3 1.0 reshape.288
  (52 shorter events, 2.2 us)
Async XLA Ops:
  6.5 196.2 %copy-start = (f32[16,127]{1,0:T(8,128)S(1)}, f32[16,127]{1,0:T(8,128)}, u32[]{:S(2)}) copy-start(f32[16,127]{1,0:T(8,128)} %param.9) | copy-start | bytes 24388
  6.5 13.1 %copy-start.2 = (bf16[2,64,1,2,1024]{4,3,2,1,0:T(2,128)(2,1)S(1)}, bf16[2,64,1,2,1024]{4,3,2,1,0:T(2,128)(2,1)}, u32[]{:S(2)}) copy-start(bf16[2,64,1,2,1024]{4,3,2,1,0:T(2,128)(2,1)} %param.6) | copy-start | bytes 1572868
  6.5 121.3 %all-gather.5.cloned.1.call-start = ((), (), s32[]{:S(2)}) async-start(), calls=%async_computation.6 | async-start | bytes 6684672 | tf_op jit(solution)/shard_map/all_gather | solution.py:28
  19.7 44.5 %copy-start.12 = (bf16[32,1024]{1,0:T(8,128)(2,1)S(1)}, bf16[32,1024]{1,0:T(8,128)(2,1)}, u32[]{:S(2)}) copy-start(bf16[32,1024]{1,0:T(8,128)(2,1)} %param.8) | copy-start | bytes 196612
  19.7 49.9 %copy-start.13 = (f32[16,63]{1,0:T(8,128)S(1)}, f32[16,63]{1,0:T(8,128)}, u32[]{:S(2)}) copy-start(f32[16,63]{1,0:T(8,128)} %param.11) | copy-start | bytes 12100
  21.1 49.8 %copy-start.14 = (f32[16,63]{1,0:T(8,128)S(1)}, f32[16,63]{1,0:T(8,128)}, u32[]{:S(2)}) copy-start(f32[16,63]{1,0:T(8,128)} %param.10) | copy-start | bytes 12100
  48.3 54.2 %all-to-all-start = ((bf16[2,64,1,2,1024]{4,3,2,0,1:T(2,128)(2,1)}), bf16[2,64,1,2,1024]{4,3,2,0,1:T(2,128)(2,1)S(1)}, u32[]{:S(2)}, u32[]{:S(2)}) async-start(bf16[2,64,1,2,1024]{4,3,2,0,1:T(2,128)(2,1)} %multiply_convert_fusion), calls=%async_computation | async-start | bytes 1048576 | tf_op jit(solution)/shard_map/all_to_all | solution.py:119
  64.1 145.3 %all-gather.7.cloned.1.call-start = ((), (), s32[]{:S(2)}) async-start(), calls=%async_computation.7 | async-start | bytes 2228224 | tf_op jit(solution)/shard_map/all_gather | solution.py:28
  71.0 66.1 %copy-start.11 = (f32[16,32,32]{1,2,0:T(8,128)}, f32[16,32,32]{1,2,0:T(8,128)S(1)}, u32[]{:S(2)}) copy-start(f32[16,32,32]{1,2,0:T(8,128)S(1)} %copy.162) | copy-start | bytes 196612
  131.1 2.7 %copy-start.1 = (bf16[2,16,32,3072]{3,2,1,0:T(8,128)(2,1)}, bf16[2,16,32,3072]{3,2,1,0:T(8,128)(2,1)S(1)}, u32[]{:S(2)}) copy-start(bf16[2,16,32,3072]{3,2,1,0:T(8,128)(2,1)S(1)} %copy.142) | copy-start | bytes 18874372
  142.8 35.6 %all-to-all-start.3 = ((bf16[1,4,1,32,1024]{4,1,2,0,3:T(4,128)(2,1)}), bf16[1,4,1,32,1024]{4,1,2,0,3:T(4,128)(2,1)S(1)}, u32[]{:S(2)}, u32[]{:S(2)}) async-start(bf16[1,4,1,32,1024]{4,1,2,0,3:T(4,128)(2,1)} %reshape.299), calls=%async_computation.3 | async-start | bytes 524288 | tf_op jit(solution)/shard_map/all_to_all | solution.py:99
  174.0 10.0 %copy-start.8 = (bf16[2,2,32,2,1,16,64]{6,5,4,3,2,1,0:T(8,128)(2,1)S(1)}, bf16[2,2,32,2,1,16,64]{6,5,4,3,2,1,0:T(8,128)(2,1)}, u32[]{:S(2)}) copy-start(bf16[2,2,32,2,1,16,64]{6,5,4,3,2,1,0:T(8,128)(2,1)} %get-tuple-element.8) | copy-start | bytes 1572868
  178.3 12.9 %all-to-all-start.5 = ((bf16[1,4,1,32,1024]{4,1,2,0,3:T(4,128)(2,1)}), bf16[1,4,1,32,1024]{4,1,2,0,3:T(4,128)(2,1)S(1)}, u32[]{:S(2)}, u32[]{:S(2)}) async-start(bf16[1,4,1,32,1024]{4,1,2,0,3:T(4,128)(2,1)} %reshape.300), calls=%async_computation.5 | async-start | bytes 524288 | tf_op jit(solution)/shard_map/all_to_all | solution.py:99
  191.2 15.8 %copy-start.6 = (bf16[1,4,1,32,1024]{4,1,2,0,3:T(4,128)(2,1)}, bf16[1,4,1,32,1024]{4,1,2,0,3:T(4,128)(2,1)S(1)}, u32[]{:S(2)}) copy-start(bf16[1,4,1,32,1024]{4,1,2,0,3:T(4,128)(2,1)S(1)} %all-to-all-done.5) | copy-start | bytes 786436
  191.2 43.6 %all-to-all-start.1 = ((bf16[2,2,32,2,1024]{4,3,1,0,2:T(2,128)(2,1)}), bf16[2,2,32,2,1024]{4,3,1,0,2:T(2,128)(2,1)}, u32[]{:S(2)}, u32[]{:S(2)}) async-start(bf16[2,2,32,2,1024]{4,3,1,0,2:T(2,128)(2,1)} %reshape.298), calls=%async_computation.1 | async-start | bytes 1048576 | tf_op jit(solution)/shard_map/all_to_all | solution.py:95
  201.1 6.0 %copy-start.3 = (bf16[2,64,1,2,1024]{4,3,2,1,0:T(2,128)(2,1)S(1)}, bf16[2,64,1,2,1024]{4,3,2,1,0:T(2,128)(2,1)}, u32[]{:S(2)}) copy-start(bf16[2,64,1,2,1024]{4,3,2,1,0:T(2,128)(2,1)} %param.6) | copy-start | bytes 1572868
  224.0 3.1 %copy-start.9 = (bf16[2,64,1,2,1,16,64]{6,5,4,3,1,0,2:T(8,128)(2,1)S(1)}, bf16[2,64,1,2,1,16,64]{6,5,4,3,1,0,2:T(8,128)(2,1)}, u32[]{:S(2)}) copy-start(bf16[2,64,1,2,1,16,64]{6,5,4,3,1,0,2:T(8,128)(2,1)} %get-tuple-element.6) | copy-start | bytes 1572868
  224.1 3.1 %copy-start.10 = (bf16[2,64,1,2,1,16,64]{6,5,4,3,1,0,2:T(8,128)(2,1)S(1)}, bf16[2,64,1,2,1,16,64]{6,5,4,3,1,0,2:T(8,128)(2,1)}, u32[]{:S(2)}) copy-start(bf16[2,64,1,2,1,16,64]{6,5,4,3,1,0,2:T(8,128)(2,1)} %get-tuple-element.7) | copy-start | bytes 1572868
  230.8 2.0 copy-start.7
  237.6 2.3 copy-start.5
  243.9 4.3 %copy-start.4 = (bf16[2,16,32,1024]{3,2,1,0:T(8,128)(2,1)S(1)}, bf16[2,16,32,1024]{3,2,1,0:T(8,128)(2,1)}, u32[]{:S(2)}) copy-start(bf16[2,16,32,1024]{3,2,1,0:T(8,128)(2,1)} %copy.178) | copy-start | bytes 6291460
Sparse Core Ops, SparseCore 0:
  16.2 111.6 all-gather.4
  129.9 63.7 all-gather.6
where the time goes:
time: 259 us; the launch traced here: 258 us
  waiting for transfers between devices  56.7 us (22%)
  local copies, waits for them, and re-layouts  53 us (20%)
  matrix products  47.2 us (18%)
  blocking collectives  40.7 us (16%)
  starting transfers between devices  39.6 us (15%)
  between operations  13.8 us (5%)
  other arithmetic  7.16 us (3%)
    all_to_all x1, waiting for transfers between devices, shards(): lax.all_to_all(normed, GY, split_axis=1, concat_axis=2, tiled=True)  28.8 us
    all_to_all x2, blocking collectives, moved(): lax.all_to_all(group, axis, split_axis=split_dim, concat_axis=concat_dim,...  25.8 us
    all_gather x2, waiting for transfers between devices, stacked_from(): tiles = lax.all_gather(tiles, axes[k], axis=0, tiled=True)  24.8 us
    dot_general x4, matrix products, project(): jnp.dot(inputs.reshape(-1, features), gathered, preferred_element_type=jn...  16.4 us
    all_to_all x1, starting transfers between devices, shards(): lax.all_to_all(normed, GY, split_axis=1, concat_axis=2, tiled=True)  15.8 us
    all_gather x2, blocking collectives, stacked_from(): tiles = lax.all_gather(tiles, axes[k], axis=0, tiled=True)  14.9 us
    all_to_all x2, starting transfers between devices, return_z(): return lax.all_to_all(result, 'gz', split_axis=3, concat_axis=1, tiled=True)  13.9 us
    sub x4, matrix products, attend(): scores = scores - jnp.max(scores, axis=-1, keepdims=True)  13.6 us
  transfers between devices with their start and end apart: 6, of which 3 were waited for; matrix products, arithmetic and copies ran while one was open for 34% of the time, Pallas kernels for 0%

commit v1 on v0

v1 whole, which is shorter than its diff:
```python
import functools
import jax
import jax.numpy as jnp
from jax import lax
from jax.experimental import pallas as pl
from jax.experimental.pallas import tpu as pltpu
from jax.sharding import Mesh
from jax.sharding import PartitionSpec as P

HEADS = 16
HEAD = 64
PAIRS = HEADS // 2
BLOCK = 128
NEG = -1e30
DIMS = (2, 16, 2, 4, 2)
ALL = ("yh", "z", "yl", "x", "c")
GY = ("yh", "z")
GZ = ("yl", "x", "c")
BF = jnp.bfloat16
F32 = jnp.float32


def index_of(yh, z, yl, x, c):
    return (((yh * DIMS[1] + z) * DIMS[2] + yl) * DIMS[3] + x) * DIMS[4] + c


def every_device():
    for yh in range(DIMS[0]):
        for z in range(DIMS[1]):
            for yl in range(DIMS[2]):
                for x in range(DIMS[3]):
                    for c in range(DIMS[4]):
                        yield yh, z, yl, x, c


def step_x():
    return [
        (index_of(*d), index_of(d[0], d[1], d[2], (d[3] + (1 - 2 * d[4])) % DIMS[3], d[4]))
        for d in every_device()
    ]


def step_y():
    pairs = []
    for yh, z, yl, x, c in every_device():
        y = (yh * 2 + yl + (1 - 2 * c)) % 4
        pairs.append((index_of(yh, z, yl, x, c), index_of(y // 2, z, y % 2, x, c)))
    return pairs


def iota(shape, dim):
    return lax.broadcasted_iota(jnp.int32, shape, dim)


def line_rows(axis, i):
    if axis == 1:
        return (i // 128) * 128 + (i % 64) * 2 + (i // 64) % 2
    if axis == 2:
        return (i % 32) * 8 + i // 32
    return ((i % 32) // 2) * 16 + (i // 32) * 2 + i % 2


def norm_kernel(tokens_ref, out_ref):
    values = tokens_ref[...].astype(F32)
    center = jnp.mean(values, axis=-1, keepdims=True)
    values = values - center
    spread = jnp.mean(values * values, axis=-1, keepdims=True)
    out_ref[...] = (values * lax.rsqrt(spread + 1e-05)).astype(BF)


def bias_kernel(length, table_ref, out_ref):
    lanes = iota((length, BLOCK), 1) // length
    for head in range(HEADS):
        row = jnp.broadcast_to(table_ref[head : head + 1, :], (length, BLOCK))
        for place in range(BLOCK // length):
            shift = (place * length - length + 1) % BLOCK
            turned = pltpu.roll(row, shift, 1, stride=1, stride_axis=0)
            out_ref[
                head // 2,
                place * length : (place + 1) * length,
                (head % 2) * BLOCK : (head % 2 + 1) * BLOCK,
            ] = jnp.where(lanes == place, turned, NEG)


def attend_kernel(axis, groups, pair_ref, tokens_ref, *refs):
    weight_refs = refs[: 2 * groups]
    bias_ref, out_ref, lines_ref = refs[2 * groups :]
    step = pl.program_id(0)
    rows = tokens_ref.shape[0]
    order = line_rows(axis, iota((rows, rows), 0)) == iota((rows, rows), 1)

    @pl.when(step == 0)
    def _():
        turn = order.astype(F32).astype(BF)
        lines_ref[...] = jnp.dot(turn, tokens_ref[...], preferred_element_type=F32).astype(BF)

    own, other = weight_refs[0][0], weight_refs[1][0]
    if groups == 2:
        first = step < 4
        own = jnp.where(first, own, weight_refs[2][0])
        other = jnp.where(first, other, weight_refs[3][0])
    core = pair_ref[pair_ref.shape[0] - 1]
    low = jnp.where(core == 0, own, other)
    high = jnp.where(core == 0, other, own)
    depth, width = low.shape
    weights = jnp.stack(
        [low.reshape(depth // 16, 16, width), high.reshape(depth // 16, 16, width)], axis=1
    ).reshape(2 * depth, width)
    qkv = jnp.dot(lines_ref[...], weights, preferred_element_type=F32).astype(BF)
    left = iota((BLOCK, BLOCK), 1) < HEAD
    zero = jnp.zeros((BLOCK, BLOCK), BF)
    mixed = []
    for start in range(0, rows, BLOCK):
        part = qkv[start : start + BLOCK]
        q, k, v = part[:, :BLOCK], part[:, BLOCK : 2 * BLOCK], part[:, 2 * BLOCK :]
        keys = jnp.concatenate([jnp.where(left, k, zero), jnp.where(left, zero, k)], axis=0)
        values = jnp.concatenate([jnp.where(left, v, zero), jnp.where(left, zero, v)], axis=0)
        scores = lax.dot_general(q, keys, (((1,), (1,)), ((), ())), preferred_element_type=F32)
        scores = scores * HEAD ** (-0.5) + bias_ref[0]
        probs = []
        for half in range(2):
            s = scores[:, half * BLOCK : (half + 1) * BLOCK]
            e = jnp.exp(s - jnp.max(s, axis=-1, keepdims=True))
            probs.append((e / jnp.sum(e, axis=-1, keepdims=True)).astype(BF))
        probs = jnp.concatenate(probs, axis=1)
        mixed.append(jnp.dot(probs, values, preferred_element_type=F32).astype(BF))
    mixed = jnp.concatenate(mixed, axis=0)
    back = (line_rows(axis, iota((rows, rows), 1)) == iota((rows, rows), 0)).astype(F32).astype(BF)
    out_ref[...] = jnp.dot(back, mixed, preferred_element_type=F32).astype(BF)


def attend(axis, tokens, weights, bias, pairs, columns, core):
    groups = len(weights) // 2
    steps = 4 * groups
    rows, features = tokens.shape
    half, width = weights[0].shape[1:]
    specs = [pl.BlockSpec((rows, features), lambda s, p: (0, 0))]
    for group in range(groups):

        def own_slot(s, p, group=group):
            return (jnp.clip(s - 4 * group, 0, 3), 0, 0)

        def other_slot(s, p, group=group):
            return ((4 - jnp.clip(s - 4 * group, 0, 3)) % 4, 0, 0)

        specs.append(pl.BlockSpec((1, half, width), own_slot))
        specs.append(pl.BlockSpec((1, half, width), other_slot))
    specs.append(pl.BlockSpec((1, BLOCK, 2 * BLOCK), lambda s, p: (p[s], 0, 0)))
    scalars = jnp.concatenate([pairs, columns, core[None]]).astype(jnp.int32)
    return pl.pallas_call(
        functools.partial(attend_kernel, axis, groups),
        out_shape=jax.ShapeDtypeStruct((rows, steps * BLOCK), BF),
        grid_spec=pltpu.PrefetchScalarGridSpec(
            num_scalar_prefetch=1,
            grid=(steps,),
            in_specs=specs,
            out_specs=pl.BlockSpec((rows, BLOCK), lambda s, p: (0, p[steps + s])),
            scratch_shapes=[pltpu.VMEM((rows, features), BF)],
        ),
        compiler_params=pltpu.CompilerParams(vmem_limit_bytes=40 * 2**20),
        cost_estimate=pl.CostEstimate(
            flops=2 * rows * features * 3 * BLOCK * steps,
            bytes_accessed=steps * 1024 * 1024,
            transcendentals=steps * rows * 2 * BLOCK,
        ),
        name=f"attend_{axis}_{groups}",
    )(scalars, tokens, *weights, bias)


def final_kernel(side_ref, tokens_ref, x_ref, ya_ref, yb_ref, z_ref, w_ref, out_ref):
    side = side_ref[0]
    ya, yb = ya_ref[...], yb_ref[...]
    y = jnp.concatenate([jnp.where(side == 0, ya, yb), jnp.where(side == 0, yb, ya)], axis=1)
    summed = x_ref[...].astype(F32) + y.astype(F32) + z_ref[...].astype(F32)
    result = jnp.dot(summed.astype(BF), w_ref[...], preferred_element_type=F32)
    out_ref[...] = (tokens_ref[...].astype(F32) + result).astype(BF)


def whole(kernel, out, name, scalars=0):
    vmem = pl.BlockSpec(memory_space=pltpu.VMEM)
    smem = pl.BlockSpec(memory_space=pltpu.SMEM)

    def call(*args):
        return pl.pallas_call(
            kernel,
            out_shape=out,
            in_specs=[smem] * scalars + [vmem] * (len(args) - scalars),
            out_specs=vmem,
            compiler_params=pltpu.CompilerParams(vmem_limit_bytes=40 * 2**20),
            name=name,
        )(*args)

    return call


def reversed_table(table):
    turned = table[:, ::-1]
    return jnp.pad(turned, ((0, 0), (0, BLOCK - turned.shape[1])))


def bias_blocks(table):
    length = (table.shape[1] + 1) // 2
    shape = jax.ShapeDtypeStruct((PAIRS, BLOCK, 2 * BLOCK), F32)
    return whole(functools.partial(bias_kernel, length), shape, f"bias_{length}")(
        reversed_table(table)
    )


def exchange(array, axes):
    return lax.all_to_all(array, axes, split_axis=0, concat_axis=0, tiled=True)


def swap_cores(array):
    return lax.ppermute(array, "c", [(0, 1), (1, 0)])


def shards(tokens, w_qkv, w_out, bias_x, bias_y, bias_z):
    features = tokens.shape[-1]
    shape = tokens.shape
    yl, x, c = lax.axis_index("yl"), lax.axis_index("x"), lax.axis_index("c")
    pair = yl * DIMS[3] + x

    depth = w_qkv.shape[0] // 2
    mine = jnp.concatenate(
        [
            lax.dynamic_slice(w_qkv, (c * depth, part * features + pair * BLOCK), (depth, BLOCK))
            for part in range(3)
        ],
        axis=1,
    )
    peers = DIMS[0] * DIMS[1]
    piece = exchange(jnp.broadcast_to(mine[None], (peers, *mine.shape)), GY)
    piece = piece.reshape(peers * depth, 3 * BLOCK)

    flat = tokens.reshape(-1, features)
    rows = flat.shape[0]
    normed = whole(norm_kernel, jax.ShapeDtypeStruct(flat.shape, BF), "norm")(flat)
    y_lines = exchange(normed.reshape(peers, -1, features), GY).reshape(rows, features)
    zs = DIMS[2] * DIMS[3] * DIMS[4]
    z_lines = exchange(normed.reshape(zs, -1, features), GZ).reshape(rows, features)

    around_x = functools.partial(lax.ppermute, axis_name=ALL, perm=step_x())
    around_y = functools.partial(lax.ppermute, axis_name=ALL, perm=step_y())
    held = [piece]
    for _ in range(DIMS[3] - 1):
        held.append(around_x(held[-1]))
    across = [around_y(p) for p in held]
    own_a = jnp.stack(held)
    own_b = jnp.stack(across)
    other_a = swap_cores(own_a)
    other_b = swap_cores(own_b)

    columns = (x - jnp.arange(4) * (1 - 2 * c)) % DIMS[3]
    pairs_a = yl * 4 + columns
    pairs_b = (1 - yl) * 4 + columns
    pairs = jnp.concatenate([pairs_a, pairs_b])

    blocks_x = bias_blocks(bias_x)
    blocks_y = bias_blocks(bias_y)
    blocks_z = bias_blocks(bias_z)

    w_half = lax.dynamic_slice(
        w_out, (0, c * (features // 2)), (w_out.shape[0], features // 2)
    )
    w_half = lax.all_gather(w_half, "z", axis=0, tiled=True)
    w_half = lax.all_gather(w_half, "yh", axis=0, tiled=True)
    w_other = swap_cores(w_half)
    w_full = jnp.concatenate(
        [jnp.where(c == 0, w_half, w_other), jnp.where(c == 0, w_other, w_half)], axis=1
    )

    y_a = attend(2, y_lines, (own_a, other_a), blocks_y, pairs_a, columns, c)
    y_a = exchange(y_a.reshape(peers, -1, features // 2), GY).reshape(rows, -1)
    y_b = attend(2, y_lines, (own_b, other_b), blocks_y, pairs_b, columns, c)
    y_b = exchange(y_b.reshape(peers, -1, features // 2), GY).reshape(rows, -1)
    every = (own_a, other_a, own_b, other_b)
    z = attend(3, z_lines, every, blocks_z, pairs, pairs, c)
    z = exchange(z.reshape(zs, -1, features), GZ).reshape(rows, features)
    along_x = attend(1, normed, every, blocks_x, pairs, pairs, c)
    mixed = whole(final_kernel, jax.ShapeDtypeStruct(flat.shape, BF), "mix", 1)(
        yl[None], flat, along_x, y_a, y_b, z, w_full
    )
    return mixed.reshape(shape)


def solution(mesh):
    torus = Mesh(mesh.devices.reshape(DIMS), ALL)
    in_specs = (P(None, None, GY, GZ, None), P(GY, None), P(GY, None), P(), P(), P())
    return jax.shard_map(
        shards, mesh=torus, in_specs=in_specs, out_specs=in_specs[0], check_vma=False
    )
```

time: 259 us -> 266 us (1.027)
  the two profiles are of different devices: /device:TPU:1 before, /device:TPU:2 now
where the time goes in v1:
time: 266 us; the launch traced here: 264 us
  blocking collectives  86.4 us (32%)
  starting transfers between devices  65.7 us (25%)
  Pallas kernels  41.1 us (15%)
  waiting for transfers between devices  37 us (14%)
  local copies, waits for them, and re-layouts  15.4 us (6%)
  between operations  13.8 us (5%)
  other arithmetic  4.93 us (2%)
    all_to_all x1, blocking collectives, exchange(): return lax.all_to_all(array, axes, split_axis=0, concat_axis=0, tiled=True)  46.6 us
    all_gather x1, blocking collectives, shards(): w_half = lax.all_gather(w_half, 'z', axis=0, tiled=True)  39.8 us
    pallas_call x4, Pallas kernels, attend(): pl.pallas_call(functools.partial(attend_kernel, axis, groups), out_shape=...  37.2 us
    all_to_all x5, starting transfers between devices, exchange(): return lax.all_to_all(array, axes, split_axis=0, concat_axis=0, tiled=True)  35 us
    all_to_all x5, waiting for transfers between devices, exchange(): return lax.all_to_all(array, axes, split_axis=0, concat_axis=0, tiled=True)  19.6 us
    unnamed x40, local copies, waits for them, and re-layouts  13.1 us
    ppermute x3, waiting for transfers between devices, shards(): held.append(around_x(held[-1]))  12.5 us
    ppermute x4, starting transfers between devices, shards(): across = [around_y(p) for p in held]  12.3 us
  transfers between devices with their start and end apart: 16, of which 7 were waited for; matrix products, arithmetic and copies ran while one was open for 2% of the time, Pallas kernels for 15%

profile of v1, /device:TPU:2, one launch (start us, length us, event | category | flops | bytes accessed | tf_op | source)
XLA Modules:
  0.0 264.4 jit_solution(2456198915977136376)
XLA Ops:
  6.5 0.8 fusion.1
  7.4 46.6 %all_to_all.30 = bf16[32,16,384]{2,1,0:T(8,128)(2,1)S(1)} all-to-all(bf16[32,16,384]{2,1,0:T(8,128)(2,1)S(1)} %broadcast_in_dim.8), channel_id=1, replica_groups=mesh['yh'=2,'z'=16,'yl'=2,'x'=4,'c'=2] {'yh','z'}, dimensions={0} | all-to-all | bytes 786432 | tf_op jit(solution)/shard_map/all_to_all | solution.py:210
  53.9 3.4 %collective-permute-start = (bf16[512,384]{1,0:T(8,128)(2,1)S(1)}, bf16[512,384]{1,0:T(8,128)(2,1)S(1)}, u32[]{:S(2)}, u32[]{:S(2)}) collective-permute-start(bf16[512,384]{1,0:T(8,128)(2,1)S(1)} %bitcast.27), channel_id=1, source_target_pairs={{0,2},{1,7},{2,4},{3,1},{4,6},{5,3},{6,0},{7,5},{8,10},{9,15},{10,... | collective-permute-start | bytes 1179656 | tf_op jit(solution)/shard_map/ppermute | solution.py:246
  57.3 6.3 %collective-permute-done = bf16[512,384]{1,0:T(8,128)(2,1)S(1)} collective-permute-done((bf16[512,384]{1,0:T(8,128)(2,1)S(1)}, bf16[512,384]{1,0:T(8,128)(2,1)S(1)}, u32[]{:S(2)}, u32[]{:S(2)}) %collective-permute-start) | collective-permute-done | bytes 393248 | tf_op jit(solution)/shard_map/ppermute | solution.py:246
  63.6 3.4 %collective-permute-start.1 = (bf16[512,384]{1,0:T(8,128)(2,1)S(1)}, bf16[512,384]{1,0:T(8,128)(2,1)S(1)}, u32[]{:S(2)}, u32[]{:S(2)}) collective-permute-start(bf16[512,384]{1,0:T(8,128)(2,1)S(1)} %collective-permute-done), channel_id=1, source_target_pairs={{0,2},{1,7},{2,4},{3,1},{4,6},{5,3},{6,0},{7,5},{8,10},{9,15},{10,... | collective-permute-start | bytes 1179656 | tf_op jit(solution)/shard_map/ppermute | solution.py:246
  67.0 6.3 %collective-permute-done.1 = bf16[512,384]{1,0:T(8,128)(2,1)S(1)} collective-permute-done((bf16[512,384]{1,0:T(8,128)(2,1)S(1)}, bf16[512,384]{1,0:T(8,128)(2,1)S(1)}, u32[]{:S(2)}, u32[]{:S(2)}) %collective-permute-start.1) | collective-permute-done | bytes 393248 | tf_op jit(solution)/shard_map/ppermute | solution.py:246
  73.3 3.4 %collective-permute-start.2 = (bf16[512,384]{1,0:T(8,128)(2,1)S(1)}, bf16[512,384]{1,0:T(8,128)(2,1)S(1)}, u32[]{:S(2)}, u32[]{:S(2)}) collective-permute-start(bf16[512,384]{1,0:T(8,128)(2,1)S(1)} %collective-permute-done.1), channel_id=1, source_target_pairs={{0,2},{1,7},{2,4},{3,1},{4,6},{5,3},{6,0},{7,5},{8,10},{9,15},{10,... | collective-permute-start | bytes 1179656 | tf_op jit(solution)/shard_map/ppermute | solution.py:246
  76.7 0.2 reshape.40.tokens_ref
  76.9 0.0 copy-start.4
  76.9 1.1 norm.1.tokens_ref
  78.0 6.1 %all-to-all-start.4 = ((bf16[16,16,1024]{2,1,0:T(8,128)(2,1)}), bf16[16,16,1024]{2,1,0:T(8,128)(2,1)S(1)}, u32[]{:S(2)}, u32[]{:S(2)}) async-start(bf16[16,16,1024]{2,1,0:T(8,128)(2,1)} %bitcast.17), calls=%async_computation.4 | async-start | bytes 1048576 | tf_op jit(solution)/shard_map/all_to_all | solution.py:210
  84.1 3.4 %collective-permute-start.4 = (bf16[512,384]{1,0:T(8,128)(2,1)S(1)}, bf16[512,384]{1,0:T(8,128)(2,1)}, u32[]{:S(2)}, u32[]{:S(2)}) collective-permute-start(bf16[512,384]{1,0:T(8,128)(2,1)S(1)} %bitcast.28), channel_id=1, source_target_pairs={{0,8},{1,265},{2,10},{3,267},{4,12},{5,269},{6,14},{7,271},{8,256}... | collective-permute-start | bytes 1179656 | tf_op jit(solution)/shard_map/ppermute | solution.py:247
  87.5 1.9 collective-permute-start.5
  89.4 3.4 %collective-permute-start.6 = (bf16[512,384]{1,0:T(8,128)(2,1)S(1)}, bf16[512,384]{1,0:T(8,128)(2,1)}, u32[]{:S(2)}, u32[]{:S(2)}) collective-permute-start(bf16[512,384]{1,0:T(8,128)(2,1)S(1)} %collective-permute-done.1), channel_id=1, source_target_pairs={{0,8},{1,265},{2,10},{3,267},{4,12},{5,269},{6,14},{7,271},{8,256}... | collective-permute-start | bytes 1179656 | tf_op jit(solution)/shard_map/ppermute | solution.py:247
  92.8 3.6 %collective-permute-start.7 = (bf16[512,384]{1,0:T(8,128)(2,1)S(1)}, bf16[512,384]{1,0:T(8,128)(2,1)}, u32[]{:S(2)}, u32[]{:S(2)}) collective-permute-start(bf16[512,384]{1,0:T(8,128)(2,1)S(1)} %collective-permute-done.2), channel_id=1, source_target_pairs={{0,8},{1,265},{2,10},{3,267},{4,12},{5,269},{6,14},{7,271},{8,256}... | collective-permute-start | bytes 1179656 | tf_op jit(solution)/shard_map/ppermute | solution.py:247
  96.5 4.7 %all-to-all-start.1 = ((bf16[32,8,1024]{2,1,0:T(8,128)(2,1)}), bf16[32,8,1024]{2,1,0:T(8,128)(2,1)}, u32[]{:S(2)}, u32[]{:S(2)}) async-start(bf16[32,8,1024]{2,1,0:T(8,128)(2,1)} %bitcast.11), calls=%async_computation.1 | async-start | bytes 1048576 | tf_op jit(solution)/shard_map/all_to_all | solution.py:210
  101.2 0.0 all-gather.2.cloned.1.call-start
  101.3 0.2 pad_maximum_fusion.1.refs_0_
  101.5 1.9 collective-permute-start.3
  103.5 0.0 collective-permute-done.5
  103.5 0.2 collective-permute-done.6
  103.7 4.6 %collective-permute-done.7 = bf16[512,384]{1,0:T(8,128)(2,1)} collective-permute-done((bf16[512,384]{1,0:T(8,128)(2,1)S(1)}, bf16[512,384]{1,0:T(8,128)(2,1)}, u32[]{:S(2)}, u32[]{:S(2)}) %collective-permute-start.7) | collective-permute-done | bytes 393248 | tf_op jit(solution)/shard_map/ppermute | solution.py:247
  108.3 1.6 pad_maximum_fusion.2.refs_2_.refs_0_
  109.9 4.1 %collective-permute-start.8 = (bf16[4,512,384]{2,1,0:T(8,128)(2,1)S(1)}, bf16[4,512,384]{2,1,0:T(8,128)(2,1)}, u32[]{:S(2)}, u32[]{:S(2)}) collective-permute-start(bf16[4,512,384]{2,1,0:T(8,128)(2,1)S(1)} %pad_maximum_fusion.2.refs_2_.refs_0_), channel_id=1, source_target_pairs={{0,1},{1,0},{2,3},{3,2},{4,5},{5,4},{6,7},{7,6},{8,9},{9,8},{10,11... | collective-permute-start | bytes 4718600 | tf_op jit(solution)/shard_map/ppermute | solution.py:214
  114.1 39.8 %all_gather.6 = bf16[512,512]{1,0:T(8,128)(2,1)} all-gather(bf16[32,512]{1,0:T(8,128)(2,1)S(1)} %constant_dynamic-slice_fusion), channel_id=1, replica_groups=mesh['yh'=2,'z'=16,'yl'=2,'x'=4,'c'=2] {'z'}, dimensions={0}, use_global_device_ids=true | all-gather | bytes 557056 | tf_op jit(solution)/shard_map/all_gather | solution.py:265
  153.9 0.0 all-gather.2.cloned.1.call-update
  154.0 0.1 rev.11
  154.1 0.3 bias_32.3.refs_4_
  154.4 1.0 copy-done.6
  155.4 0.1 concatenate.19.pair_ref
  155.5 1.2 copy-done.7
  156.7 1.0 copy-done.11
  157.8 11.8 %attend_3_2.1 = bf16[256,1024]{1,0:T(8,128)(2,1)S(1)} custom-call(s32[17]{0:T(128)S(1)} %concatenate.19.pair_ref, bf16[256,1024]{1,0:T(8,128)(2,1)S(1)} %bitcast.22, bf16[4,512,384]{2,1,0:T(8,128)(2,1)S(1)} %pad_maximum_fusion.1.refs_0_, bf16[4,512,384]{2,1,0:T(8,128)(2,1)} %collective-permute-done.3.refs_1_, ...), custom_call_target="tpu_custom_call" | custom-call | flops 1610612736 | bytes 8388608 | tf_op jit(solution)/shard_map/attend_3_2/pallas_call | solution.py:150
  169.5 0.8 copy-done.12
  170.3 0.0 all-to-all-done.1
  170.3 5.6 %all-to-all-start.5 = ((bf16[16,16,1024]{2,1,0:T(8,128)(2,1)}), bf16[16,16,1024]{2,1,0:T(8,128)(2,1)}, u32[]{:S(2)}, u32[]{:S(2)}) async-start(bf16[16,16,1024]{2,1,0:T(8,128)(2,1)} %bitcast.23), calls=%async_computation.5 | async-start | bytes 1048576 | tf_op jit(solution)/shard_map/all_to_all | solution.py:210
  175.9 0.1 rev.10
  176.0 0.3 bias_32.2.refs_2_
  176.3 0.1 add_add_fusion.1
  176.4 6.8 %attend_2_1.2 = bf16[256,512]{1,0:T(8,128)(2,1)S(1)} custom-call(s32[9]{0:T(128)S(1)} %get-tuple-element.13.pair_ref, bf16[256,1024]{1,0:T(8,128)(2,1)} %bitcast.12.tokens_ref, bf16[4,512,384]{2,1,0:T(8,128)(2,1)S(1)} %pad_maximum_fusion.1.refs_0_, bf16[4,512,384]{2,1,0:T(8,128)(2,1)} %collective-permute-done.3.refs_1_, f32[8,128,256]{2,1,0:T(8,128)S(1)} %bias_32.2.refs_2_), custom_call_target="tpu_custom_call" | custom-call | flops 805306368 | bytes 4194304 | tf_op jit(solution)/shard_map/attend_2_1/pallas_call | solution.py:150
  183.2 1.1 copy-done.1
  184.2 0.7 copy-done.14
  184.9 0.6 all-to-all-done.5
  185.5 14.0 %all-to-all-start.2 = ((bf16[32,8,512]{2,1,0:T(8,128)(2,1)}), bf16[32,8,512]{2,1,0:T(8,128)(2,1)S(1)}, u32[]{:S(2)}, u32[]{:S(2)}) async-start(bf16[32,8,512]{2,1,0:T(8,128)(2,1)} %bitcast.26), calls=%async_computation.2 | async-start | bytes 524288 | tf_op jit(solution)/shard_map/all_to_all | solution.py:210
  199.5 0.0 all-gather.2.cloned.1.call-done
  199.5 2.2 collective-permute-start.9
  201.7 1.2 copy-done.2
  202.9 6.8 %attend_2_1.3 = bf16[256,512]{1,0:T(8,128)(2,1)S(1)} custom-call(s32[9]{0:T(128)S(1)} %get-tuple-element.12.pair_ref, bf16[256,1024]{1,0:T(8,128)(2,1)} %bitcast.12.tokens_ref, bf16[4,512,384]{2,1,0:T(8,128)(2,1)S(1)} %pad_maximum_fusion.2.refs_2_.refs_0_, bf16[4,512,384]{2,1,0:T(8,128)(2,1)} %collective-permute-done.8.refs_3_.refs_1_, ...), custom_call_target="tpu_custom_call" | custom-call | flops 805306368 | bytes 4194304 | tf_op jit(solution)/shard_map/attend_2_1/pallas_call | solution.py:150
  209.7 0.7 copy-done.13
  210.4 13.5 %all-to-all-done.2 = bf16[32,8,512]{2,1,0:T(8,128)(2,1)S(1)} async-done(((bf16[32,8,512]{2,1,0:T(8,128)(2,1)}), bf16[32,8,512]{2,1,0:T(8,128)(2,1)S(1)}, u32[]{:S(2)}, u32[]{:S(2)}) %all-to-all-start.2) | async-done | bytes 262176 | tf_op jit(solution)/shard_map/all_to_all | solution.py:210
  223.9 4.6 %all-to-all-start.3 = ((bf16[32,8,512]{2,1,0:T(8,128)(2,1)}), bf16[32,8,512]{2,1,0:T(8,128)(2,1)}, u32[]{:S(2)}, u32[]{:S(2)}) async-start(bf16[32,8,512]{2,1,0:T(8,128)(2,1)} %bitcast.25), calls=%async_computation.3 | async-start | bytes 524288 | tf_op jit(solution)/shard_map/all_to_all | solution.py:210
  228.5 0.1 rev.9
  228.6 0.3 bias_64.1.refs_4_
  229.0 0.9 copy-done.15
  229.8 1.4 broadcast_select_fusion.1
  231.2 1.6 pad_maximum_fusion.w_ref
  232.8 11.9 %attend_1_2.1.x_ref = bf16[256,1024]{1,0:T(8,128)(2,1)S(1)} custom-call(s32[17]{0:T(128)S(1)} %concatenate.19.pair_ref, bf16[256,1024]{1,0:T(8,128)(2,1)} %norm.1.tokens_ref, bf16[4,512,384]{2,1,0:T(8,128)(2,1)S(1)} %pad_maximum_fusion.1.refs_0_, bf16[4,512,384]{2,1,0:T(8,128)(2,1)} %collective-permute-done.3.refs_1_, ...), custom_call_target="tpu_custom_call" | custom-call | flops 1610612736 | bytes 8388608 | tf_op jit(solution)/shard_map/attend_1_2/pallas_call | solution.py:150
  244.8 0.8 copy-done.8
  245.5 5.5 %all-to-all-done.3 = bf16[32,8,512]{2,1,0:T(8,128)(2,1)} async-done(((bf16[32,8,512]{2,1,0:T(8,128)(2,1)}), bf16[32,8,512]{2,1,0:T(8,128)(2,1)}, u32[]{:S(2)}, u32[]{:S(2)}) %all-to-all-start.3) | async-done | bytes 262176 | tf_op jit(solution)/shard_map/all_to_all | solution.py:210
  251.0 1.6 copy-done.3
  252.6 1.0 copy-done.5
  253.7 1.0 copy-done.9
  254.7 1.8 mix.1
  256.6 1.0 reshape.52
  (40 shorter events, 0.2 us)
Async XLA Ops:
  6.5 107.5 %copy-start = (bf16[32,1024]{1,0:T(8,128)(2,1)S(1)}, bf16[32,1024]{1,0:T(8,128)(2,1)}, u32[]{:S(2)}) copy-start(bf16[32,1024]{1,0:T(8,128)(2,1)} %param.8) | copy-start | bytes 196612
  6.5 70.1 %copy-start.16 = (bf16[2,64,1,2,1024]{4,3,2,1,0:T(2,128)(2,1)S(1)}, bf16[2,64,1,2,1024]{4,3,2,1,0:T(2,128)(2,1)}, u32[]{:S(2)}) copy-start(bf16[2,64,1,2,1024]{4,3,2,1,0:T(2,128)(2,1)} %param.6) | copy-start | bytes 1572868
  53.9 9.7 %collective-permute-start = (bf16[512,384]{1,0:T(8,128)(2,1)S(1)}, bf16[512,384]{1,0:T(8,128)(2,1)S(1)}, u32[]{:S(2)}, u32[]{:S(2)}) collective-permute-start(bf16[512,384]{1,0:T(8,128)(2,1)S(1)} %bitcast.27), channel_id=1, source_target_pairs={{0,2},{1,7},{2,4},{3,1},{4,6},{5,3},{6,0},{7,5},{8,10},{9,15},{10,... | collective-permute-start | bytes 1179656 | tf_op jit(solution)/shard_map/ppermute | solution.py:246
  63.6 9.7 %collective-permute-start.1 = (bf16[512,384]{1,0:T(8,128)(2,1)S(1)}, bf16[512,384]{1,0:T(8,128)(2,1)S(1)}, u32[]{:S(2)}, u32[]{:S(2)}) collective-permute-start(bf16[512,384]{1,0:T(8,128)(2,1)S(1)} %collective-permute-done), channel_id=1, source_target_pairs={{0,2},{1,7},{2,4},{3,1},{4,6},{5,3},{6,0},{7,5},{8,10},{9,15},{10,... | collective-permute-start | bytes 1179656 | tf_op jit(solution)/shard_map/ppermute | solution.py:246
  73.3 19.6 %collective-permute-start.2 = (bf16[512,384]{1,0:T(8,128)(2,1)S(1)}, bf16[512,384]{1,0:T(8,128)(2,1)S(1)}, u32[]{:S(2)}, u32[]{:S(2)}) collective-permute-start(bf16[512,384]{1,0:T(8,128)(2,1)S(1)} %collective-permute-done.1), channel_id=1, source_target_pairs={{0,2},{1,7},{2,4},{3,1},{4,6},{5,3},{6,0},{7,5},{8,10},{9,15},{10,... | collective-permute-start | bytes 1179656 | tf_op jit(solution)/shard_map/ppermute | solution.py:246
  76.9 19.6 %copy-start.4 = (bf16[256,1024]{1,0:T(8,128)(2,1)}, bf16[256,1024]{1,0:T(8,128)(2,1)S(1)}, u32[]{:S(2)}) copy-start(bf16[256,1024]{1,0:T(8,128)(2,1)S(1)} %reshape.40.tokens_ref) | copy-start | bytes 1572868
  78.0 18.4 %all-to-all-start.4 = ((bf16[16,16,1024]{2,1,0:T(8,128)(2,1)}), bf16[16,16,1024]{2,1,0:T(8,128)(2,1)S(1)}, u32[]{:S(2)}, u32[]{:S(2)}) async-start(bf16[16,16,1024]{2,1,0:T(8,128)(2,1)} %bitcast.17), calls=%async_computation.4 | async-start | bytes 1048576 | tf_op jit(solution)/shard_map/all_to_all | solution.py:210
  84.1 19.3 %collective-permute-start.4 = (bf16[512,384]{1,0:T(8,128)(2,1)S(1)}, bf16[512,384]{1,0:T(8,128)(2,1)}, u32[]{:S(2)}, u32[]{:S(2)}) collective-permute-start(bf16[512,384]{1,0:T(8,128)(2,1)S(1)} %bitcast.28), channel_id=1, source_target_pairs={{0,8},{1,265},{2,10},{3,267},{4,12},{5,269},{6,14},{7,271},{8,256}... | collective-permute-start | bytes 1179656 | tf_op jit(solution)/shard_map/ppermute | solution.py:247
  87.5 16.0 %collective-permute-start.5 = (bf16[512,384]{1,0:T(8,128)(2,1)S(1)}, bf16[512,384]{1,0:T(8,128)(2,1)}, u32[]{:S(2)}, u32[]{:S(2)}) collective-permute-start(bf16[512,384]{1,0:T(8,128)(2,1)S(1)} %collective-permute-done), channel_id=1, source_target_pairs={{0,8},{1,265},{2,10},{3,267},{4,12},{5,269},{6,14},{7,271},{8,256}... | collective-permute-start | bytes 1179656 | tf_op jit(solution)/shard_map/ppermute | solution.py:247
  89.4 14.3 %collective-permute-start.6 = (bf16[512,384]{1,0:T(8,128)(2,1)S(1)}, bf16[512,384]{1,0:T(8,128)(2,1)}, u32[]{:S(2)}, u32[]{:S(2)}) collective-permute-start(bf16[512,384]{1,0:T(8,128)(2,1)S(1)} %collective-permute-done.1), channel_id=1, source_target_pairs={{0,8},{1,265},{2,10},{3,267},{4,12},{5,269},{6,14},{7,271},{8,256}... | collective-permute-start | bytes 1179656 | tf_op jit(solution)/shard_map/ppermute | solution.py:247
  92.8 15.5 %collective-permute-start.7 = (bf16[512,384]{1,0:T(8,128)(2,1)S(1)}, bf16[512,384]{1,0:T(8,128)(2,1)}, u32[]{:S(2)}, u32[]{:S(2)}) collective-permute-start(bf16[512,384]{1,0:T(8,128)(2,1)S(1)} %collective-permute-done.2), channel_id=1, source_target_pairs={{0,8},{1,265},{2,10},{3,267},{4,12},{5,269},{6,14},{7,271},{8,256}... | collective-permute-start | bytes 1179656 | tf_op jit(solution)/shard_map/ppermute | solution.py:247
  96.5 4.8 %copy-start.10 = (bf16[16,16,1024]{2,1,0:T(8,128)(2,1)}, bf16[16,16,1024]{2,1,0:T(8,128)(2,1)S(1)}, u32[]{:S(2)}) copy-start(bf16[16,16,1024]{2,1,0:T(8,128)(2,1)S(1)} %all-to-all-done.4) | copy-start | bytes 1572868
  96.5 73.9 %all-to-all-start.1 = ((bf16[32,8,1024]{2,1,0:T(8,128)(2,1)}), bf16[32,8,1024]{2,1,0:T(8,128)(2,1)}, u32[]{:S(2)}, u32[]{:S(2)}) async-start(bf16[32,8,1024]{2,1,0:T(8,128)(2,1)} %bitcast.11), calls=%async_computation.1 | async-start | bytes 1048576 | tf_op jit(solution)/shard_map/all_to_all | solution.py:210
  101.2 98.3 %all-gather.2.cloned.1.call-start = ((), (), s32[]{:S(2)}) async-start(), calls=%async_computation.6 | async-start | bytes 1572864 | tf_op jit(solution)/shard_map/all_gather | solution.py:266
  101.5 54.0 %collective-permute-start.3 = (bf16[4,512,384]{2,1,0:T(8,128)(2,1)S(1)}, bf16[4,512,384]{2,1,0:T(8,128)(2,1)}, u32[]{:S(2)}, u32[]{:S(2)}) collective-permute-start(bf16[4,512,384]{2,1,0:T(8,128)(2,1)S(1)} %pad_maximum_fusion.1.refs_0_), channel_id=1, source_target_pairs={{0,1},{1,0},{2,3},{3,2},{4,5},{5,4},{6,7},{7,6},{8,9},{9,8},{10,11... | collective-permute-start | bytes 4718600 | tf_op jit(solution)/shard_map/ppermute | solution.py:214
  108.3 45.7 %copy-start.17 = (f32[16,63]{1,0:T(8,128)S(1)}, f32[16,63]{1,0:T(8,128)}, u32[]{:S(2)}) copy-start(f32[16,63]{1,0:T(8,128)} %param.11) | copy-start | bytes 12100
  109.9 45.6 %collective-permute-start.8 = (bf16[4,512,384]{2,1,0:T(8,128)(2,1)S(1)}, bf16[4,512,384]{2,1,0:T(8,128)(2,1)}, u32[]{:S(2)}, u32[]{:S(2)}) collective-permute-start(bf16[4,512,384]{2,1,0:T(8,128)(2,1)S(1)} %pad_maximum_fusion.2.refs_2_.refs_0_), channel_id=1, source_target_pairs={{0,1},{1,0},{2,3},{3,2},{4,5},{5,4},{6,7},{7,6},{8,9},{9,8},{10,11... | collective-permute-start | bytes 4718600 | tf_op jit(solution)/shard_map/ppermute | solution.py:214
  154.4 1.0 copy-start.6
  155.5 1.2 copy-start.7
  156.7 1.0 copy-start.11
  157.8 18.1 %copy-start.18 = (f32[16,63]{1,0:T(8,128)S(1)}, f32[16,63]{1,0:T(8,128)}, u32[]{:S(2)}) copy-start(f32[16,63]{1,0:T(8,128)} %param.10) | copy-start | bytes 12100
  169.5 0.8 copy-start.12
  170.3 15.2 %all-to-all-start.5 = ((bf16[16,16,1024]{2,1,0:T(8,128)(2,1)}), bf16[16,16,1024]{2,1,0:T(8,128)(2,1)}, u32[]{:S(2)}, u32[]{:S(2)}) async-start(bf16[16,16,1024]{2,1,0:T(8,128)(2,1)} %bitcast.23), calls=%async_computation.5 | async-start | bytes 1048576 | tf_op jit(solution)/shard_map/all_to_all | solution.py:210
  183.2 1.1 copy-start.1
  184.2 0.7 copy-start.14
  185.5 38.4 %all-to-all-start.2 = ((bf16[32,8,512]{2,1,0:T(8,128)(2,1)}), bf16[32,8,512]{2,1,0:T(8,128)(2,1)S(1)}, u32[]{:S(2)}, u32[]{:S(2)}) async-start(bf16[32,8,512]{2,1,0:T(8,128)(2,1)} %bitcast.26), calls=%async_computation.2 | async-start | bytes 524288 | tf_op jit(solution)/shard_map/all_to_all | solution.py:210
  199.5 29.5 %collective-permute-start.9 = (bf16[1024,512]{1,0:T(8,128)(2,1)}, bf16[1024,512]{1,0:T(8,128)(2,1)}, u32[]{:S(2)}, u32[]{:S(2)}) collective-permute-start(bf16[1024,512]{1,0:T(8,128)(2,1)} %all-gather.2.cloned.1.call-done), channel_id=1, source_target_pairs={{0,1},{1,0},{2,3},{3,2},{4,5},{5,4},{6,7},{7,6},{8,9},{9,8},{10,11... | collective-permute-start | bytes 3145736 | tf_op jit(solution)/shard_map/ppermute | solution.py:214
  201.7 1.2 copy-start.2
  202.9 25.6 %copy-start.19 = (f32[16,127]{1,0:T(8,128)S(1)}, f32[16,127]{1,0:T(8,128)}, u32[]{:S(2)}) copy-start(f32[16,127]{1,0:T(8,128)} %param.9) | copy-start | bytes 24388
  209.7 0.7 copy-start.13
  223.9 27.1 %all-to-all-start.3 = ((bf16[32,8,512]{2,1,0:T(8,128)(2,1)}), bf16[32,8,512]{2,1,0:T(8,128)(2,1)}, u32[]{:S(2)}, u32[]{:S(2)}) async-start(bf16[32,8,512]{2,1,0:T(8,128)(2,1)} %bitcast.25), calls=%async_computation.3 | async-start | bytes 524288 | tf_op jit(solution)/shard_map/all_to_all | solution.py:210
  228.6 1.2 copy-start.15
  244.7 0.8 copy-start.8
  251.0 1.6 copy-start.3
  252.6 1.0 copy-start.5
  253.7 1.0 copy-start.9
Sparse Core Ops, SparseCore 0:
  154.1 38.9 all-gather.1

commit v2 on v1

v2 whole, which is shorter than its diff:
```python
import functools
import jax
import jax.numpy as jnp
from jax import lax
from jax.experimental import pallas as pl
from jax.experimental.pallas import tpu as pltpu
from jax.sharding import Mesh
from jax.sharding import PartitionSpec as P

HEADS = 16
HEAD = 64
PAIRS = HEADS // 2
BLOCK = 128
NEG = -1e30
DIMS = (2, 16, 2, 4, 2)
ALL = ("yh", "z", "yl", "x", "c")
GY = ("yh", "z")
GZ = ("yl", "x", "c")
BF = jnp.bfloat16
F32 = jnp.float32


def index_of(yh, z, yl, x, c):
    return (((yh * DIMS[1] + z) * DIMS[2] + yl) * DIMS[3] + x) * DIMS[4] + c


def every_device():
    for yh in range(DIMS[0]):
        for z in range(DIMS[1]):
            for yl in range(DIMS[2]):
                for x in range(DIMS[3]):
                    for c in range(DIMS[4]):
                        yield yh, z, yl, x, c


def hop_x(far):
    return [
        (index_of(*d), index_of(d[0], d[1], d[2], (d[3] + far) % DIMS[3], d[4]))
        for d in every_device()
    ]


def hop_y(far):
    pairs = []
    for yh, z, yl, x, c in every_device():
        y = (yh * 2 + yl + far) % 4
        pairs.append((index_of(yh, z, yl, x, c), index_of(y // 2, z, y % 2, x, c)))
    return pairs


def iota(shape, dim):
    return lax.broadcasted_iota(jnp.int32, shape, dim)


def line_rows(axis, i):
    if axis == 1:
        return (i & 128) + (i & 63) * 2 + ((i >> 6) & 1)
    if axis == 2:
        return (i & 31) * 8 + (i >> 5)
    return ((i & 30) << 3) + ((i >> 5) << 1) + (i & 1)


def norm_kernel(tokens_ref, out_ref):
    values = tokens_ref[...].astype(F32)
    center = jnp.mean(values, axis=-1, keepdims=True)
    values = values - center
    spread = jnp.mean(values * values, axis=-1, keepdims=True)
    out_ref[...] = (values * lax.rsqrt(spread + 1e-05)).astype(BF)


def bias_kernel(length, table_ref, out_ref):
    lanes = iota((length, BLOCK), 1) // length
    for head in range(HEADS):
        row = jnp.broadcast_to(table_ref[head : head + 1, :], (length, BLOCK))
        for place in range(BLOCK // length):
            shift = (place * length - length + 1) % BLOCK
            turned = pltpu.roll(row, shift, 1, stride=1, stride_axis=0)
            out_ref[
                head // 2,
                place * length : (place + 1) * length,
                (head % 2) * BLOCK : (head % 2 + 1) * BLOCK,
            ] = jnp.where(lanes == place, turned, NEG)


def interleaved(own, other, core):
    depth, width = own.shape
    low = jnp.where(core == 0, own, other).reshape(depth // 16, 16, width)
    high = jnp.where(core == 0, other, own).reshape(depth // 16, 16, width)
    return jnp.stack([low, high], axis=1).reshape(2 * depth, width)


def assembled(parts, turned, core):
    halves = [interleaved(own, other, core) for own, other in parts]
    low = jnp.where(turned == 0, halves[0], halves[1])
    high = jnp.where(turned == 0, halves[1], halves[0])
    return jnp.concatenate([low, high], axis=0)


def attend_kernel(axis, scalar_ref, tokens_ref, *refs):
    weight_refs, bias_refs = refs[:4], refs[4:6]
    out_ref, lines_ref, back_ref, qkv_ref, mixed_ref = refs[-5:]
    step = pl.program_id(0)
    rows = tokens_ref.shape[0]
    core, turned_a, turned_b, yl, x = [scalar_ref[8 + n] for n in range(5)]

    @pl.when(step == 0)
    def _():
        turn = line_rows(axis, iota((rows, 1), 0)) == iota((rows, rows), 1)
        turn = turn.astype(F32).astype(BF)
        lines_ref[...] = jnp.dot(turn, tokens_ref[...], preferred_element_type=F32).astype(BF)
        place = iota((rows, 1), 0)
        if axis == 3:
            dx, dy, dc = place >> 6, (place >> 5) & 1, (place >> 4) & 1
            to = (yl ^ dy) * 8 + ((x + dx) & 3) * 2 + (core ^ dc)
            back = ((place >> 1) & 7) * 32 + to * 2 + (place & 1) == iota((rows, rows), 1)
        else:
            back = line_rows(axis, iota((1, rows), 1)) == iota((rows, rows), 0)
        back_ref[...] = back.astype(F32).astype(BF)

    width = 3 * BLOCK
    left = iota((BLOCK, BLOCK), 1) < HEAD
    zero = jnp.zeros((BLOCK, BLOCK), BF)
    projected = (step + 1) % 2
    for n in range(2):
        mixed = []
        for start in range(0, rows, BLOCK):
            q, k, v = [
                qkv_ref[projected, start : start + BLOCK, n * width + m * BLOCK : n * width + (m + 1) * BLOCK]
                for m in range(3)
            ]
            keys = jnp.concatenate([jnp.where(left, k, zero), jnp.where(left, zero, k)], axis=0)
            values = jnp.concatenate([jnp.where(left, v, zero), jnp.where(left, zero, v)], axis=0)
            scores = lax.dot_general(q, keys, (((1,), (1,)), ((), ())), preferred_element_type=F32)
            scores = scores * HEAD ** (-0.5) + bias_refs[n][0]
            probs = []
            for half in range(2):
                s = scores[:, half * BLOCK : (half + 1) * BLOCK]
                e = jnp.exp(s - jnp.max(s, axis=-1, keepdims=True))
                probs.append((e * (1.0 / jnp.sum(e, axis=-1, keepdims=True))).astype(BF))
            probs = jnp.concatenate(probs, axis=1)
            mixed.append(jnp.dot(probs, values, preferred_element_type=F32).astype(BF))
        pair = scalar_ref[2 * jnp.maximum(step - 1, 0) + n]
        columns = pl.ds(pl.multiple_of(pair * BLOCK, BLOCK), BLOCK)
        mixed_ref[:, columns] = jnp.concatenate(mixed, axis=0)

    turned = jnp.where(step < 2, turned_a, turned_b)
    near_own, near_other, far_own, far_other = weight_refs
    weights = []
    for n in range(2):
        parts = [
            (
                jnp.concatenate([near_own[0, m, n], far_own[n, 0, m]], axis=0),
                jnp.concatenate([near_other[0, m, n], far_other[n, 0, m]], axis=0),
            )
            for m in range(2)
        ]
        weights.append(assembled(parts, turned, core))
    weights = jnp.concatenate(weights, axis=1)
    qkv = jnp.dot(lines_ref[...], weights, preferred_element_type=F32)
    qkv_ref[step % 2] = qkv.astype(BF)

    @pl.when(step == pl.num_programs(0) - 1)
    def _():
        out_ref[...] = jnp.dot(
            back_ref[...], mixed_ref[...], preferred_element_type=F32
        ).astype(BF)


def attend(axis, tokens, weights, bias, scalars, after=()):
    rows, features = tokens.shape
    half, width = weights[0].shape[3:]
    specs = [pl.BlockSpec((rows, features), lambda s, p: (0, 0))]

    def near(s, p):
        s = jnp.minimum(s, 3)
        return (s // 2, 0, s % 2, 0, 0)

    def far(s, p):
        s = jnp.minimum(s, 3)
        return (s % 2, s // 2, 0, 0, 0)

    specs.extend([pl.BlockSpec((1, 2, 2, half, width), near)] * 2)
    specs.extend([pl.BlockSpec((2, 1, 2, half, width), far)] * 2)
    for n in range(2):

        def pair(s, p, n=n):
            return (p[2 * jnp.maximum(s - 1, 0) + n], 0, 0)

        specs.append(pl.BlockSpec((1, BLOCK, 2 * BLOCK), pair))
    specs.extend([pl.BlockSpec(memory_space=pl.ANY)] * len(after))
    return pl.pallas_call(
        functools.partial(attend_kernel, axis),
        out_shape=jax.ShapeDtypeStruct((rows, HEADS * HEAD), BF),
        grid_spec=pltpu.PrefetchScalarGridSpec(
            num_scalar_prefetch=1,
            grid=(5,),
            in_specs=specs,
            out_specs=pl.BlockSpec((rows, features), lambda s, p: (0, 0)),
            scratch_shapes=[
                pltpu.VMEM((rows, features), BF),
                pltpu.VMEM((rows, rows), BF),
                pltpu.VMEM((2, rows, 2 * width), BF),
                pltpu.VMEM((rows, features), BF),
            ],
        ),
        compiler_params=pltpu.CompilerParams(vmem_limit_bytes=61 * 2**20),
        cost_estimate=pl.CostEstimate(flops=1000, bytes_accessed=1000, transcendentals=0),
        name=f"attend_{axis}",
    )(scalars, tokens, *weights, bias, bias, *after)


def mix_kernel(scalar_ref, tokens_ref, x_ref, y_ref, z0, z1, z2, z3, zy_ref, zc_ref, own_ref, other_ref, out_ref, z_ref):
    core, yl, x = scalar_ref[8], scalar_ref[11], scalar_ref[12]
    for k, ref in enumerate((z0, z1, z2, z3)):
        for dy in range(2):
            for dc in range(2):
                if dc == 1:
                    rows = zc_ref[dy * 4 + k]
                elif dy == 1:
                    rows = zy_ref[k, :16]
                else:
                    rows = ref[:16]
                source = (yl ^ dy) * 8 + ((x - k + 4) % 4) * 2 + (core ^ dc)
                z_ref[pl.ds(pl.multiple_of(source * 16, 16), 16), :] = rows
    summed = x_ref[...].astype(F32) + y_ref[...].astype(F32) + z_ref[...].astype(F32)
    summed = summed.astype(BF)
    for pair in range(PAIRS):
        weights = jnp.concatenate(
            [interleaved(own_ref[h, pair], other_ref[h, pair], core) for h in range(2)], axis=0
        )
        columns = slice(pair * BLOCK, (pair + 1) * BLOCK)
        result = jnp.dot(summed, weights, preferred_element_type=F32)
        out_ref[:, columns] = (tokens_ref[:, columns].astype(F32) + result).astype(BF)


def whole(kernel, out, name, scalars=0, scratch=()):
    vmem = pl.BlockSpec(memory_space=pltpu.VMEM)
    smem = pl.BlockSpec(memory_space=pltpu.SMEM)

    def call(*args):
        return pl.pallas_call(
            kernel,
            out_shape=out,
            in_specs=[smem] * scalars + [vmem] * (len(args) - scalars),
            out_specs=vmem,
            scratch_shapes=list(scratch),
            compiler_params=pltpu.CompilerParams(vmem_limit_bytes=61 * 2**20),
            name=name,
        )(*args)

    return call


def reversed_table(table):
    turned = table[:, ::-1]
    return jnp.pad(turned, ((0, 0), (0, BLOCK - turned.shape[1])))


def bias_blocks(table):
    length = (table.shape[1] + 1) // 2
    shape = jax.ShapeDtypeStruct((PAIRS, BLOCK, 2 * BLOCK), F32)
    return whole(functools.partial(bias_kernel, length), shape, f"bias_{length}")(
        reversed_table(table)
    )


def exchange(array, axes):
    return lax.all_to_all(array, axes, split_axis=0, concat_axis=0, tiled=True)


def swap(array, axis):
    return lax.ppermute(array, axis, [(0, 1), (1, 0)])


def together(array, other):
    return lax.optimization_barrier((array, other))[0]


def shards(tokens, w_qkv, w_out, bias_x, bias_y, bias_z):
    features = tokens.shape[-1]
    shape = tokens.shape
    yh, yl = lax.axis_index("yh"), lax.axis_index("yl")
    x, c = lax.axis_index("x"), lax.axis_index("c")
    pair = yl * DIMS[3] + x
    peers = DIMS[0] * DIMS[1]
    zs = DIMS[2] * DIMS[3] * DIMS[4]

    depth = w_qkv.shape[0] // 2
    mine = [
        lax.dynamic_slice(w_qkv, (c * depth, part * features + pair * BLOCK), (depth, BLOCK))
        for part in range(3)
    ]
    mine.append(lax.dynamic_slice(w_out, (c * depth, pair * BLOCK), (depth, BLOCK)))
    mine = jnp.concatenate(mine, axis=1)
    piece = exchange(jnp.broadcast_to(mine[None], (DIMS[1], *mine.shape)), "z")
    piece = piece.reshape(DIMS[1] * depth, 4 * BLOCK)
    flat = tokens.reshape(-1, features)
    rows = flat.shape[0]
    normed = whole(norm_kernel, jax.ShapeDtypeStruct(flat.shape, BF), "norm")(flat)
    blocks_x = bias_blocks(bias_x)
    blocks_y = bias_blocks(bias_y)
    blocks_z = bias_blocks(bias_z)
    piece = together(piece, (normed, blocks_x, blocks_y, blocks_z))
    out_piece = piece[:, 3 * BLOCK :]
    piece = piece[:, : 3 * BLOCK]

    y_lines = exchange(normed.reshape(peers, -1, features), GY).reshape(rows, features)
    z_lines = exchange(together(normed, y_lines).reshape(zs, -1, features), GZ)
    z_lines = z_lines.reshape(rows, features)

    tall = piece.shape[0] // 2
    along = [piece[:tall]] + [lax.ppermute(piece[:tall], ALL, hop_x(k)) for k in range(1, 4)]
    across = [piece[tall:]] + [lax.ppermute(piece[tall:], ALL, hop_y(m)) for m in range(1, 4)]
    along = jnp.stack(along)
    across = jnp.stack([across[m] for m in (0, 2, 1, 3)])
    near = [along] + [lax.ppermute(along, ALL, hop_y(m)) for m in range(1, 4)]
    far = [across] + [lax.ppermute(across, ALL, hop_x(k)) for k in range(1, 4)]
    near = jnp.stack([near[m] for m in (0, 2, 1, 3)]).reshape(2, 2, *along.shape)
    far = jnp.stack(far).reshape(4, 2, 2, *piece[:tall].shape)
    near_other = swap(near, "c")
    far_other = swap(far, "c")

    out_own = lax.all_gather(out_piece, ("yh", "yl", "x"), axis=0, tiled=True)
    out_own = out_own.reshape(2, PAIRS, -1, BLOCK)

    columns = (x - jnp.arange(4)) % DIMS[3]
    y = yh * 2 + yl
    turned_b = ((y - 1) % 4) // 2
    scalars = jnp.concatenate(
        [yl * 4 + columns, (1 - yl) * 4 + columns, jnp.stack([c, yh, turned_b, yl, x])]
    ).astype(jnp.int32)

    every = (near, near_other, far, far_other)
    along_y = attend(2, y_lines, every, blocks_y, scalars)
    z = attend(3, z_lines, every, blocks_z, scalars, (along_y,))
    along_y = exchange(together(along_y, z_lines).reshape(peers, -1, features), GY).reshape(rows, features)
    along_x = attend(1, normed, every, blocks_x, scalars, (z,))

    out_own = together(out_own, along_x)
    out_other = swap(out_own, "c")
    z = z.reshape(4, rows // 4, features)
    back = [z[0]] + [lax.ppermute(z[k], ALL, hop_x(k)) for k in range(1, 4)]
    back_y = swap(together(jnp.stack([b[32:] for b in back]), along_x), "yl")
    back_c = jnp.stack([b[16:32] for b in back] + [back_y[k, 16:] for k in range(4)])
    back_c = swap(together(back_c, along_y), "c")
    mixed = whole(
        mix_kernel, jax.ShapeDtypeStruct(flat.shape, BF), "mix", 1, [pltpu.VMEM(flat.shape, BF)]
    )(scalars, flat, along_x, along_y, *back, back_y, back_c, out_own, out_other)
    return mixed.reshape(shape)


def solution(mesh):
    torus = Mesh(mesh.devices.reshape(DIMS), ALL)
    in_specs = (P(None, None, GY, GZ, None), P(GY, None), P(GY, None), P(), P(), P())
    return jax.shard_map(
        shards, mesh=torus, in_specs=in_specs, out_specs=in_specs[0], check_vma=False
    )
```

time: 266 us -> 212 us (0.80)
  the two profiles are of different devices: /device:TPU:2 before, /device:TPU:1 now
where the time goes in v2:
time: 212 us; the launch traced here: 210 us
  starting transfers between devices  116 us (55%)
  Pallas kernels  45.3 us (21%)
  waiting for transfers between devices  19.7 us (9%)
  between operations  13.9 us (7%)
  local copies, waits for them, and re-layouts  13.7 us (6%)
    all_to_all x4, starting transfers between devices, exchange(): return lax.all_to_all(array, axes, split_axis=0, concat_axis=0, tiled=True)  45.6 us
    pallas_call x3, Pallas kernels, attend(): pl.pallas_call(functools.partial(attend_kernel, axis), out_shape=jax.Shap...  32.5 us
    ppermute x5, starting transfers between devices, swap(): return lax.ppermute(array, axis, [(0, 1), (1, 0)])  19.2 us
    pallas_call x5, Pallas kernels, call(): pl.pallas_call(kernel, out_shape=out, in_specs=[smem] * scalars + [vmem]...  12.8 us
    ppermute x3, starting transfers between devices, shards(): lax.ppermute(piece[tall:], ALL, hop_y(m))  11.3 us
    ppermute x3, starting transfers between devices, shards(): near = [along] + [lax.ppermute(along, ALL, hop_y(m)) for m in range(1, 4)]  11.1 us
    ppermute x3, starting transfers between devices, shards(): lax.ppermute(piece[:tall], ALL, hop_x(k))  10.2 us
    ppermute x3, starting transfers between devices, shards(): back = [z[0]] + [lax.ppermute(z[k], ALL, hop_x(k)) for k in range(1, 4)]  9.36 us
  transfers between devices with their start and end apart: 25, of which 7 were waited for; matrix products, arithmetic and copies ran while one was open for 5% of the time, Pallas kernels for 19%

profile of v2, /device:TPU:1, one launch (start us, length us, event | category | flops | bytes accessed | tf_op | source)
XLA Modules:
  0.0 210.2 jit_solution(1730018696305743533)
XLA Ops:
  6.5 0.7 dynamic_slice.15
  7.2 0.7 fusion.8
  8.0 0.7 broadcast_in_dim.2
  8.7 15.7 %all-to-all-start = ((bf16[16,16,512]{2,1,0:T(8,128)(2,1)}), bf16[16,16,512]{2,1,0:T(8,128)(2,1)S(1)}, u32[]{:S(2)}, u32[]{:S(2)}) async-start(bf16[16,16,512]{2,1,0:T(8,128)(2,1)} %broadcast_in_dim.2), calls=%async_computation | async-start | bytes 524288 | tf_op jit(solution)/shard_map/all_to_all | solution.py:268
  24.5 0.0 copy-start.11
  24.5 2.0 reshape.52.tokens_ref
  26.5 2.2 %norm.1.tokens_ref = bf16[256,1024]{1,0:T(8,128)(2,1)} custom-call(bf16[256,1024]{1,0:T(8,128)(2,1)} %reshape.52.tokens_ref), custom_call_target="tpu_custom_call" | custom-call | tf_op jit(solution)/shard_map/norm/pallas_call | solution.py:241
  28.7 0.1 rev.9
  28.8 0.6 pad.11.table_ref
  29.4 2.1 bias_64.1.refs_4_.refs_5_
  31.4 0.1 rev.10
  31.5 0.6 pad.12.table_ref
  32.1 2.0 bias_32.2.refs_4_.refs_5_
  34.1 0.1 rev.11
  34.2 0.6 pad.13.table_ref
  34.8 2.0 bias_32.3.refs_4_.refs_5_
  36.8 0.8 all-to-all-done
  37.6 4.8 %collective-permute-start.7 = (bf16[128,384]{1,0:T(8,128)(2,1)S(1)}, bf16[128,384]{1,0:T(8,128)(2,1)S(1)}, u32[]{:S(2)}, u32[]{:S(2)}) collective-permute-start(bf16[128,384]{1,0:T(8,128)(2,1)S(1)} %get-tuple-element.25), channel_id=1, source_target_pairs={{0,256},{1,257},{2,258},{3,259},{4,260},{5,261},{6,262},{7,263},{8... | collective-permute-start | bytes 294920 | tf_op jit(solution)/shard_map/ppermute | solution.py:313
  42.5 2.3 %collective-permute-start.8 = (bf16[128,384]{1,0:T(8,128)(2,1)S(1)}, bf16[128,384]{1,0:T(8,128)(2,1)S(1)}, u32[]{:S(2)}, u32[]{:S(2)}) collective-permute-start(bf16[128,384]{1,0:T(8,128)(2,1)S(1)} %get-tuple-element.25), channel_id=1, source_target_pairs={{0,8},{1,9},{2,10},{3,11},{4,12},{5,13},{6,14},{7,15},{8,256},{9,2... | collective-permute-start | bytes 294920 | tf_op jit(solution)/shard_map/ppermute | solution.py:313
  44.8 4.2 %collective-permute-start.9 = (bf16[128,384]{1,0:T(8,128)(2,1)S(1)}, bf16[128,384]{1,0:T(8,128)(2,1)S(1)}, u32[]{:S(2)}, u32[]{:S(2)}) collective-permute-start(bf16[128,384]{1,0:T(8,128)(2,1)S(1)} %get-tuple-element.25), channel_id=1, source_target_pairs={{0,264},{1,265},{2,266},{3,267},{4,268},{5,269},{6,270},{7,271},{8... | collective-permute-start | bytes 294920 | tf_op jit(solution)/shard_map/ppermute | solution.py:313
  49.0 11.2 %all-to-all-start.1 = ((bf16[32,8,1024]{2,1,0:T(8,128)(2,1)}), bf16[32,8,1024]{2,1,0:T(8,128)(2,1)S(1)}, u32[]{:S(2)}, u32[]{:S(2)}) async-start(bf16[32,8,1024]{2,1,0:T(8,128)(2,1)} %bitcast.23), calls=%async_computation.1 | async-start | bytes 1048576 | tf_op jit(solution)/shard_map/all_to_all | solution.py:268
  60.2 0.0 all-gather.2.cloned.1.call-start
  60.3 0.0 collective-permute-done.7
  60.3 0.1 pad_maximum_fusion.3
  60.4 3.1 %collective-permute-start.10 = (bf16[4,128,384]{2,1,0:T(8,128)(2,1)S(1)}, bf16[4,128,384]{2,1,0:T(8,128)(2,1)S(1)}, u32[]{:S(2)}, u32[]{:S(2)}) collective-permute-start(bf16[4,128,384]{2,1,0:T(8,128)(2,1)S(1)} %pad_maximum_fusion.3), channel_id=1, source_target_pairs={{0,2},{1,3},{2,4},{3,5},{4,6},{5,7},{6,0},{7,1},{8,10},{9,11},{10,... | collective-permute-start | bytes 1179656 | tf_op jit(solution)/shard_map/ppermute | solution.py:317
  63.5 3.1 %collective-permute-start = (bf16[128,384]{1,0:T(8,128)(2,1)S(1)}, bf16[128,384]{1,0:T(8,128)(2,1)S(1)}, u32[]{:S(2)}, u32[]{:S(2)}) collective-permute-start(bf16[128,384]{1,0:T(8,128)(2,1)S(1)} %get-tuple-element.26), channel_id=1, source_target_pairs={{0,2},{1,3},{2,4},{3,5},{4,6},{5,7},{6,0},{7,1},{8,10},{9,11},{10,... | collective-permute-start | bytes 294920 | tf_op jit(solution)/shard_map/ppermute | solution.py:312
  66.6 3.3 %collective-permute-start.1 = (bf16[128,384]{1,0:T(8,128)(2,1)S(1)}, bf16[128,384]{1,0:T(8,128)(2,1)S(1)}, u32[]{:S(2)}, u32[]{:S(2)}) collective-permute-start(bf16[128,384]{1,0:T(8,128)(2,1)S(1)} %get-tuple-element.26), channel_id=1, source_target_pairs={{0,4},{1,5},{2,6},{3,7},{4,0},{5,1},{6,2},{7,3},{8,12},{9,13},{10,... | collective-permute-start | bytes 294920 | tf_op jit(solution)/shard_map/ppermute | solution.py:312
  70.0 3.8 %collective-permute-start.2 = (bf16[128,384]{1,0:T(8,128)(2,1)S(1)}, bf16[128,384]{1,0:T(8,128)(2,1)S(1)}, u32[]{:S(2)}, u32[]{:S(2)}) collective-permute-start(bf16[128,384]{1,0:T(8,128)(2,1)S(1)} %get-tuple-element.26), channel_id=1, source_target_pairs={{0,6},{1,7},{2,0},{3,1},{4,2},{5,3},{6,4},{7,5},{8,14},{9,15},{10,... | collective-permute-start | bytes 294920 | tf_op jit(solution)/shard_map/ppermute | solution.py:312
  73.8 2.4 %collective-permute-start.11 = (bf16[4,128,384]{2,1,0:T(8,128)(2,1)S(1)}, bf16[4,128,384]{2,1,0:T(8,128)(2,1)S(1)}, u32[]{:S(2)}, u32[]{:S(2)}) collective-permute-start(bf16[4,128,384]{2,1,0:T(8,128)(2,1)S(1)} %pad_maximum_fusion.3), channel_id=1, source_target_pairs={{0,4},{1,5},{2,6},{3,7},{4,0},{5,1},{6,2},{7,3},{8,12},{9,13},{10,... | collective-permute-start | bytes 1179656 | tf_op jit(solution)/shard_map/ppermute | solution.py:317
  76.2 3.4 %collective-permute-start.12 = (bf16[4,128,384]{2,1,0:T(8,128)(2,1)S(1)}, bf16[4,128,384]{2,1,0:T(8,128)(2,1)S(1)}, u32[]{:S(2)}, u32[]{:S(2)}) collective-permute-start(bf16[4,128,384]{2,1,0:T(8,128)(2,1)S(1)} %pad_maximum_fusion.3), channel_id=1, source_target_pairs={{0,6},{1,7},{2,0},{3,1},{4,2},{5,3},{6,4},{7,5},{8,14},{9,15},{10,... | collective-permute-start | bytes 1179656 | tf_op jit(solution)/shard_map/ppermute | solution.py:317
  79.6 0.1 fusion.6
  79.7 4.7 %collective-permute-start.3 = (bf16[4,128,384]{2,1,0:T(8,128)(2,1)S(1)}, bf16[4,128,384]{2,1,0:T(8,128)(2,1)S(1)}, u32[]{:S(2)}, u32[]{:S(2)}) collective-permute-start(bf16[4,128,384]{2,1,0:T(8,128)(2,1)S(1)} %get-tuple-element.22), channel_id=1, source_target_pairs={{0,256},{1,257},{2,258},{3,259},{4,260},{5,261},{6,262},{7,263},{8... | collective-permute-start | bytes 1179656 | tf_op jit(solution)/shard_map/ppermute | solution.py:316
  84.4 2.2 %collective-permute-start.4 = (bf16[4,128,384]{2,1,0:T(8,128)(2,1)S(1)}, bf16[4,128,384]{2,1,0:T(8,128)(2,1)S(1)}, u32[]{:S(2)}, u32[]{:S(2)}) collective-permute-start(bf16[4,128,384]{2,1,0:T(8,128)(2,1)S(1)} %get-tuple-element.22), channel_id=1, source_target_pairs={{0,8},{1,9},{2,10},{3,11},{4,12},{5,13},{6,14},{7,15},{8,256},{9,2... | collective-permute-start | bytes 1179656 | tf_op jit(solution)/shard_map/ppermute | solution.py:316
  86.6 4.3 %collective-permute-start.5 = (bf16[4,128,384]{2,1,0:T(8,128)(2,1)S(1)}, bf16[4,128,384]{2,1,0:T(8,128)(2,1)S(1)}, u32[]{:S(2)}, u32[]{:S(2)}) collective-permute-start(bf16[4,128,384]{2,1,0:T(8,128)(2,1)S(1)} %get-tuple-element.22), channel_id=1, source_target_pairs={{0,264},{1,265},{2,266},{3,267},{4,268},{5,269},{6,270},{7,271},{8... | collective-permute-start | bytes 1179656 | tf_op jit(solution)/shard_map/ppermute | solution.py:316
  90.9 3.6 %collective-permute-done.12 = bf16[4,128,384]{2,1,0:T(8,128)(2,1)S(1)} collective-permute-done((bf16[4,128,384]{2,1,0:T(8,128)(2,1)S(1)}, bf16[4,128,384]{2,1,0:T(8,128)(2,1)S(1)}, u32[]{:S(2)}, u32[]{:S(2)}) %collective-permute-start.12) | collective-permute-done | bytes 393248 | tf_op jit(solution)/shard_map/ppermute | solution.py:317
  94.5 0.2 pad_maximum_fusion.1.refs_2_
  94.8 3.7 %collective-permute-start.13 = (bf16[4,2,2,128,384]{4,3,2,1,0:T(8,128)(2,1)S(1)}, bf16[4,2,2,128,384]{4,3,2,1,0:T(8,128)(2,1)}, u32[]{:S(2)}, u32[]{:S(2)}) collective-permute-start(bf16[4,2,2,128,384]{4,3,2,1,0:T(8,128)(2,1)S(1)} %pad_maximum_fusion.1.refs_2_), channel_id=1, source_target_pairs={{0,1},{1,0},{2,3},{3,2},{4,5},{5,4},{6,7},{7,6},{8,9},{9,8},{10,11... | collective-permute-start | bytes 4718600 | tf_op jit(solution)/shard_map/ppermute | solution.py:272
  98.5 2.6 %collective-permute-done.4 = bf16[4,128,384]{2,1,0:T(8,128)(2,1)S(1)} collective-permute-done((bf16[4,128,384]{2,1,0:T(8,128)(2,1)S(1)}, bf16[4,128,384]{2,1,0:T(8,128)(2,1)S(1)}, u32[]{:S(2)}, u32[]{:S(2)}) %collective-permute-start.4) | collective-permute-done | bytes 393248 | tf_op jit(solution)/shard_map/ppermute | solution.py:316
  101.1 1.4 pad_maximum_fusion
  102.5 5.3 %collective-permute-start.6 = (bf16[2,2,4,128,384]{4,3,2,1,0:T(8,128)(2,1)}, bf16[2,2,4,128,384]{4,3,2,1,0:T(8,128)(2,1)}, u32[]{:S(2)}, u32[]{:S(2)}) collective-permute-start(bf16[2,2,4,128,384]{4,3,2,1,0:T(8,128)(2,1)} %bitcast.14.refs_0_), channel_id=1, source_target_pairs={{0,1},{1,0},{2,3},{3,2},{4,5},{5,4},{6,7},{7,6},{8,9},{9,8},{10,11... | collective-permute-start | bytes 4718600 | tf_op jit(solution)/shard_map/ppermute | solution.py:272
  107.7 0.6 slice.82
  108.4 0.0 all-gather.2.cloned.1.call-update
  108.4 4.1 %all-to-all-start.2 = ((bf16[16,16,1024]{2,1,0:T(8,128)(2,1)}), bf16[16,16,1024]{2,1,0:T(8,128)(2,1)S(1)}, u32[]{:S(2)}, u32[]{:S(2)}) async-start(bf16[16,16,1024]{2,1,0:T(8,128)(2,1)} %bitcast.25), calls=%async_computation.2 | async-start | bytes 1048576 | tf_op jit(solution)/shard_map/all_to_all | solution.py:268
  112.5 0.6 concatenate.7.scalar_ref
  113.2 10.8 %attend_2.1.refs_6_ = bf16[256,1024]{1,0:T(8,128)(2,1)} custom-call(s32[13]{0:T(128)} %concatenate.7.scalar_ref, bf16[256,1024]{1,0:T(8,128)(2,1)} %bitcast.59, bf16[2,2,4,128,384]{4,3,2,1,0:T(8,128)(2,1)} %bitcast.14.refs_0_, bf16[2,2,4,128,384]{4,3,2,1,0:T(8,128)(2,1)} %collective-permute-done.6.refs_1_, bf16[4,2,2,128,384]{4,3,2,1,0:T(8,128)(2,1)} %copy-done, ...), custom_call_target="tpu_custom_call" | custom-call | flops 1000 | bytes 1000 | tf_op jit(solution)/shard_map/attend_2/pallas_call | solution.py:191
  124.0 14.5 %all-to-all-start.3 = ((bf16[32,8,1024]{2,1,0:T(8,128)(2,1)}), bf16[32,8,1024]{2,1,0:T(8,128)(2,1)S(1)}, u32[]{:S(2)}, u32[]{:S(2)}) async-start(bf16[32,8,1024]{2,1,0:T(8,128)(2,1)} %bitcast.58), calls=%async_computation.3 | async-start | bytes 1048576 | tf_op jit(solution)/shard_map/all_to_all | solution.py:268
  138.5 10.9 %attend_3.1.refs_6_ = bf16[256,1024]{1,0:T(8,128)(2,1)} custom-call(s32[13]{0:T(128)} %concatenate.7.scalar_ref, bf16[256,1024]{1,0:T(8,128)(2,1)} %bitcast.60, bf16[2,2,4,128,384]{4,3,2,1,0:T(8,128)(2,1)} %bitcast.14.refs_0_, bf16[2,2,4,128,384]{4,3,2,1,0:T(8,128)(2,1)} %collective-permute-done.6.refs_1_, bf16[4,2,2,128,384]{4,3,2,1,0:T(8,128)(2,1)} %copy-done, ...), custom_call_target="tpu_custom_call" | custom-call | flops 1000 | bytes 1000 | tf_op jit(solution)/shard_map/attend_3/pallas_call | solution.py:191
  149.4 1.8 fusion.7
  151.2 0.8 slice_bitcast_fusion.3
  152.0 10.8 %attend_1.1.x_ref = bf16[256,1024]{1,0:T(8,128)(2,1)} custom-call(s32[13]{0:T(128)} %concatenate.7.scalar_ref, bf16[256,1024]{1,0:T(8,128)(2,1)} %norm.1.tokens_ref, bf16[2,2,4,128,384]{4,3,2,1,0:T(8,128)(2,1)} %bitcast.14.refs_0_, bf16[2,2,4,128,384]{4,3,2,1,0:T(8,128)(2,1)} %collective-permute-done.6.refs_1_, bf16[4,2,2,128,384]{4,3,2,1,0:T(8,128)(2,1)} %copy-done, ...), custom_call_target="tpu_custom_call" | custom-call | flops 1000 | bytes 1000 | tf_op jit(solution)/shard_map/attend_1/pallas_call | solution.py:191
  162.8 2.6 %all-gather.2.cloned.1.call-done = bf16[4096,128]{1,0:T(8,128)(2,1)} async-done(((bf16[256,128]{1,0:T(8,128)(2,1)}), bf16[4096,128]{1,0:T(8,128)(2,1)}) %all-gather.2.cloned.1.call-update) | async-done | bytes 1048592 | tf_op jit(solution)/shard_map/all_gather | solution.py:323
  165.5 3.8 %collective-permute-start.19 = (bf16[2,8,256,128]{3,2,1,0:T(8,128)(2,1)}, bf16[2,8,256,128]{3,2,1,0:T(8,128)(2,1)S(1)}, u32[]{:S(2)}, u32[]{:S(2)}) collective-permute-start(bf16[2,8,256,128]{3,2,1,0:T(8,128)(2,1)} %bitcast.65), channel_id=1, source_target_pairs={{0,1},{1,0},{2,3},{3,2},{4,5},{5,4},{6,7},{7,6},{8,9},{9,8},{10,11... | collective-permute-start | bytes 3145736 | tf_op jit(solution)/shard_map/ppermute | solution.py:272
  169.2 2.0 collective-permute-start.14
  171.3 4.3 %collective-permute-start.15 = (bf16[64,1024]{1,0:T(8,128)(2,1)S(1)}, bf16[64,1024]{1,0:T(8,128)(2,1)S(1)}, u32[]{:S(2)}, u32[]{:S(2)}) collective-permute-start(bf16[64,1024]{1,0:T(8,128)(2,1)S(1)} %get-tuple-element.18), channel_id=1, source_target_pairs={{0,4},{1,5},{2,6},{3,7},{4,0},{5,1},{6,2},{7,3},{8,12},{9,13},{10,... | collective-permute-start | bytes 393224 | tf_op jit(solution)/shard_map/ppermute | solution.py:342
  175.6 3.0 %collective-permute-start.16 = (bf16[64,1024]{1,0:T(8,128)(2,1)S(1)}, bf16[64,1024]{1,0:T(8,128)(2,1)S(1)}, u32[]{:S(2)}, u32[]{:S(2)}) collective-permute-start(bf16[64,1024]{1,0:T(8,128)(2,1)S(1)} %get-tuple-element.17), channel_id=1, source_target_pairs={{0,6},{1,7},{2,0},{3,1},{4,2},{5,3},{6,4},{7,5},{8,14},{9,15},{10,... | collective-permute-start | bytes 393224 | tf_op jit(solution)/shard_map/ppermute | solution.py:342
  178.6 0.8 fusion.3
  179.4 2.9 %collective-permute-done.16.z3 = bf16[64,1024]{1,0:T(8,128)(2,1)S(1)} collective-permute-done((bf16[64,1024]{1,0:T(8,128)(2,1)S(1)}, bf16[64,1024]{1,0:T(8,128)(2,1)S(1)}, u32[]{:S(2)}, u32[]{:S(2)}) %collective-permute-start.16) | collective-permute-done | bytes 131104 | tf_op jit(solution)/shard_map/ppermute | solution.py:342
  182.4 2.4 %collective-permute-start.17 = (bf16[4,32,1024]{2,1,0:T(8,128)(2,1)S(1)}, bf16[4,32,1024]{2,1,0:T(8,128)(2,1)S(1)}, u32[]{:S(2)}, u32[]{:S(2)}) collective-permute-start(bf16[4,32,1024]{2,1,0:T(8,128)(2,1)S(1)} %pad_maximum_fusion.4), channel_id=1, source_target_pairs={{0,8},{8,0},{1,9},{9,1},{2,10},{10,2},{3,11},{11,3},{4,12},{12,4},... | collective-permute-start | bytes 786440 | tf_op jit(solution)/shard_map/ppermute | solution.py:272
  184.8 6.0 %collective-permute-done.17.zy_ref = bf16[4,32,1024]{2,1,0:T(8,128)(2,1)S(1)} collective-permute-done((bf16[4,32,1024]{2,1,0:T(8,128)(2,1)S(1)}, bf16[4,32,1024]{2,1,0:T(8,128)(2,1)S(1)}, u32[]{:S(2)}, u32[]{:S(2)}) %collective-permute-start.17) | collective-permute-done | bytes 262176 | tf_op jit(solution)/shard_map/ppermute | solution.py:272
  190.9 4.1 %collective-permute-start.18 = (bf16[8,16,1024]{2,1,0:T(8,128)(2,1)S(1)}, bf16[8,16,1024]{2,1,0:T(8,128)(2,1)S(1)}, u32[]{:S(2)}, u32[]{:S(2)}) collective-permute-start(bf16[8,16,1024]{2,1,0:T(8,128)(2,1)S(1)} %slice_dynamic-update-slice_fusion), channel_id=1, source_target_pairs={{0,1},{1,0},{2,3},{3,2},{4,5},{5,4},{6,7},{7,6},{8,9},{9,8},{10,11... | collective-permute-start | bytes 786440 | tf_op jit(solution)/shard_map/ppermute | solution.py:272
  195.0 1.1 collective-permute-done.18.zc_ref
  196.2 0.7 copy-done.9
  196.8 4.5 %mix.1 = bf16[256,1024]{1,0:T(8,128)(2,1)} custom-call(s32[13]{0:T(128)} %concatenate.7.scalar_ref, bf16[256,1024]{1,0:T(8,128)(2,1)} %reshape.52.tokens_ref, bf16[256,1024]{1,0:T(8,128)(2,1)} %attend_1.1.x_ref, bf16[256,1024]{1,0:T(8,128)(2,1)} %bitcast.61, bf16[64,1024]{1,0:T(8,128)(2,1)} %get-tuple-element.20.z0, bf16[64,1024]{1,0:T(8,128)(2,1)} %copy-done.6, ...), custom_call_target="tpu_custom_call" | custom-call | tf_op jit(solution)/shard_map/mix/pallas_call | solution.py:241
  201.4 2.0 reshape.62
  (52 shorter events, 0.2 us)
Async XLA Ops:
  6.5 22.2 %copy-start.10 = (f32[16,127]{1,0:T(8,128)S(1)}, f32[16,127]{1,0:T(8,128)}, u32[]{:S(2)}) copy-start(f32[16,127]{1,0:T(8,128)} %param.9) | copy-start | bytes 24388
  8.7 28.9 %all-to-all-start = ((bf16[16,16,512]{2,1,0:T(8,128)(2,1)}), bf16[16,16,512]{2,1,0:T(8,128)(2,1)S(1)}, u32[]{:S(2)}, u32[]{:S(2)}) async-start(bf16[16,16,512]{2,1,0:T(8,128)(2,1)} %broadcast_in_dim.2), calls=%async_computation | async-start | bytes 524288 | tf_op jit(solution)/shard_map/all_to_all | solution.py:268
  24.5 7.0 %copy-start.11 = (f32[16,63]{1,0:T(8,128)S(1)}, f32[16,63]{1,0:T(8,128)}, u32[]{:S(2)}) copy-start(f32[16,63]{1,0:T(8,128)} %param.10) | copy-start | bytes 12100
  26.5 7.6 %copy-start.12 = (f32[16,63]{1,0:T(8,128)S(1)}, f32[16,63]{1,0:T(8,128)}, u32[]{:S(2)}) copy-start(f32[16,63]{1,0:T(8,128)} %param.11) | copy-start | bytes 12100
  37.6 22.6 %collective-permute-start.7 = (bf16[128,384]{1,0:T(8,128)(2,1)S(1)}, bf16[128,384]{1,0:T(8,128)(2,1)S(1)}, u32[]{:S(2)}, u32[]{:S(2)}) collective-permute-start(bf16[128,384]{1,0:T(8,128)(2,1)S(1)} %get-tuple-element.25), channel_id=1, source_target_pairs={{0,256},{1,257},{2,258},{3,259},{4,260},{5,261},{6,262},{7,263},{8... | collective-permute-start | bytes 294920 | tf_op jit(solution)/shard_map/ppermute | solution.py:313
  42.5 17.8 %collective-permute-start.8 = (bf16[128,384]{1,0:T(8,128)(2,1)S(1)}, bf16[128,384]{1,0:T(8,128)(2,1)S(1)}, u32[]{:S(2)}, u32[]{:S(2)}) collective-permute-start(bf16[128,384]{1,0:T(8,128)(2,1)S(1)} %get-tuple-element.25), channel_id=1, source_target_pairs={{0,8},{1,9},{2,10},{3,11},{4,12},{5,13},{6,14},{7,15},{8,256},{9,2... | collective-permute-start | bytes 294920 | tf_op jit(solution)/shard_map/ppermute | solution.py:313
  44.8 15.5 %collective-permute-start.9 = (bf16[128,384]{1,0:T(8,128)(2,1)S(1)}, bf16[128,384]{1,0:T(8,128)(2,1)S(1)}, u32[]{:S(2)}, u32[]{:S(2)}) collective-permute-start(bf16[128,384]{1,0:T(8,128)(2,1)S(1)} %get-tuple-element.25), channel_id=1, source_target_pairs={{0,264},{1,265},{2,266},{3,267},{4,268},{5,269},{6,270},{7,271},{8... | collective-permute-start | bytes 294920 | tf_op jit(solution)/shard_map/ppermute | solution.py:313
  49.0 59.4 %all-to-all-start.1 = ((bf16[32,8,1024]{2,1,0:T(8,128)(2,1)}), bf16[32,8,1024]{2,1,0:T(8,128)(2,1)S(1)}, u32[]{:S(2)}, u32[]{:S(2)}) async-start(bf16[32,8,1024]{2,1,0:T(8,128)(2,1)} %bitcast.23), calls=%async_computation.1 | async-start | bytes 1048576 | tf_op jit(solution)/shard_map/all_to_all | solution.py:268
  60.2 105.3 %all-gather.2.cloned.1.call-start = ((), (), s32[]{:S(2)}) async-start(), calls=%async_computation.4 | async-start | bytes 1114112 | tf_op jit(solution)/shard_map/all_gather | solution.py:323
  60.4 26.2 %collective-permute-start.10 = (bf16[4,128,384]{2,1,0:T(8,128)(2,1)S(1)}, bf16[4,128,384]{2,1,0:T(8,128)(2,1)S(1)}, u32[]{:S(2)}, u32[]{:S(2)}) collective-permute-start(bf16[4,128,384]{2,1,0:T(8,128)(2,1)S(1)} %pad_maximum_fusion.3), channel_id=1, source_target_pairs={{0,2},{1,3},{2,4},{3,5},{4,6},{5,7},{6,0},{7,1},{8,10},{9,11},{10,... | collective-permute-start | bytes 1179656 | tf_op jit(solution)/shard_map/ppermute | solution.py:317
  63.5 12.7 %collective-permute-start = (bf16[128,384]{1,0:T(8,128)(2,1)S(1)}, bf16[128,384]{1,0:T(8,128)(2,1)S(1)}, u32[]{:S(2)}, u32[]{:S(2)}) collective-permute-start(bf16[128,384]{1,0:T(8,128)(2,1)S(1)} %get-tuple-element.26), channel_id=1, source_target_pairs={{0,2},{1,3},{2,4},{3,5},{4,6},{5,7},{6,0},{7,1},{8,10},{9,11},{10,... | collective-permute-start | bytes 294920 | tf_op jit(solution)/shard_map/ppermute | solution.py:312
  66.6 13.0 %collective-permute-start.1 = (bf16[128,384]{1,0:T(8,128)(2,1)S(1)}, bf16[128,384]{1,0:T(8,128)(2,1)S(1)}, u32[]{:S(2)}, u32[]{:S(2)}) collective-permute-start(bf16[128,384]{1,0:T(8,128)(2,1)S(1)} %get-tuple-element.26), channel_id=1, source_target_pairs={{0,4},{1,5},{2,6},{3,7},{4,0},{5,1},{6,2},{7,3},{8,12},{9,13},{10,... | collective-permute-start | bytes 294920 | tf_op jit(solution)/shard_map/ppermute | solution.py:312
  70.0 9.6 %collective-permute-start.2 = (bf16[128,384]{1,0:T(8,128)(2,1)S(1)}, bf16[128,384]{1,0:T(8,128)(2,1)S(1)}, u32[]{:S(2)}, u32[]{:S(2)}) collective-permute-start(bf16[128,384]{1,0:T(8,128)(2,1)S(1)} %get-tuple-element.26), channel_id=1, source_target_pairs={{0,6},{1,7},{2,0},{3,1},{4,2},{5,3},{6,4},{7,5},{8,14},{9,15},{10,... | collective-permute-start | bytes 294920 | tf_op jit(solution)/shard_map/ppermute | solution.py:312
  73.8 17.1 %collective-permute-start.11 = (bf16[4,128,384]{2,1,0:T(8,128)(2,1)S(1)}, bf16[4,128,384]{2,1,0:T(8,128)(2,1)S(1)}, u32[]{:S(2)}, u32[]{:S(2)}) collective-permute-start(bf16[4,128,384]{2,1,0:T(8,128)(2,1)S(1)} %pad_maximum_fusion.3), channel_id=1, source_target_pairs={{0,4},{1,5},{2,6},{3,7},{4,0},{5,1},{6,2},{7,3},{8,12},{9,13},{10,... | collective-permute-start | bytes 1179656 | tf_op jit(solution)/shard_map/ppermute | solution.py:317
  76.2 18.3 %collective-permute-start.12 = (bf16[4,128,384]{2,1,0:T(8,128)(2,1)S(1)}, bf16[4,128,384]{2,1,0:T(8,128)(2,1)S(1)}, u32[]{:S(2)}, u32[]{:S(2)}) collective-permute-start(bf16[4,128,384]{2,1,0:T(8,128)(2,1)S(1)} %pad_maximum_fusion.3), channel_id=1, source_target_pairs={{0,6},{1,7},{2,0},{3,1},{4,2},{5,3},{6,4},{7,5},{8,14},{9,15},{10,... | collective-permute-start | bytes 1179656 | tf_op jit(solution)/shard_map/ppermute | solution.py:317
  79.7 18.8 %collective-permute-start.3 = (bf16[4,128,384]{2,1,0:T(8,128)(2,1)S(1)}, bf16[4,128,384]{2,1,0:T(8,128)(2,1)S(1)}, u32[]{:S(2)}, u32[]{:S(2)}) collective-permute-start(bf16[4,128,384]{2,1,0:T(8,128)(2,1)S(1)} %get-tuple-element.22), channel_id=1, source_target_pairs={{0,256},{1,257},{2,258},{3,259},{4,260},{5,261},{6,262},{7,263},{8... | collective-permute-start | bytes 1179656 | tf_op jit(solution)/shard_map/ppermute | solution.py:316
  84.4 16.7 %collective-permute-start.4 = (bf16[4,128,384]{2,1,0:T(8,128)(2,1)S(1)}, bf16[4,128,384]{2,1,0:T(8,128)(2,1)S(1)}, u32[]{:S(2)}, u32[]{:S(2)}) collective-permute-start(bf16[4,128,384]{2,1,0:T(8,128)(2,1)S(1)} %get-tuple-element.22), channel_id=1, source_target_pairs={{0,8},{1,9},{2,10},{3,11},{4,12},{5,13},{6,14},{7,15},{8,256},{9,2... | collective-permute-start | bytes 1179656 | tf_op jit(solution)/shard_map/ppermute | solution.py:316
  86.6 14.4 %collective-permute-start.5 = (bf16[4,128,384]{2,1,0:T(8,128)(2,1)S(1)}, bf16[4,128,384]{2,1,0:T(8,128)(2,1)S(1)}, u32[]{:S(2)}, u32[]{:S(2)}) collective-permute-start(bf16[4,128,384]{2,1,0:T(8,128)(2,1)S(1)} %get-tuple-element.22), channel_id=1, source_target_pairs={{0,264},{1,265},{2,266},{3,267},{4,268},{5,269},{6,270},{7,271},{8... | collective-permute-start | bytes 1179656 | tf_op jit(solution)/shard_map/ppermute | solution.py:316
  94.7 7.7 %copy-start = (bf16[4,2,2,128,384]{4,3,2,1,0:T(8,128)(2,1)}, bf16[4,2,2,128,384]{4,3,2,1,0:T(8,128)(2,1)S(1)}, u32[]{:S(2)}) copy-start(bf16[4,2,2,128,384]{4,3,2,1,0:T(8,128)(2,1)S(1)} %pad_maximum_fusion.1.refs_2_) | copy-start | bytes 4718596
  94.8 18.4 %collective-permute-start.13 = (bf16[4,2,2,128,384]{4,3,2,1,0:T(8,128)(2,1)S(1)}, bf16[4,2,2,128,384]{4,3,2,1,0:T(8,128)(2,1)}, u32[]{:S(2)}, u32[]{:S(2)}) collective-permute-start(bf16[4,2,2,128,384]{4,3,2,1,0:T(8,128)(2,1)S(1)} %pad_maximum_fusion.1.refs_2_), channel_id=1, source_target_pairs={{0,1},{1,0},{2,3},{3,2},{4,5},{5,4},{6,7},{7,6},{8,9},{9,8},{10,11... | collective-permute-start | bytes 4718600 | tf_op jit(solution)/shard_map/ppermute | solution.py:272
  102.5 10.7 %collective-permute-start.6 = (bf16[2,2,4,128,384]{4,3,2,1,0:T(8,128)(2,1)}, bf16[2,2,4,128,384]{4,3,2,1,0:T(8,128)(2,1)}, u32[]{:S(2)}, u32[]{:S(2)}) collective-permute-start(bf16[2,2,4,128,384]{4,3,2,1,0:T(8,128)(2,1)} %bitcast.14.refs_0_), channel_id=1, source_target_pairs={{0,1},{1,0},{2,3},{3,2},{4,5},{5,4},{6,7},{7,6},{8,9},{9,8},{10,11... | collective-permute-start | bytes 4718600 | tf_op jit(solution)/shard_map/ppermute | solution.py:272
  108.4 4.8 %copy-start.1 = (bf16[32,8,1024]{2,1,0:T(8,128)(2,1)}, bf16[32,8,1024]{2,1,0:T(8,128)(2,1)S(1)}, u32[]{:S(2)}) copy-start(bf16[32,8,1024]{2,1,0:T(8,128)(2,1)S(1)} %all-to-all-done.1) | copy-start | bytes 1572868
  108.4 15.6 %all-to-all-start.2 = ((bf16[16,16,1024]{2,1,0:T(8,128)(2,1)}), bf16[16,16,1024]{2,1,0:T(8,128)(2,1)S(1)}, u32[]{:S(2)}, u32[]{:S(2)}) async-start(bf16[16,16,1024]{2,1,0:T(8,128)(2,1)} %bitcast.25), calls=%async_computation.2 | async-start | bytes 1048576 | tf_op jit(solution)/shard_map/all_to_all | solution.py:268
  124.0 14.5 %copy-start.2 = (bf16[16,16,1024]{2,1,0:T(8,128)(2,1)}, bf16[16,16,1024]{2,1,0:T(8,128)(2,1)S(1)}, u32[]{:S(2)}) copy-start(bf16[16,16,1024]{2,1,0:T(8,128)(2,1)S(1)} %all-to-all-done.2) | copy-start | bytes 1572868
  124.0 66.9 %all-to-all-start.3 = ((bf16[32,8,1024]{2,1,0:T(8,128)(2,1)}), bf16[32,8,1024]{2,1,0:T(8,128)(2,1)S(1)}, u32[]{:S(2)}, u32[]{:S(2)}) async-start(bf16[32,8,1024]{2,1,0:T(8,128)(2,1)} %bitcast.58), calls=%async_computation.3 | async-start | bytes 1048576 | tf_op jit(solution)/shard_map/all_to_all | solution.py:268
  165.5 29.5 %collective-permute-start.19 = (bf16[2,8,256,128]{3,2,1,0:T(8,128)(2,1)}, bf16[2,8,256,128]{3,2,1,0:T(8,128)(2,1)S(1)}, u32[]{:S(2)}, u32[]{:S(2)}) collective-permute-start(bf16[2,8,256,128]{3,2,1,0:T(8,128)(2,1)} %bitcast.65), channel_id=1, source_target_pairs={{0,1},{1,0},{2,3},{3,2},{4,5},{5,4},{6,7},{7,6},{8,9},{9,8},{10,11... | collective-permute-start | bytes 3145736 | tf_op jit(solution)/shard_map/ppermute | solution.py:272
  169.2 13.1 %collective-permute-start.14 = (bf16[64,1024]{1,0:T(8,128)(2,1)S(1)}, bf16[64,1024]{1,0:T(8,128)(2,1)S(1)}, u32[]{:S(2)}, u32[]{:S(2)}) collective-permute-start(bf16[64,1024]{1,0:T(8,128)(2,1)S(1)} %get-tuple-element.19), channel_id=1, source_target_pairs={{0,2},{1,3},{2,4},{3,5},{4,6},{5,7},{6,0},{7,1},{8,10},{9,11},{10,... | collective-permute-start | bytes 393224 | tf_op jit(solution)/shard_map/ppermute | solution.py:342
  171.3 11.0 %collective-permute-start.15 = (bf16[64,1024]{1,0:T(8,128)(2,1)S(1)}, bf16[64,1024]{1,0:T(8,128)(2,1)S(1)}, u32[]{:S(2)}, u32[]{:S(2)}) collective-permute-start(bf16[64,1024]{1,0:T(8,128)(2,1)S(1)} %get-tuple-element.18), channel_id=1, source_target_pairs={{0,4},{1,5},{2,6},{3,7},{4,0},{5,1},{6,2},{7,3},{8,12},{9,13},{10,... | collective-permute-start | bytes 393224 | tf_op jit(solution)/shard_map/ppermute | solution.py:342
  175.6 6.7 %collective-permute-start.16 = (bf16[64,1024]{1,0:T(8,128)(2,1)S(1)}, bf16[64,1024]{1,0:T(8,128)(2,1)S(1)}, u32[]{:S(2)}, u32[]{:S(2)}) collective-permute-start(bf16[64,1024]{1,0:T(8,128)(2,1)S(1)} %get-tuple-element.17), channel_id=1, source_target_pairs={{0,6},{1,7},{2,0},{3,1},{4,2},{5,3},{6,4},{7,5},{8,14},{9,15},{10,... | collective-permute-start | bytes 393224 | tf_op jit(solution)/shard_map/ppermute | solution.py:342
  182.3 13.8 %copy-start.8 = (bf16[64,1024]{1,0:T(8,128)(2,1)}, bf16[64,1024]{1,0:T(8,128)(2,1)S(1)}, u32[]{:S(2)}) copy-start(bf16[64,1024]{1,0:T(8,128)(2,1)S(1)} %collective-permute-done.16.z3) | copy-start | bytes 393220
  182.3 13.8 %copy-start.7 = (bf16[64,1024]{1,0:T(8,128)(2,1)}, bf16[64,1024]{1,0:T(8,128)(2,1)S(1)}, u32[]{:S(2)}) copy-start(bf16[64,1024]{1,0:T(8,128)(2,1)S(1)} %collective-permute-done.15.z2) | copy-start | bytes 393220
  182.3 13.8 %copy-start.6 = (bf16[64,1024]{1,0:T(8,128)(2,1)}, bf16[64,1024]{1,0:T(8,128)(2,1)S(1)}, u32[]{:S(2)}) copy-start(bf16[64,1024]{1,0:T(8,128)(2,1)S(1)} %collective-permute-done.14.z1) | copy-start | bytes 393220
  182.4 8.4 %collective-permute-start.17 = (bf16[4,32,1024]{2,1,0:T(8,128)(2,1)S(1)}, bf16[4,32,1024]{2,1,0:T(8,128)(2,1)S(1)}, u32[]{:S(2)}, u32[]{:S(2)}) collective-permute-start(bf16[4,32,1024]{2,1,0:T(8,128)(2,1)S(1)} %pad_maximum_fusion.4), channel_id=1, source_target_pairs={{0,8},{8,0},{1,9},{9,1},{2,10},{10,2},{3,11},{11,3},{4,12},{12,4},... | collective-permute-start | bytes 786440 | tf_op jit(solution)/shard_map/ppermute | solution.py:272
  190.8 5.3 %copy-start.5 = (bf16[4,32,1024]{2,1,0:T(8,128)(2,1)}, bf16[4,32,1024]{2,1,0:T(8,128)(2,1)S(1)}, u32[]{:S(2)}) copy-start(bf16[4,32,1024]{2,1,0:T(8,128)(2,1)S(1)} %collective-permute-done.17.zy_ref) | copy-start | bytes 786436
  190.8 5.3 %copy-start.3 = (bf16[32,8,1024]{2,1,0:T(8,128)(2,1)}, bf16[32,8,1024]{2,1,0:T(8,128)(2,1)S(1)}, u32[]{:S(2)}) copy-start(bf16[32,8,1024]{2,1,0:T(8,128)(2,1)S(1)} %all-to-all-done.3) | copy-start | bytes 1572868
  190.9 5.3 %collective-permute-start.18 = (bf16[8,16,1024]{2,1,0:T(8,128)(2,1)S(1)}, bf16[8,16,1024]{2,1,0:T(8,128)(2,1)S(1)}, u32[]{:S(2)}, u32[]{:S(2)}) collective-permute-start(bf16[8,16,1024]{2,1,0:T(8,128)(2,1)S(1)} %slice_dynamic-update-slice_fusion), channel_id=1, source_target_pairs={{0,1},{1,0},{2,3},{3,2},{4,5},{5,4},{6,7},{7,6},{8,9},{9,8},{10,11... | collective-permute-start | bytes 786440 | tf_op jit(solution)/shard_map/ppermute | solution.py:272
  195.0 1.2 copy-start.4
  196.1 0.7 copy-start.9
Sparse Core Ops, SparseCore 0:
  108.5 56.9 all-gather.1

commit v3 on v2

v3 whole, which is shorter than its diff:
```python
import functools
import jax
import jax.numpy as jnp
from jax import lax
from jax.experimental import pallas as pl
from jax.experimental.pallas import tpu as pltpu
from jax.sharding import Mesh
from jax.sharding import PartitionSpec as P

HEADS = 16
HEAD = 64
PAIRS = HEADS // 2
BLOCK = 128
NEG = -1e30
HOPS = (0, 2, 1, 3)
DIMS = (2, 16, 2, 4, 2)
ALL = ("yh", "z", "yl", "x", "c")
GY = ("yh", "z")
GZ = ("yl", "x", "c")
BF = jnp.bfloat16
F32 = jnp.float32


def index_of(yh, z, yl, x, c):
    return (((yh * DIMS[1] + z) * DIMS[2] + yl) * DIMS[3] + x) * DIMS[4] + c


def every_device():
    for yh in range(DIMS[0]):
        for z in range(DIMS[1]):
            for yl in range(DIMS[2]):
                for x in range(DIMS[3]):
                    for c in range(DIMS[4]):
                        yield yh, z, yl, x, c


def hop_x(far):
    return [
        (index_of(*d), index_of(d[0], d[1], d[2], (d[3] + far) % DIMS[3], d[4]))
        for d in every_device()
    ]


def hop_plane(far, x_core):
    pairs = []
    for yh, z, yl, x, c in every_device():
        y = yh * 2 + yl
        if c == x_core:
            x_to, y_to = (x + far) % 4, y
        else:
            x_to, y_to = x, (y + far) % 4
        pairs.append((index_of(yh, z, yl, x, c), index_of(y_to // 2, z, y_to % 2, x_to, c)))
    return pairs


def iota(shape, dim):
    return lax.broadcasted_iota(jnp.int32, shape, dim)


def line_rows(axis, i):
    if axis == 1:
        return (i & 128) + (i & 63) * 2 + ((i >> 6) & 1)
    if axis == 2:
        return (i & 31) * 8 + (i >> 5)
    return ((i & 30) << 3) + ((i >> 5) << 1) + (i & 1)


def norm_kernel(tokens_ref, out_ref):
    values = tokens_ref[...].astype(F32)
    center = jnp.mean(values, axis=-1, keepdims=True)
    values = values - center
    spread = jnp.mean(values * values, axis=-1, keepdims=True)
    out_ref[...] = (values * lax.rsqrt(spread + 1e-05)).astype(BF)


def bias_kernel(length, table_ref, out_ref):
    lanes = iota((length, BLOCK), 1) // length
    for head in range(HEADS):
        row = jnp.broadcast_to(table_ref[head : head + 1, :], (length, BLOCK))
        for place in range(BLOCK // length):
            shift = (place * length - length + 1) % BLOCK
            turned = pltpu.roll(row, shift, 1, stride=1, stride_axis=0)
            out_ref[
                head // 2,
                place * length : (place + 1) * length,
                (head % 2) * BLOCK : (head % 2 + 1) * BLOCK,
            ] = jnp.where(lanes == place, turned, NEG)


def attend_kernel(axes, scalar_ref, *refs):
    count = len(axes)
    token_refs, refs = refs[:count], refs[count:]
    weight_refs, refs = refs[:8], refs[8:]
    bias_refs = refs[: 2 * count]
    refs = refs[-(count * 2 + 3) :]
    out_refs, back_refs = refs[:count], refs[count : 2 * count]
    lines_ref, qkv_ref, mixed_ref = refs[2 * count :]
    step = pl.program_id(0)
    rows = token_refs[0].shape[0]
    core, turned_a, turned_b, yl, x = [scalar_ref[8 + n] for n in range(5)]

    @pl.when(step == 0)
    def _():
        for a, axis in enumerate(axes):
            turn = line_rows(axis, iota((rows, 1), 0)) == iota((rows, rows), 1)
            turn = turn.astype(F32).astype(BF)
            lines = jnp.dot(turn, token_refs[a][...], preferred_element_type=F32)
            lines_ref[a * rows : (a + 1) * rows] = lines.astype(BF)
            place = iota((rows, 1), 0)
            if axis == 3:
                dx, dy, dc = place >> 6, (place >> 5) & 1, (place >> 4) & 1
                to = (yl ^ dy) * 8 + ((x + dx) & 3) * 2 + (core ^ dc)
                back = ((place >> 1) & 7) * 32 + to * 2 + (place & 1) == iota((rows, rows), 1)
            else:
                back = line_rows(axis, iota((1, rows), 1)) == iota((rows, rows), 0)
            back_refs[a][...] = back.astype(F32).astype(BF)

    width = 3 * BLOCK

    def attention():
        left = iota((BLOCK, BLOCK), 1) < HEAD
        zero = jnp.zeros((BLOCK, BLOCK), BF)
        projected = (step + 1) % 2
        for n in range(2):
            pair = scalar_ref[2 * jnp.maximum(step - 1, 0) + n]
            columns = pl.ds(pl.multiple_of(pair * BLOCK, BLOCK), BLOCK)
            for start in range(0, count * rows, BLOCK):
                q, k, v = [
                    qkv_ref[
                        projected,
                        start : start + BLOCK,
                        n * width + m * BLOCK : n * width + (m + 1) * BLOCK,
                    ]
                    for m in range(3)
                ]
                keys = jnp.concatenate([jnp.where(left, k, zero), jnp.where(left, zero, k)], axis=0)
                values = jnp.concatenate([jnp.where(left, v, zero), jnp.where(left, zero, v)], axis=0)
                scores = lax.dot_general(q, keys, (((1,), (1,)), ((), ())), preferred_element_type=F32)
                scores = scores * HEAD ** (-0.5) + bias_refs[2 * (start // rows) + n][0]
                probs = []
                for half in range(2):
                    s = scores[:, half * BLOCK : (half + 1) * BLOCK]
                    e = jnp.exp(s - jnp.max(s, axis=-1, keepdims=True))
                    probs.append((e * (1.0 / jnp.sum(e, axis=-1, keepdims=True))).astype(BF))
                probs = jnp.concatenate(probs, axis=1)
                mixed = jnp.dot(probs, values, preferred_element_type=F32).astype(BF)
                mixed_ref[start : start + BLOCK, columns] = mixed

    def projection():
        turned = jnp.where(step < 2, turned_a, turned_b)
        near_first, far_first = step < 2, step % 2 == 0
        own_first = jnp.where(core == 0, near_first, far_first)
        other_first = jnp.where(core == 0, far_first, near_first)
        own_refs, other_refs = weight_refs[:4], weight_refs[4:]
        weights = []
        for n in range(2):
            halves = []
            for m in range(2):
                own, other = [
                    [jnp.where(early, part[2 * i][j], part[2 * i + 1][j]) for i, j in ((m, n), (n, m))]
                    for part, early in ((own_refs, own_first), (other_refs, other_first))
                ]
                near = jnp.where(core == 0, own[0], other[0])
                far = jnp.where(core == 0, other[1], own[1])
                halves.append(jnp.concatenate([near, far], axis=0))
            low = jnp.where(turned == 0, halves[0], halves[1])
            high = jnp.where(turned == 0, halves[1], halves[0])
            weights.append(jnp.concatenate([low, high], axis=0))
        weights = jnp.concatenate(weights, axis=1)
        qkv = jnp.dot(lines_ref[...], weights, preferred_element_type=F32)
        qkv_ref[step % 2] = qkv.astype(BF)

    last = pl.num_programs(0) - 1

    @pl.when(step == 0)
    def _():
        projection()

    @pl.when(jnp.logical_and(step > 0, step < last))
    def _():
        attention()
        projection()

    @pl.when(step == last)
    def _():
        attention()
        for a in range(count):
            mixed = mixed_ref[a * rows : (a + 1) * rows]
            out = jnp.dot(back_refs[a][...], mixed, preferred_element_type=F32)
            out_refs[a][...] = out.astype(BF)


def attend(axes, tokens, weights, biases, scalars, after=()):
    rows, features = tokens[0].shape
    half, width = weights[0].shape[1], 3 * BLOCK
    count = len(axes)
    specs = [pl.BlockSpec((rows, features), lambda s, p: (0, 0))] * count

    for other in range(2):
        for hop in range(4):
            late = hop % 2

            def block(s, p, other=other, late=late):
                s = jnp.minimum(s, 3)
                y_part, x_part = s // 2, s % 2
                near = jnp.where(y_part == late, x_part, 1 - late)
                return (jnp.where(p[8] == other, near, y_part), 0, 0)

            specs.append(pl.BlockSpec((2, half, width), block))
    for _ in range(count):
        for n in range(2):

            def pair(s, p, n=n):
                return (p[2 * jnp.maximum(s - 1, 0) + n], 0, 0)

            specs.append(pl.BlockSpec((1, BLOCK, 2 * BLOCK), pair))
    specs.extend([pl.BlockSpec(memory_space=pl.ANY)] * len(after))
    bias_args = [b for bias in biases for b in (bias, bias)]
    return pl.pallas_call(
        functools.partial(attend_kernel, axes),
        out_shape=[jax.ShapeDtypeStruct((rows, HEADS * HEAD), BF)] * count,
        grid_spec=pltpu.PrefetchScalarGridSpec(
            num_scalar_prefetch=1,
            grid=(5,),
            in_specs=specs,
            out_specs=[pl.BlockSpec((rows, features), lambda s, p: (0, 0))] * count,
            scratch_shapes=[pltpu.VMEM((rows, rows), BF)] * count
            + [
                pltpu.VMEM((count * rows, features), BF),
                pltpu.VMEM((2, count * rows, 2 * width), BF),
                pltpu.VMEM((count * rows, features), BF),
            ],
        ),
        compiler_params=pltpu.CompilerParams(vmem_limit_bytes=61 * 2**20),
        cost_estimate=pl.CostEstimate(flops=1000, bytes_accessed=1000, transcendentals=0),
        name="attend_" + "_".join(map(str, axes)),
    )(scalars, *tokens, *weights, *bias_args, *after)


def mix_kernel(scalar_ref, tokens_ref, x_ref, y_ref, z0, z1, z2, z3, zy_ref, zc_ref, *refs):
    own_refs, other_refs, (out_ref, z_ref) = refs[:4], refs[4:8], refs[8:]
    core, turned_a, turned_b, yl, x = [scalar_ref[8 + n] for n in range(5)]
    for k, ref in enumerate((z0, z1, z2, z3)):
        for dy in range(2):
            for dc in range(2):
                if dy == 1:
                    rows = zy_ref[dc * 4 + k]
                elif dc == 1:
                    rows = zc_ref[k]
                else:
                    rows = ref[:16]
                source = (yl ^ dy) * 8 + ((x - k + 4) % 4) * 2 + (core ^ dc)
                z_ref[pl.ds(pl.multiple_of(source * 16, 16), 16), :] = rows
    summed = x_ref[...].astype(F32) + y_ref[...].astype(F32) + z_ref[...].astype(F32)
    summed = summed.astype(BF)
    for slot in range(PAIRS):
        group, k = slot // 4, slot % 4
        halves = []
        for m in (2 * group, 2 * group + 1):
            near = jnp.where(core == 0, own_refs[HOPS[m]][k], other_refs[HOPS[m]][k])
            far = jnp.where(core == 0, other_refs[HOPS[k]][m], own_refs[HOPS[k]][m])
            halves.append(jnp.concatenate([near, far], axis=0))
        turned = turned_b if group else turned_a
        low = jnp.where(turned == 0, halves[0], halves[1])
        high = jnp.where(turned == 0, halves[1], halves[0])
        weights = jnp.concatenate([low, high], axis=0)
        columns = pl.ds(pl.multiple_of(scalar_ref[slot] * BLOCK, BLOCK), BLOCK)
        result = jnp.dot(summed, weights, preferred_element_type=F32)
        out_ref[:, columns] = (tokens_ref[:, columns].astype(F32) + result).astype(BF)


def mix(scalars, tokens, along_x, along_y, along_z, weights):
    whole_block = [
        pl.BlockSpec(a.shape, lambda i, p, n=a.ndim: (0,) * n)
        for a in (tokens, along_x, along_y, *along_z)
    ]
    half = weights[0].shape[1]
    out_block = [pl.BlockSpec((4, half, BLOCK), lambda i, p: (0, 0, 3))] * 8
    return pl.pallas_call(
        mix_kernel,
        out_shape=jax.ShapeDtypeStruct(tokens.shape, BF),
        grid_spec=pltpu.PrefetchScalarGridSpec(
            num_scalar_prefetch=1,
            grid=(1,),
            in_specs=whole_block + out_block,
            out_specs=pl.BlockSpec(tokens.shape, lambda i, p: (0, 0)),
            scratch_shapes=[pltpu.VMEM(tokens.shape, BF)],
        ),
        compiler_params=pltpu.CompilerParams(vmem_limit_bytes=61 * 2**20),
        name="mix",
    )(scalars, tokens, along_x, along_y, *along_z, *weights)


def whole(kernel, out, name, scalars=0, scratch=()):
    vmem = pl.BlockSpec(memory_space=pltpu.VMEM)
    smem = pl.BlockSpec(memory_space=pltpu.SMEM)

    def call(*args):
        return pl.pallas_call(
            kernel,
            out_shape=out,
            in_specs=[smem] * scalars + [vmem] * (len(args) - scalars),
            out_specs=vmem,
            scratch_shapes=list(scratch),
            compiler_params=pltpu.CompilerParams(vmem_limit_bytes=24 * 2**20),
            name=name,
        )(*args)

    return call


def reversed_table(table):
    turned = table[:, ::-1]
    return jnp.pad(turned, ((0, 0), (0, BLOCK - turned.shape[1])))


def bias_blocks(table):
    length = (table.shape[1] + 1) // 2
    shape = jax.ShapeDtypeStruct((PAIRS, BLOCK, 2 * BLOCK), F32)
    return whole(functools.partial(bias_kernel, length), shape, f"bias_{length}")(
        reversed_table(table)
    )


def exchange(array, axes):
    return lax.all_to_all(array, axes, split_axis=0, concat_axis=0, tiled=True)


def swap(array, axis):
    return lax.ppermute(array, axis, [(0, 1), (1, 0)])


def together(array, other):
    return lax.optimization_barrier((array, other))[0]


def shards(tokens, w_qkv, w_out, bias_x, bias_y, bias_z):
    features = tokens.shape[-1]
    shape = tokens.shape
    yh, yl = lax.axis_index("yh"), lax.axis_index("yl")
    x, c = lax.axis_index("x"), lax.axis_index("c")
    pair = yl * DIMS[3] + x
    peers = DIMS[0] * DIMS[1]
    zs = DIMS[2] * DIMS[3] * DIMS[4]

    depth = w_qkv.shape[0] // 2
    mine = [
        lax.dynamic_slice(w_qkv, (c * depth, part * features + pair * BLOCK), (depth, BLOCK))
        for part in range(3)
    ]
    mine.append(lax.dynamic_slice(w_out, (c * depth, pair * BLOCK), (depth, BLOCK)))
    mine = jnp.concatenate(mine, axis=1)
    piece = exchange(jnp.broadcast_to(mine[None], (DIMS[1], *mine.shape)), "z")
    piece = piece.reshape(DIMS[1] * depth, 4 * BLOCK)
    flat = tokens.reshape(-1, features)
    rows = flat.shape[0]
    normed = whole(norm_kernel, jax.ShapeDtypeStruct(flat.shape, BF), "norm")(flat)
    blocks_x = bias_blocks(bias_x)
    blocks_y = bias_blocks(bias_y)
    blocks_z = bias_blocks(bias_z)
    normed = together(normed, (blocks_x, blocks_y, blocks_z))
    piece = together(piece, normed)

    y_lines = exchange(normed.reshape(peers, -1, features), GY).reshape(rows, features)
    z_lines = exchange(together(normed, y_lines).reshape(zs, -1, features), GZ)
    z_lines = z_lines.reshape(rows, features)

    tall = piece.shape[0] // 2
    kept = jnp.where(c == 0, piece[:tall], piece[tall:])
    taken = swap(jnp.where(c == 0, piece[tall:], piece[:tall]), "c")
    rows_of = [jnp.where(c == 0, kept, taken), jnp.where(c == 0, taken, kept)]
    rows_of = [r.reshape(-1, depth, 4 * BLOCK) for r in rows_of]
    piece = jnp.stack(rows_of, axis=1).reshape(-1, 4 * BLOCK)
    first = [piece] + [lax.ppermute(piece, ALL, hop_plane(k, 0)) for k in range(1, 4)]
    first = jnp.stack([first[k] for k in HOPS])
    second = [first] + [lax.ppermute(first, ALL, hop_plane(k, 1)) for k in range(1, 4)]
    waits = {1: y_lines, 2: z_lines}
    others = [
        swap(together(second[k], waits[k]) if k in waits else second[k], "c") for k in range(4)
    ]

    columns = (x - jnp.array(HOPS)) % DIMS[3]
    y = yh * 2 + yl
    turned_b = ((y - 1) % 4) // 2
    scalars = jnp.concatenate(
        [yl * 4 + columns, (1 - yl) * 4 + columns, jnp.stack([c, yh, turned_b, yl, x])]
    ).astype(jnp.int32)

    every = (*second, *others)
    (along_y,) = attend((2,), (y_lines,), every, (blocks_y,), scalars)
    z, along_x = attend((3, 1), (z_lines, normed), every, (blocks_z, blocks_x), scalars, (along_y,))
    along_y = exchange(together(along_y, z_lines).reshape(peers, -1, features), GY)
    along_y = along_y.reshape(rows, features)

    z = z.reshape(4, rows // 4, features)
    back = [z[0]] + [lax.ppermute(z[k], ALL, hop_x(k)) for k in range(1, 4)]
    back_c = jnp.stack([b[r : r + 16] for r in (16, 48) for b in back])
    back_c = swap(together(back_c, along_y), "c")
    back_y = jnp.concatenate([jnp.stack([b[32:48] for b in back]), back_c[4:]], axis=0)
    back_y = swap(back_y, "yl")
    mixed = mix(scalars, flat, along_x, along_y, (*back, back_y, back_c), every)
    return mixed.reshape(shape)


def solution(mesh):
    torus = Mesh(mesh.devices.reshape(DIMS), ALL)
    in_specs = (P(None, None, GY, GZ, None), P(GY, None), P(GY, None), P(), P(), P())
    return jax.shard_map(
        shards, mesh=torus, in_specs=in_specs, out_specs=in_specs[0], check_vma=False
    )
```

time: 212 us -> 190 us (0.90)
  waiting for transfers between devices: 19.7 us -> 44.5 us
  starting transfers between devices: 116 us -> 94.9 us
  between operations: 13.9 us -> 0.48 us
  Pallas kernels: 45.3 us -> 33.7 us
    ppermute x12 -> x6, starting transfers between devices: 41.6 us -> 20.1 us  [the longest x3 10.2 us: shards(): lax.ppermute(piece, ALL, hop_plane(k, 0))]
    ppermute x12 -> x6, waiting for transfers between devices: 6.19 us -> 17.7 us  [the longest x3 9.91 us: shards(): lax.ppermute(first, ALL, hop_plane(k, 1))]
    pallas_call x5 -> x4, Pallas kernels: 12.8 us -> 2.13 us  [call(): pl.pallas_call(kernel, out_shape=out, in_specs=[smem] * scalars + [vmem]...]
    all_to_all x4, waiting for transfers between devices: 0.78 us -> 10.1 us  [exchange(): return lax.all_to_all(array, axes, split_axis=0, concat_axis=0, tiled=True)]
    unnamed x30 -> x43, local copies, waits for them, and re-layouts: 1.49 us -> 7.23 us
    all_to_all x4, starting transfers between devices: 45.6 us -> 49.7 us  [exchange(): return lax.all_to_all(array, axes, split_axis=0, concat_axis=0, tiled=True)]
    ppermute x5 -> x7, waiting for transfers between devices: 7.14 us -> 10.8 us  [swap(): return lax.ppermute(array, axis, [(0, 1), (1, 0)])]
    ppermute x3, waiting for transfers between devices: 2.9 us -> 5.87 us  [shards(): back = [z[0]] + [lax.ppermute(z[k], ALL, hop_x(k)) for k in range(1, 4)]]
  transfers between devices with their start and end apart: 25 -> 20, of which waited for: 7 -> 11; matrix products, arithmetic and copies ran while one was open for 5% -> 3% of each run, Pallas kernels for 19% -> 9%
where the time goes in v3:
time: 190 us; the launch traced here: 188 us
  starting transfers between devices  94.9 us (50%)
  waiting for transfers between devices  44.5 us (23%)
  Pallas kernels  33.7 us (18%)
  local copies, waits for them, and re-layouts  14.4 us (8%)
    all_to_all x4, starting transfers between devices, exchange(): return lax.all_to_all(array, axes, split_axis=0, concat_axis=0, tiled=True)  49.7 us
    pallas_call x2, Pallas kernels, attend(): pl.pallas_call(functools.partial(attend_kernel, axes), out_shape=[jax.Sha...  26.2 us
    ppermute x7, starting transfers between devices, swap(): return lax.ppermute(array, axis, [(0, 1), (1, 0)])  16.3 us
    ppermute x7, waiting for transfers between devices, swap(): return lax.ppermute(array, axis, [(0, 1), (1, 0)])  10.8 us
    ppermute x3, starting transfers between devices, shards(): lax.ppermute(piece, ALL, hop_plane(k, 0))  10.2 us
    all_to_all x4, waiting for transfers between devices, exchange(): return lax.all_to_all(array, axes, split_axis=0, concat_axis=0, tiled=True)  10.1 us
    ppermute x3, starting transfers between devices, shards(): lax.ppermute(first, ALL, hop_plane(k, 1))  9.94 us
    ppermute x3, waiting for transfers between devices, shards(): lax.ppermute(first, ALL, hop_plane(k, 1))  9.91 us
  transfers between devices with their start and end apart: 20, of which 11 were waited for; matrix products, arithmetic and copies ran while one was open for 3% of the time, Pallas kernels for 9%

profile of v3, /device:TPU:1, one launch (start us, length us, event | category | flops | bytes accessed | tf_op | source)
XLA Modules:
  0.0 188.1 jit_solution(14053402242251858193)
XLA Ops:
  0.0 0.7 dynamic_slice.15
  0.7 0.7 fusion.11
  1.5 0.7 broadcast_in_dim.2
  2.2 15.9 %all-to-all-start.2 = ((bf16[16,16,512]{2,1,0:T(8,128)(2,1)}), bf16[16,16,512]{2,1,0:T(8,128)(2,1)S(1)}, u32[]{:S(2)}, u32[]{:S(2)}) async-start(bf16[16,16,512]{2,1,0:T(8,128)(2,1)} %broadcast_in_dim.2), calls=%async_computation.2 | async-start | bytes 524288 | tf_op jit(solution)/shard_map/all_to_all | solution.py:326
  18.1 0.0 copy-start.15
  18.1 0.1 rev.9
  18.2 0.6 copy-done.15
  18.8 0.1 rev.10
  18.9 0.7 copy-done.16
  19.6 0.1 rev.11
  19.7 0.2 reshape.40.tokens_ref
  19.9 0.0 copy-start.3
  19.9 1.1 norm.1.refs_1_
  21.0 0.3 bias_32.3.refs_10_.refs_11_
  21.4 1.0 copy-done.1
  22.3 0.3 bias_32.2.refs_9_.refs_10_
  22.7 1.0 copy-done
  23.6 0.3 bias_64.1.refs_12_.refs_13_
  24.0 1.0 copy-done.2
  24.9 6.3 %all-to-all-done.2 = bf16[16,16,512]{2,1,0:T(8,128)(2,1)S(1)} async-done(((bf16[16,16,512]{2,1,0:T(8,128)(2,1)}), bf16[16,16,512]{2,1,0:T(8,128)(2,1)S(1)}, u32[]{:S(2)}, u32[]{:S(2)}) %all-to-all-start.2) | async-done | bytes 262176 | tf_op jit(solution)/shard_map/all_to_all | solution.py:326
  31.2 13.9 %all-to-all-start = ((bf16[32,8,1024]{2,1,0:T(8,128)(2,1)}), bf16[32,8,1024]{2,1,0:T(8,128)(2,1)S(1)}, u32[]{:S(2)}, u32[]{:S(2)}) async-start(bf16[32,8,1024]{2,1,0:T(8,128)(2,1)} %bitcast.5), calls=%async_computation | async-start | bytes 1048576 | tf_op jit(solution)/shard_map/all_to_all | solution.py:326
  45.1 2.9 %collective-permute-start = (bf16[128,512]{1,0:T(8,128)(2,1)S(1)}, bf16[128,512]{1,0:T(8,128)(2,1)S(1)}, u32[]{:S(2)}, u32[]{:S(2)}) collective-permute-start(bf16[128,512]{1,0:T(8,128)(2,1)S(1)} %broadcast_select_fusion.2), channel_id=1, source_target_pairs={{0,1},{1,0},{2,3},{3,2},{4,5},{5,4},{6,7},{7,6},{8,9},{9,8},{10,11... | collective-permute-start | bytes 393224 | tf_op jit(solution)/shard_map/ppermute | solution.py:330
  48.1 1.0 collective-permute-done
  49.1 4.8 %collective-permute-start.3 = (bf16[256,512]{1,0:T(8,128)(2,1)S(1)}, bf16[256,512]{1,0:T(8,128)(2,1)S(1)}, u32[]{:S(2)}, u32[]{:S(2)}) collective-permute-start(bf16[256,512]{1,0:T(8,128)(2,1)S(1)} %bitcast.67), channel_id=1, source_target_pairs={{0,6},{1,265},{2,0},{3,267},{4,2},{5,269},{6,4},{7,271},{8,14},{9,... | collective-permute-start | bytes 786440 | tf_op jit(solution)/shard_map/ppermute | solution.py:374
  53.9 1.9 %collective-permute-start.2 = (bf16[256,512]{1,0:T(8,128)(2,1)S(1)}, bf16[256,512]{1,0:T(8,128)(2,1)S(1)}, u32[]{:S(2)}, u32[]{:S(2)}) collective-permute-start(bf16[256,512]{1,0:T(8,128)(2,1)S(1)} %bitcast.68), channel_id=1, source_target_pairs={{0,2},{1,9},{2,4},{3,11},{4,6},{5,13},{6,0},{7,15},{8,10},{9,257},... | collective-permute-start | bytes 786440 | tf_op jit(solution)/shard_map/ppermute | solution.py:374
  55.8 3.5 %collective-permute-start.1 = (bf16[256,512]{1,0:T(8,128)(2,1)S(1)}, bf16[256,512]{1,0:T(8,128)(2,1)S(1)}, u32[]{:S(2)}, u32[]{:S(2)}) collective-permute-start(bf16[256,512]{1,0:T(8,128)(2,1)S(1)} %bitcast.69), channel_id=1, source_target_pairs={{0,4},{1,257},{2,6},{3,259},{4,0},{5,261},{6,2},{7,263},{8,12},{9,... | collective-permute-start | bytes 786440 | tf_op jit(solution)/shard_map/ppermute | solution.py:374
  59.3 7.7 %collective-permute-done.2 = bf16[256,512]{1,0:T(8,128)(2,1)S(1)} collective-permute-done((bf16[256,512]{1,0:T(8,128)(2,1)S(1)}, bf16[256,512]{1,0:T(8,128)(2,1)S(1)}, u32[]{:S(2)}, u32[]{:S(2)}) %collective-permute-start.2) | collective-permute-done | bytes 262176 | tf_op jit(solution)/shard_map/ppermute | solution.py:374
  67.1 0.0 collective-permute-done.1
  67.1 0.1 pad_maximum_fusion.refs_1_.refs_2_.refs_0_
  67.2 3.1 %collective-permute-start.4 = (bf16[4,256,512]{2,1,0:T(8,128)(2,1)S(1)}, bf16[4,256,512]{2,1,0:T(8,128)(2,1)S(1)}, u32[]{:S(2)}, u32[]{:S(2)}) collective-permute-start(bf16[4,256,512]{2,1,0:T(8,128)(2,1)S(1)} %pad_maximum_fusion.refs_1_.refs_2_.refs_0_), channel_id=1, source_target_pairs={{0,8},{1,3},{2,10},{3,5},{4,12},{5,7},{6,14},{7,1},{8,256},{9,11},... | collective-permute-start | bytes 3145736 | tf_op jit(solution)/shard_map/ppermute | solution.py:376
  70.4 3.4 %collective-permute-start.6 = (bf16[4,256,512]{2,1,0:T(8,128)(2,1)S(1)}, bf16[4,256,512]{2,1,0:T(8,128)(2,1)}, u32[]{:S(2)}, u32[]{:S(2)}) collective-permute-start(bf16[4,256,512]{2,1,0:T(8,128)(2,1)S(1)} %pad_maximum_fusion.refs_1_.refs_2_.refs_0_), channel_id=1, source_target_pairs={{0,264},{1,7},{2,266},{3,1},{4,268},{5,3},{6,270},{7,5},{8,0},{9,1... | collective-permute-start | bytes 3145736 | tf_op jit(solution)/shard_map/ppermute | solution.py:376
  73.8 3.4 %collective-permute-start.5 = (bf16[4,256,512]{2,1,0:T(8,128)(2,1)S(1)}, bf16[4,256,512]{2,1,0:T(8,128)(2,1)}, u32[]{:S(2)}, u32[]{:S(2)}) collective-permute-start(bf16[4,256,512]{2,1,0:T(8,128)(2,1)S(1)} %pad_maximum_fusion.refs_1_.refs_2_.refs_0_), channel_id=1, source_target_pairs={{0,256},{1,5},{2,258},{3,7},{4,260},{5,1},{6,262},{7,3},{8,264},{9... | collective-permute-start | bytes 3145736 | tf_op jit(solution)/shard_map/ppermute | solution.py:376
  77.2 0.1 all-to-all-done
  77.3 6.0 %all-to-all-start.1 = ((bf16[16,16,1024]{2,1,0:T(8,128)(2,1)}), bf16[16,16,1024]{2,1,0:T(8,128)(2,1)}, u32[]{:S(2)}, u32[]{:S(2)}) async-start(bf16[16,16,1024]{2,1,0:T(8,128)(2,1)} %bitcast.7), calls=%async_computation.1 | async-start | bytes 1048576 | tf_op jit(solution)/shard_map/all_to_all | solution.py:326
  83.3 2.1 %collective-permute-start.7 = (bf16[4,256,512]{2,1,0:T(8,128)(2,1)S(1)}, bf16[4,256,512]{2,1,0:T(8,128)(2,1)}, u32[]{:S(2)}, u32[]{:S(2)}) collective-permute-start(bf16[4,256,512]{2,1,0:T(8,128)(2,1)S(1)} %pad_maximum_fusion.refs_1_.refs_2_.refs_0_), channel_id=1, source_target_pairs={{0,1},{1,0},{2,3},{3,2},{4,5},{5,4},{6,7},{7,6},{8,9},{9,8},{10,11... | collective-permute-start | bytes 3145736 | tf_op jit(solution)/shard_map/ppermute | solution.py:330
  85.3 2.3 %collective-permute-start.8 = (bf16[4,256,512]{2,1,0:T(8,128)(2,1)S(1)}, bf16[4,256,512]{2,1,0:T(8,128)(2,1)}, u32[]{:S(2)}, u32[]{:S(2)}) collective-permute-start(bf16[4,256,512]{2,1,0:T(8,128)(2,1)S(1)} %collective-permute-done.4.refs_2_.refs_3_.refs_1_), channel_id=1, source_target_pairs={{0,1},{1,0},{2,3},{3,2},{4,5},{5,4},{6,7},{7,6},{8,9},{9,8},{10,11... | collective-permute-start | bytes 3145736 | tf_op jit(solution)/shard_map/ppermute | solution.py:330
  87.6 3.4 %collective-permute-done.6.refs_4_.refs_5_.refs_3_ = bf16[4,256,512]{2,1,0:T(8,128)(2,1)} collective-permute-done((bf16[4,256,512]{2,1,0:T(8,128)(2,1)S(1)}, bf16[4,256,512]{2,1,0:T(8,128)(2,1)}, u32[]{:S(2)}, u32[]{:S(2)}) %collective-permute-start.6) | collective-permute-done | bytes 1048608 | tf_op jit(solution)/shard_map/ppermute | solution.py:376
  91.0 1.9 %collective-permute-start.10 = (bf16[4,256,512]{2,1,0:T(8,128)(2,1)}, bf16[4,256,512]{2,1,0:T(8,128)(2,1)}, u32[]{:S(2)}, u32[]{:S(2)}) collective-permute-start(bf16[4,256,512]{2,1,0:T(8,128)(2,1)} %collective-permute-done.6.refs_4_.refs_5_.refs_3_), channel_id=1, source_target_pairs={{0,1},{1,0},{2,3},{3,2},{4,5},{5,4},{6,7},{7,6},{8,9},{9,8},{10,11... | collective-permute-start | bytes 3145736 | tf_op jit(solution)/shard_map/ppermute | solution.py:330
  92.9 6.5 %collective-permute-done.5.refs_3_.refs_4_.refs_2_ = bf16[4,256,512]{2,1,0:T(8,128)(2,1)} collective-permute-done((bf16[4,256,512]{2,1,0:T(8,128)(2,1)S(1)}, bf16[4,256,512]{2,1,0:T(8,128)(2,1)}, u32[]{:S(2)}, u32[]{:S(2)}) %collective-permute-start.5) | collective-permute-done | bytes 1048608 | tf_op jit(solution)/shard_map/ppermute | solution.py:376
  99.4 3.8 %all-to-all-done.1 = bf16[16,16,1024]{2,1,0:T(8,128)(2,1)} async-done(((bf16[16,16,1024]{2,1,0:T(8,128)(2,1)}), bf16[16,16,1024]{2,1,0:T(8,128)(2,1)}, u32[]{:S(2)}, u32[]{:S(2)}) %all-to-all-start.1) | async-done | bytes 524320 | tf_op jit(solution)/shard_map/all_to_all | solution.py:326
  103.2 2.3 %collective-permute-start.9 = (bf16[4,256,512]{2,1,0:T(8,128)(2,1)}, bf16[4,256,512]{2,1,0:T(8,128)(2,1)}, u32[]{:S(2)}, u32[]{:S(2)}) collective-permute-start(bf16[4,256,512]{2,1,0:T(8,128)(2,1)} %collective-permute-done.5.refs_3_.refs_4_.refs_2_), channel_id=1, source_target_pairs={{0,1},{1,0},{2,3},{3,2},{4,5},{5,4},{6,7},{7,6},{8,9},{9,8},{10,11... | collective-permute-start | bytes 3145736 | tf_op jit(solution)/shard_map/ppermute | solution.py:330
  105.6 0.0 copy-start.17
  105.6 0.6 copy-done.17
  106.2 0.7 concatenate.9.scalar_ref
  106.9 0.0 collective-permute-done.7.refs_5_.refs_6_.refs_4_
  106.9 0.0 collective-permute-done.10.refs_8_.refs_9_.refs_7_
  106.9 1.2 collective-permute-done.9.refs_7_.refs_8_.refs_6_
  108.1 11.2 %attend_2.1.refs_14_ = bf16[256,1024]{1,0:T(8,128)(2,1)} custom-call(s32[13]{0:T(128)} %concatenate.9.scalar_ref, bf16[256,1024]{1,0:T(8,128)(2,1)} %bitcast.65, bf16[4,256,512]{2,1,0:T(8,128)(2,1)} %copy-done.4, bf16[4,256,512]{2,1,0:T(8,128)(2,1)} %copy-done.5, bf16[4,256,512]{2,1,0:T(8,128)(2,1)} %collective-permute-done.5.refs_3_.refs_4_.refs_2_, ...), custom_call_target="tpu_custom_call" | custom-call | flops 1000 | bytes 1000 | tf_op jit(solution)/shard_map/attend_2/pallas_call | solution.py:219
  119.3 14.0 %all-to-all-start.3 = ((bf16[32,8,1024]{2,1,0:T(8,128)(2,1)}), bf16[32,8,1024]{2,1,0:T(8,128)(2,1)S(1)}, u32[]{:S(2)}, u32[]{:S(2)}) async-start(bf16[32,8,1024]{2,1,0:T(8,128)(2,1)} %bitcast.62), calls=%async_computation.3 | async-start | bytes 1048576 | tf_op jit(solution)/shard_map/all_to_all | solution.py:326
  133.4 15.0 %attend_3_1.1 = (bf16[256,1024]{1,0:T(8,128)(2,1)}, bf16[256,1024]{1,0:T(8,128)(2,1)}) custom-call(s32[13]{0:T(128)} %concatenate.9.scalar_ref, bf16[256,1024]{1,0:T(8,128)(2,1)} %bitcast.8.refs_0_, bf16[256,1024]{1,0:T(8,128)(2,1)} %norm.1.refs_1_, bf16[4,256,512]{2,1,0:T(8,128)(2,1)} %copy-done.4, bf16[4,256,512]{2,1,0:T(8,128)(2,1)} %copy-done.5, ...), custom_call_target="tpu_custom_call" | custom-call | flops 1000 | bytes 1000 | tf_op jit(solution)/shard_map/attend_3_1/pallas_call | solution.py:219
  148.3 1.8 fusion.10
  150.1 4.3 %collective-permute-start.13 = (bf16[64,1024]{1,0:T(8,128)(2,1)S(1)}, bf16[64,1024]{1,0:T(8,128)(2,1)S(1)}, u32[]{:S(2)}, u32[]{:S(2)}) collective-permute-start(bf16[64,1024]{1,0:T(8,128)(2,1)S(1)} %get-tuple-element.27), channel_id=1, source_target_pairs={{0,6},{1,7},{2,0},{3,1},{4,2},{5,3},{6,4},{7,5},{8,14},{9,15},{10,... | collective-permute-start | bytes 393224 | tf_op jit(solution)/shard_map/ppermute | solution.py:396
  154.4 1.9 %collective-permute-start.12 = (bf16[64,1024]{1,0:T(8,128)(2,1)S(1)}, bf16[64,1024]{1,0:T(8,128)(2,1)S(1)}, u32[]{:S(2)}, u32[]{:S(2)}) collective-permute-start(bf16[64,1024]{1,0:T(8,128)(2,1)S(1)} %get-tuple-element.28), channel_id=1, source_target_pairs={{0,4},{1,5},{2,6},{3,7},{4,0},{5,1},{6,2},{7,3},{8,12},{9,13},{10,... | collective-permute-start | bytes 393224 | tf_op jit(solution)/shard_map/ppermute | solution.py:396
  156.3 2.5 %collective-permute-start.11 = (bf16[64,1024]{1,0:T(8,128)(2,1)S(1)}, bf16[64,1024]{1,0:T(8,128)(2,1)S(1)}, u32[]{:S(2)}, u32[]{:S(2)}) collective-permute-start(bf16[64,1024]{1,0:T(8,128)(2,1)S(1)} %get-tuple-element.29), channel_id=1, source_target_pairs={{0,2},{1,3},{2,4},{3,5},{4,6},{5,7},{6,0},{7,1},{8,10},{9,11},{10,... | collective-permute-start | bytes 393224 | tf_op jit(solution)/shard_map/ppermute | solution.py:396
  158.8 0.8 bitcast_dynamic-update-slice_fusion.1
  159.6 5.9 %collective-permute-done.11.z1 = bf16[64,1024]{1,0:T(8,128)(2,1)S(1)} collective-permute-done((bf16[64,1024]{1,0:T(8,128)(2,1)S(1)}, bf16[64,1024]{1,0:T(8,128)(2,1)S(1)}, u32[]{:S(2)}, u32[]{:S(2)}) %collective-permute-start.11) | collective-permute-done | bytes 131104 | tf_op jit(solution)/shard_map/ppermute | solution.py:396
  165.5 0.9 bitcast_dynamic-update-slice_fusion
  166.5 3.0 %collective-permute-start.14 = (bf16[8,16,1024]{2,1,0:T(8,128)(2,1)S(1)}, bf16[8,16,1024]{2,1,0:T(8,128)(2,1)S(1)}, u32[]{:S(2)}, u32[]{:S(2)}) collective-permute-start(bf16[8,16,1024]{2,1,0:T(8,128)(2,1)S(1)} %get-tuple-element.22), channel_id=1, source_target_pairs={{0,1},{1,0},{2,3},{3,2},{4,5},{5,4},{6,7},{7,6},{8,9},{9,8},{10,11... | collective-permute-start | bytes 786440 | tf_op jit(solution)/shard_map/ppermute | solution.py:330
  169.5 1.1 collective-permute-done.14.zc_ref
  170.6 1.9 %collective-permute-start.15 = (bf16[8,16,1024]{2,1,0:T(8,128)(2,1)S(1)}, bf16[8,16,1024]{2,1,0:T(8,128)(2,1)S(1)}, u32[]{:S(2)}, u32[]{:S(2)}) collective-permute-start(bf16[8,16,1024]{2,1,0:T(8,128)(2,1)S(1)} %slice_dynamic-update-slice_fusion), channel_id=1, source_target_pairs={{0,8},{8,0},{1,9},{9,1},{2,10},{10,2},{3,11},{11,3},{4,12},{12,4},... | collective-permute-start | bytes 786440 | tf_op jit(solution)/shard_map/ppermute | solution.py:330
  172.6 7.5 %collective-permute-done.15.zy_ref = bf16[8,16,1024]{2,1,0:T(8,128)(2,1)S(1)} collective-permute-done((bf16[8,16,1024]{2,1,0:T(8,128)(2,1)S(1)}, bf16[8,16,1024]{2,1,0:T(8,128)(2,1)S(1)}, u32[]{:S(2)}, u32[]{:S(2)}) %collective-permute-start.15) | collective-permute-done | bytes 262176 | tf_op jit(solution)/shard_map/ppermute | solution.py:330
  180.0 0.7 copy-done.13
  180.7 5.3 %mix.1 = bf16[256,1024]{1,0:T(8,128)(2,1)} custom-call(s32[13]{0:T(128)} %concatenate.9.scalar_ref, bf16[256,1024]{1,0:T(8,128)(2,1)} %copy-done.3, bf16[256,1024]{1,0:T(8,128)(2,1)} %get-tuple-element.19.x_ref, bf16[256,1024]{1,0:T(8,128)(2,1)} %bitcast.66, bf16[64,1024]{1,0:T(8,128)(2,1)} %get-tuple-element.30.z0, bf16[64,1024]{1,0:T(8,128)(2,1)} %copy-done.12, ...), custom_call_target="tpu_custom_call" | custom-call | tf_op jit(solution)/shard_map/mix/pallas_call | solution.py:279
  186.1 2.0 %reshape.49 = bf16[2,64,1,2,1024]{4,3,1,0,2:T(2,128)(2,1)} reshape(bf16[256,1024]{1,0:T(8,128)(2,1)} %mix.1) | data formatting | bytes 1048576 | tf_op jit(solution)/shard_map/reshape | solution.py:402
  (48 shorter events, 0.2 us)
Async XLA Ops:
  0.0 19.7 %copy-start.9 = (bf16[2,64,1,2,1024]{4,3,2,1,0:T(2,128)(2,1)S(1)}, bf16[2,64,1,2,1024]{4,3,2,1,0:T(2,128)(2,1)}, u32[]{:S(2)}) copy-start(bf16[2,64,1,2,1024]{4,3,2,1,0:T(2,128)(2,1)} %param.7) | copy-start | bytes 1572868
  2.2 15.9 %copy-start.14 = (f32[16,127]{1,0:T(8,128)S(1)}, f32[16,127]{1,0:T(8,128)}, u32[]{:S(2)}) copy-start(f32[16,127]{1,0:T(8,128)} %param.10) | copy-start | bytes 24388
  2.2 29.0 %all-to-all-start.2 = ((bf16[16,16,512]{2,1,0:T(8,128)(2,1)}), bf16[16,16,512]{2,1,0:T(8,128)(2,1)S(1)}, u32[]{:S(2)}, u32[]{:S(2)}) async-start(bf16[16,16,512]{2,1,0:T(8,128)(2,1)} %broadcast_in_dim.2), calls=%async_computation.2 | async-start | bytes 524288 | tf_op jit(solution)/shard_map/all_to_all | solution.py:326
  18.1 0.7 copy-start.15
  18.9 0.7 copy-start.16
  19.9 1.2 copy-start.3
  21.4 1.0 copy-start.1
  22.7 1.0 copy-start
  24.0 1.0 copy-start.2
  31.2 46.0 %all-to-all-start = ((bf16[32,8,1024]{2,1,0:T(8,128)(2,1)}), bf16[32,8,1024]{2,1,0:T(8,128)(2,1)S(1)}, u32[]{:S(2)}, u32[]{:S(2)}) async-start(bf16[32,8,1024]{2,1,0:T(8,128)(2,1)} %bitcast.5), calls=%async_computation | async-start | bytes 1048576 | tf_op jit(solution)/shard_map/all_to_all | solution.py:326
  45.1 3.9 %collective-permute-start = (bf16[128,512]{1,0:T(8,128)(2,1)S(1)}, bf16[128,512]{1,0:T(8,128)(2,1)S(1)}, u32[]{:S(2)}, u32[]{:S(2)}) collective-permute-start(bf16[128,512]{1,0:T(8,128)(2,1)S(1)} %broadcast_select_fusion.2), channel_id=1, source_target_pairs={{0,1},{1,0},{2,3},{3,2},{4,5},{5,4},{6,7},{7,6},{8,9},{9,8},{10,11... | collective-permute-start | bytes 393224 | tf_op jit(solution)/shard_map/ppermute | solution.py:330
  49.1 10.2 %collective-permute-start.3 = (bf16[256,512]{1,0:T(8,128)(2,1)S(1)}, bf16[256,512]{1,0:T(8,128)(2,1)S(1)}, u32[]{:S(2)}, u32[]{:S(2)}) collective-permute-start(bf16[256,512]{1,0:T(8,128)(2,1)S(1)} %bitcast.67), channel_id=1, source_target_pairs={{0,6},{1,265},{2,0},{3,267},{4,2},{5,269},{6,4},{7,271},{8,14},{9,... | collective-permute-start | bytes 786440 | tf_op jit(solution)/shard_map/ppermute | solution.py:374
  53.9 13.2 %collective-permute-start.2 = (bf16[256,512]{1,0:T(8,128)(2,1)S(1)}, bf16[256,512]{1,0:T(8,128)(2,1)S(1)}, u32[]{:S(2)}, u32[]{:S(2)}) collective-permute-start(bf16[256,512]{1,0:T(8,128)(2,1)S(1)} %bitcast.68), channel_id=1, source_target_pairs={{0,2},{1,9},{2,4},{3,11},{4,6},{5,13},{6,0},{7,15},{8,10},{9,257},... | collective-permute-start | bytes 786440 | tf_op jit(solution)/shard_map/ppermute | solution.py:374
  55.8 11.3 %collective-permute-start.1 = (bf16[256,512]{1,0:T(8,128)(2,1)S(1)}, bf16[256,512]{1,0:T(8,128)(2,1)S(1)}, u32[]{:S(2)}, u32[]{:S(2)}) collective-permute-start(bf16[256,512]{1,0:T(8,128)(2,1)S(1)} %bitcast.69), channel_id=1, source_target_pairs={{0,4},{1,257},{2,6},{3,259},{4,0},{5,261},{6,2},{7,263},{8,12},{9,... | collective-permute-start | bytes 786440 | tf_op jit(solution)/shard_map/ppermute | solution.py:374
  67.2 40.9 %copy-start.4 = (bf16[4,256,512]{2,1,0:T(8,128)(2,1)}, bf16[4,256,512]{2,1,0:T(8,128)(2,1)S(1)}, u32[]{:S(2)}) copy-start(bf16[4,256,512]{2,1,0:T(8,128)(2,1)S(1)} %pad_maximum_fusion.refs_1_.refs_2_.refs_0_) | copy-start | bytes 3145732
  67.2 18.1 %collective-permute-start.4 = (bf16[4,256,512]{2,1,0:T(8,128)(2,1)S(1)}, bf16[4,256,512]{2,1,0:T(8,128)(2,1)S(1)}, u32[]{:S(2)}, u32[]{:S(2)}) collective-permute-start(bf16[4,256,512]{2,1,0:T(8,128)(2,1)S(1)} %pad_maximum_fusion.refs_1_.refs_2_.refs_0_), channel_id=1, source_target_pairs={{0,8},{1,3},{2,10},{3,5},{4,12},{5,7},{6,14},{7,1},{8,256},{9,11},... | collective-permute-start | bytes 3145736 | tf_op jit(solution)/shard_map/ppermute | solution.py:376
  70.4 20.6 %collective-permute-start.6 = (bf16[4,256,512]{2,1,0:T(8,128)(2,1)S(1)}, bf16[4,256,512]{2,1,0:T(8,128)(2,1)}, u32[]{:S(2)}, u32[]{:S(2)}) collective-permute-start(bf16[4,256,512]{2,1,0:T(8,128)(2,1)S(1)} %pad_maximum_fusion.refs_1_.refs_2_.refs_0_), channel_id=1, source_target_pairs={{0,264},{1,7},{2,266},{3,1},{4,268},{5,3},{6,270},{7,5},{8,0},{9,1... | collective-permute-start | bytes 3145736 | tf_op jit(solution)/shard_map/ppermute | solution.py:376
  73.8 25.7 %collective-permute-start.5 = (bf16[4,256,512]{2,1,0:T(8,128)(2,1)S(1)}, bf16[4,256,512]{2,1,0:T(8,128)(2,1)}, u32[]{:S(2)}, u32[]{:S(2)}) collective-permute-start(bf16[4,256,512]{2,1,0:T(8,128)(2,1)S(1)} %pad_maximum_fusion.refs_1_.refs_2_.refs_0_), channel_id=1, source_target_pairs={{0,256},{1,5},{2,258},{3,7},{4,260},{5,1},{6,262},{7,3},{8,264},{9... | collective-permute-start | bytes 3145736 | tf_op jit(solution)/shard_map/ppermute | solution.py:376
  77.3 30.9 %copy-start.6 = (bf16[32,8,1024]{2,1,0:T(8,128)(2,1)}, bf16[32,8,1024]{2,1,0:T(8,128)(2,1)S(1)}, u32[]{:S(2)}) copy-start(bf16[32,8,1024]{2,1,0:T(8,128)(2,1)S(1)} %all-to-all-done) | copy-start | bytes 1572868
  77.3 25.9 %all-to-all-start.1 = ((bf16[16,16,1024]{2,1,0:T(8,128)(2,1)}), bf16[16,16,1024]{2,1,0:T(8,128)(2,1)}, u32[]{:S(2)}, u32[]{:S(2)}) async-start(bf16[16,16,1024]{2,1,0:T(8,128)(2,1)} %bitcast.7), calls=%async_computation.1 | async-start | bytes 1048576 | tf_op jit(solution)/shard_map/all_to_all | solution.py:326
  83.3 23.7 %collective-permute-start.7 = (bf16[4,256,512]{2,1,0:T(8,128)(2,1)S(1)}, bf16[4,256,512]{2,1,0:T(8,128)(2,1)}, u32[]{:S(2)}, u32[]{:S(2)}) collective-permute-start(bf16[4,256,512]{2,1,0:T(8,128)(2,1)S(1)} %pad_maximum_fusion.refs_1_.refs_2_.refs_0_), channel_id=1, source_target_pairs={{0,1},{1,0},{2,3},{3,2},{4,5},{5,4},{6,7},{7,6},{8,9},{9,8},{10,11... | collective-permute-start | bytes 3145736 | tf_op jit(solution)/shard_map/ppermute | solution.py:330
  85.3 22.8 %copy-start.5 = (bf16[4,256,512]{2,1,0:T(8,128)(2,1)}, bf16[4,256,512]{2,1,0:T(8,128)(2,1)S(1)}, u32[]{:S(2)}) copy-start(bf16[4,256,512]{2,1,0:T(8,128)(2,1)S(1)} %collective-permute-done.4.refs_2_.refs_3_.refs_1_) | copy-start | bytes 3145732
  85.3 21.6 %collective-permute-start.8 = (bf16[4,256,512]{2,1,0:T(8,128)(2,1)S(1)}, bf16[4,256,512]{2,1,0:T(8,128)(2,1)}, u32[]{:S(2)}, u32[]{:S(2)}) collective-permute-start(bf16[4,256,512]{2,1,0:T(8,128)(2,1)S(1)} %collective-permute-done.4.refs_2_.refs_3_.refs_1_), channel_id=1, source_target_pairs={{0,1},{1,0},{2,3},{3,2},{4,5},{5,4},{6,7},{7,6},{8,9},{9,8},{10,11... | collective-permute-start | bytes 3145736 | tf_op jit(solution)/shard_map/ppermute | solution.py:330
  91.0 15.9 %collective-permute-start.10 = (bf16[4,256,512]{2,1,0:T(8,128)(2,1)}, bf16[4,256,512]{2,1,0:T(8,128)(2,1)}, u32[]{:S(2)}, u32[]{:S(2)}) collective-permute-start(bf16[4,256,512]{2,1,0:T(8,128)(2,1)} %collective-permute-done.6.refs_4_.refs_5_.refs_3_), channel_id=1, source_target_pairs={{0,1},{1,0},{2,3},{3,2},{4,5},{5,4},{6,7},{7,6},{8,9},{9,8},{10,11... | collective-permute-start | bytes 3145736 | tf_op jit(solution)/shard_map/ppermute | solution.py:330
  103.2 4.9 %collective-permute-start.9 = (bf16[4,256,512]{2,1,0:T(8,128)(2,1)}, bf16[4,256,512]{2,1,0:T(8,128)(2,1)}, u32[]{:S(2)}, u32[]{:S(2)}) collective-permute-start(bf16[4,256,512]{2,1,0:T(8,128)(2,1)} %collective-permute-done.5.refs_3_.refs_4_.refs_2_), channel_id=1, source_target_pairs={{0,1},{1,0},{2,3},{3,2},{4,5},{5,4},{6,7},{7,6},{8,9},{9,8},{10,11... | collective-permute-start | bytes 3145736 | tf_op jit(solution)/shard_map/ppermute | solution.py:330
  105.6 0.7 copy-start.17
  119.3 47.1 %all-to-all-start.3 = ((bf16[32,8,1024]{2,1,0:T(8,128)(2,1)}), bf16[32,8,1024]{2,1,0:T(8,128)(2,1)S(1)}, u32[]{:S(2)}, u32[]{:S(2)}) async-start(bf16[32,8,1024]{2,1,0:T(8,128)(2,1)} %bitcast.62), calls=%async_computation.3 | async-start | bytes 1048576 | tf_op jit(solution)/shard_map/all_to_all | solution.py:326
  150.1 15.4 %collective-permute-start.13 = (bf16[64,1024]{1,0:T(8,128)(2,1)S(1)}, bf16[64,1024]{1,0:T(8,128)(2,1)S(1)}, u32[]{:S(2)}, u32[]{:S(2)}) collective-permute-start(bf16[64,1024]{1,0:T(8,128)(2,1)S(1)} %get-tuple-element.27), channel_id=1, source_target_pairs={{0,6},{1,7},{2,0},{3,1},{4,2},{5,3},{6,4},{7,5},{8,14},{9,15},{10,... | collective-permute-start | bytes 393224 | tf_op jit(solution)/shard_map/ppermute | solution.py:396
  154.4 11.1 %collective-permute-start.12 = (bf16[64,1024]{1,0:T(8,128)(2,1)S(1)}, bf16[64,1024]{1,0:T(8,128)(2,1)S(1)}, u32[]{:S(2)}, u32[]{:S(2)}) collective-permute-start(bf16[64,1024]{1,0:T(8,128)(2,1)S(1)} %get-tuple-element.28), channel_id=1, source_target_pairs={{0,4},{1,5},{2,6},{3,7},{4,0},{5,1},{6,2},{7,3},{8,12},{9,13},{10,... | collective-permute-start | bytes 393224 | tf_op jit(solution)/shard_map/ppermute | solution.py:396
  156.3 9.1 %collective-permute-start.11 = (bf16[64,1024]{1,0:T(8,128)(2,1)S(1)}, bf16[64,1024]{1,0:T(8,128)(2,1)S(1)}, u32[]{:S(2)}, u32[]{:S(2)}) collective-permute-start(bf16[64,1024]{1,0:T(8,128)(2,1)S(1)} %get-tuple-element.29), channel_id=1, source_target_pairs={{0,2},{1,3},{2,4},{3,5},{4,6},{5,7},{6,0},{7,1},{8,10},{9,11},{10,... | collective-permute-start | bytes 393224 | tf_op jit(solution)/shard_map/ppermute | solution.py:396
  165.5 0.9 copy-start.12
  165.5 0.9 copy-start.11
  165.5 0.9 copy-start.10
  166.5 13.6 %copy-start.7 = (bf16[32,8,1024]{2,1,0:T(8,128)(2,1)}, bf16[32,8,1024]{2,1,0:T(8,128)(2,1)S(1)}, u32[]{:S(2)}) copy-start(bf16[32,8,1024]{2,1,0:T(8,128)(2,1)S(1)} %all-to-all-done.3) | copy-start | bytes 1572868
  166.5 4.1 %collective-permute-start.14 = (bf16[8,16,1024]{2,1,0:T(8,128)(2,1)S(1)}, bf16[8,16,1024]{2,1,0:T(8,128)(2,1)S(1)}, u32[]{:S(2)}, u32[]{:S(2)}) collective-permute-start(bf16[8,16,1024]{2,1,0:T(8,128)(2,1)S(1)} %get-tuple-element.22), channel_id=1, source_target_pairs={{0,1},{1,0},{2,3},{3,2},{4,5},{5,4},{6,7},{7,6},{8,9},{9,8},{10,11... | collective-permute-start | bytes 786440 | tf_op jit(solution)/shard_map/ppermute | solution.py:330
  170.6 9.4 %copy-start.8 = (bf16[8,16,1024]{2,1,0:T(8,128)(2,1)}, bf16[8,16,1024]{2,1,0:T(8,128)(2,1)S(1)}, u32[]{:S(2)}) copy-start(bf16[8,16,1024]{2,1,0:T(8,128)(2,1)S(1)} %collective-permute-done.14.zc_ref) | copy-start | bytes 786436
  170.6 9.4 %collective-permute-start.15 = (bf16[8,16,1024]{2,1,0:T(8,128)(2,1)S(1)}, bf16[8,16,1024]{2,1,0:T(8,128)(2,1)S(1)}, u32[]{:S(2)}, u32[]{:S(2)}) collective-permute-start(bf16[8,16,1024]{2,1,0:T(8,128)(2,1)S(1)} %slice_dynamic-update-slice_fusion), channel_id=1, source_target_pairs={{0,8},{8,0},{1,9},{9,1},{2,10},{10,2},{3,11},{11,3},{4,12},{12,4},... | collective-permute-start | bytes 786440 | tf_op jit(solution)/shard_map/ppermute | solution.py:330
  180.0 0.7 copy-start.13

commit v4 on v3

--- a/solution.py
+++ b/solution.py
@@ -237,22 +237,9 @@
     )(scalars, *tokens, *weights, *bias_args, *after)
 
 
-def mix_kernel(scalar_ref, tokens_ref, x_ref, y_ref, z0, z1, z2, z3, zy_ref, zc_ref, *refs):
-    own_refs, other_refs, (out_ref, z_ref) = refs[:4], refs[4:8], refs[8:]
-    core, turned_a, turned_b, yl, x = [scalar_ref[8 + n] for n in range(5)]
-    for k, ref in enumerate((z0, z1, z2, z3)):
-        for dy in range(2):
-            for dc in range(2):
-                if dy == 1:
-                    rows = zy_ref[dc * 4 + k]
-                elif dc == 1:
-                    rows = zc_ref[k]
-                else:
-                    rows = ref[:16]
-                source = (yl ^ dy) * 8 + ((x - k + 4) % 4) * 2 + (core ^ dc)
-                z_ref[pl.ds(pl.multiple_of(source * 16, 16), 16), :] = rows
-    summed = x_ref[...].astype(F32) + y_ref[...].astype(F32) + z_ref[...].astype(F32)
-    summed = summed.astype(BF)
+def gather_kernel(scalar_ref, *refs):
+    own_refs, other_refs, out_ref = refs[:4], refs[4:8], refs[-1]
+    core, turned_a, turned_b = [scalar_ref[8 + n] for n in range(3)]
     for slot in range(PAIRS):
         group, k = slot // 4, slot % 4
         halves = []
@@ -263,32 +250,57 @@
         turned = turned_b if group else turned_a
         low = jnp.where(turned == 0, halves[0], halves[1])
         high = jnp.where(turned == 0, halves[1], halves[0])
-        weights = jnp.concatenate([low, high], axis=0)
         columns = pl.ds(pl.multiple_of(scalar_ref[slot] * BLOCK, BLOCK), BLOCK)
-        result = jnp.dot(summed, weights, preferred_element_type=F32)
-        out_ref[:, columns] = (tokens_ref[:, columns].astype(F32) + result).astype(BF)
-
-
-def mix(scalars, tokens, along_x, along_y, along_z, weights):
-    whole_block = [
-        pl.BlockSpec(a.shape, lambda i, p, n=a.ndim: (0,) * n)
-        for a in (tokens, along_x, along_y, *along_z)
-    ]
+        out_ref[:, columns] = jnp.concatenate([low, high], axis=0)
+
+
+def gather_out(scalars, weights, after):
     half = weights[0].shape[1]
-    out_block = [pl.BlockSpec((4, half, BLOCK), lambda i, p: (0, 0, 3))] * 8
+    size = HEADS * HEAD
+    specs = [pl.BlockSpec((4, half, BLOCK), lambda i, p: (0, 0, 3))] * 8
+    specs.append(pl.BlockSpec(memory_space=pl.ANY))
     return pl.pallas_call(
-        mix_kernel,
-        out_shape=jax.ShapeDtypeStruct(tokens.shape, BF),
+        gather_kernel,
+        out_shape=jax.ShapeDtypeStruct((size, size), BF),
         grid_spec=pltpu.PrefetchScalarGridSpec(
             num_scalar_prefetch=1,
             grid=(1,),
-            in_specs=whole_block + out_block,
-            out_specs=pl.BlockSpec(tokens.shape, lambda i, p: (0, 0)),
-            scratch_shapes=[pltpu.VMEM(tokens.shape, BF)],
+            in_specs=specs,
+            out_specs=pl.BlockSpec((size, size), lambda i, p: (0, 0)),
         ),
-        compiler_params=pltpu.CompilerParams(vmem_limit_bytes=61 * 2**20),
-        name="mix",
-    )(scalars, tokens, along_x, along_y, *along_z, *weights)
+        compiler_params=pltpu.CompilerParams(vmem_limit_bytes=24 * 2**20),
+        name="gather_out",
+    )(scalars, *weights, after)
+
+
+def mix_kernel(distance, scalar_ref, tokens_ref, x_ref, y_ref, parts_ref, w_ref, *refs):
+    out_ref, z_ref = refs[-2:]
+    core, yl, x = scalar_ref[8], scalar_ref[11], scalar_ref[12]
+    half = z_ref.shape[0]
+    for k in range(4):
+        for dc in range(2):
+            source = ((x - k + 4) & 3) * 2 + (core ^ dc)
+            z_ref[pl.ds(pl.multiple_of(source * 16, 16), 16), :] = parts_ref[dc * 4 + k]
+    mine = pl.ds(pl.multiple_of((yl ^ distance) * half, half), half)
+    summed = x_ref[mine, :].astype(F32) + y_ref[mine, :].astype(F32) + z_ref[...].astype(F32)
+    result = jnp.dot(summed.astype(BF), w_ref[...], preferred_element_type=F32)
+    result = (tokens_ref[mine, :].astype(F32) + result).astype(BF)
+    if distance == 0:
+        out_ref[...] = result
+    else:
+        out_ref[mine, :] = result
+        out_ref[pl.ds(pl.multiple_of(yl * half, half), half), :] = refs[0][...]
+
+
+def mix(distance, shape, scalars, *args):
+    half = (args[0].shape[0] // 2, args[0].shape[1])
+    return whole(
+        functools.partial(mix_kernel, distance),
+        jax.ShapeDtypeStruct(shape, BF),
+        f"mix_{distance}",
+        1,
+        [pltpu.VMEM(half, BF)],
+    )(scalars, *args)
 
 
 def whole(kernel, out, name, scalars=0, scratch=()):
@@ -387,18 +399,20 @@
     ).astype(jnp.int32)
 
     every = (*second, *others)
-    (along_y,) = attend((2,), (y_lines,), every, (blocks_y,), scalars)
-    z, along_x = attend((3, 1), (z_lines, normed), every, (blocks_z, blocks_x), scalars, (along_y,))
-    along_y = exchange(together(along_y, z_lines).reshape(peers, -1, features), GY)
-    along_y = along_y.reshape(rows, features)
+    along_y, z = attend((2, 3), (y_lines, z_lines), every, (blocks_y, blocks_z), scalars)
+    along_y = exchange(along_y.reshape(peers, -1, features), GY).reshape(rows, features)
 
     z = z.reshape(4, rows // 4, features)
     back = [z[0]] + [lax.ppermute(z[k], ALL, hop_x(k)) for k in range(1, 4)]
+    (along_x,) = attend((1,), (normed,), every, (blocks_x,), scalars)
+    w_whole = gather_out(scalars, every, along_x)
     back_c = jnp.stack([b[r : r + 16] for r in (16, 48) for b in back])
-    back_c = swap(together(back_c, along_y), "c")
+    back_c = swap(together(back_c, (along_y, w_whole)), "c")
     back_y = jnp.concatenate([jnp.stack([b[32:48] for b in back]), back_c[4:]], axis=0)
     back_y = swap(back_y, "yl")
-    mixed = mix(scalars, flat, along_x, along_y, (*back, back_y, back_c), every)
+    near_z = jnp.concatenate([jnp.stack([b[:16] for b in back]), back_c[:4]], axis=0)
+    mixed = mix(0, (rows // 2, features), scalars, flat, along_x, along_y, near_z, w_whole)
+    mixed = mix(1, flat.shape, scalars, flat, along_x, along_y, back_y, w_whole, mixed)
     return mixed.reshape(shape)
 
 

time: 190 us -> 188 us (0.989)
  waiting for transfers between devices: 44.5 us -> 38.8 us
    ppermute x3, waiting for transfers between devices: 5.87 us -> 0.01 us  [shards(): back = [z[0]] + [lax.ppermute(z[k], ALL, hop_x(k)) for k in range(1, 4)]]
    all_to_all x4, waiting for transfers between devices: 10.1 us -> 13.3 us  [exchange(): return lax.all_to_all(array, axes, split_axis=0, concat_axis=0, tiled=True)]
    pallas_call x4 -> x6, Pallas kernels: 2.13 us -> 5.2 us  [call(): pl.pallas_call(kernel, out_shape=out, in_specs=[smem] * scalars + [vmem]...]
    ppermute x7, waiting for transfers between devices: 10.8 us -> 7.82 us  [swap(): return lax.ppermute(array, axis, [(0, 1), (1, 0)])]
    pallas_call x1, Pallas kernels: 5.34 us -> 2.69 us  [gather_out(): pl.pallas_call(gather_kernel, out_shape=jax.ShapeDtypeStruct((size, size)...]
    unnamed x43 -> x42, local copies, waits for them, and re-layouts: 7.23 us -> 8.89 us
where the time goes in v4:
time: 188 us; the launch traced here: 185 us
  starting transfers between devices  95.7 us (51%)
  waiting for transfers between devices  38.8 us (21%)
  Pallas kernels  33.9 us (18%)
  local copies, waits for them, and re-layouts  16 us (9%)
    all_to_all x4, starting transfers between devices, exchange(): return lax.all_to_all(array, axes, split_axis=0, concat_axis=0, tiled=True)  49.6 us
    pallas_call x2, Pallas kernels, attend(): pl.pallas_call(functools.partial(attend_kernel, axes), out_shape=[jax.Sha...  26 us
    ppermute x7, starting transfers between devices, swap(): return lax.ppermute(array, axis, [(0, 1), (1, 0)])  16.4 us
    all_to_all x4, waiting for transfers between devices, exchange(): return lax.all_to_all(array, axes, split_axis=0, concat_axis=0, tiled=True)  13.3 us
    ppermute x3, starting transfers between devices, shards(): lax.ppermute(piece, ALL, hop_plane(k, 0))  10.2 us
    ppermute x3, starting transfers between devices, shards(): lax.ppermute(first, ALL, hop_plane(k, 1))  9.94 us
    ppermute x3, waiting for transfers between devices, shards(): lax.ppermute(first, ALL, hop_plane(k, 1))  9.92 us
    ppermute x3, starting transfers between devices, shards(): back = [z[0]] + [lax.ppermute(z[k], ALL, hop_x(k)) for k in range(1, 4)]  9.57 us
  transfers between devices with their start and end apart: 20, of which 11 were waited for; matrix products, arithmetic and copies ran while one was open for 3% of the time, Pallas kernels for 9%

profile of v4, /device:TPU:1, one launch (start us, length us, event | category | flops | bytes accessed | tf_op | source)
XLA Modules:
  0.0 185.1 jit_solution(12663894621943069564)
XLA Ops:
  0.0 0.7 dynamic_slice.15
  0.7 0.7 fusion.2
  1.4 0.7 broadcast_in_dim.2
  2.2 15.7 %all-to-all-start = ((bf16[16,16,512]{2,1,0:T(8,128)(2,1)}), bf16[16,16,512]{2,1,0:T(8,128)(2,1)S(1)}, u32[]{:S(2)}, u32[]{:S(2)}) async-start(bf16[16,16,512]{2,1,0:T(8,128)(2,1)} %broadcast_in_dim.2), calls=%async_computation | async-start | bytes 524288 | tf_op jit(solution)/shard_map/all_to_all | solution.py:338
  17.9 0.0 copy-start.15
  17.9 1.2 reshape.42.tokens_ref
  19.2 0.0 copy-start.9
  19.2 1.1 norm.1.refs_0_
  20.3 0.1 rev.9
  20.4 0.3 bias_64.1.refs_9_.refs_10_
  20.8 1.0 copy-done.2
  21.8 0.1 rev.10
  21.8 0.3 bias_32.2.refs_10_.refs_11_
  22.2 1.0 copy-done.5
  23.2 0.1 rev.11
  23.2 0.3 bias_32.3.refs_12_.refs_13_
  23.6 1.0 copy-done.6
  24.6 6.5 %all-to-all-done = bf16[16,16,512]{2,1,0:T(8,128)(2,1)S(1)} async-done(((bf16[16,16,512]{2,1,0:T(8,128)(2,1)}), bf16[16,16,512]{2,1,0:T(8,128)(2,1)S(1)}, u32[]{:S(2)}, u32[]{:S(2)}) %all-to-all-start) | async-done | bytes 262176 | tf_op jit(solution)/shard_map/all_to_all | solution.py:338
  31.1 13.9 %all-to-all-start.1 = ((bf16[32,8,1024]{2,1,0:T(8,128)(2,1)}), bf16[32,8,1024]{2,1,0:T(8,128)(2,1)S(1)}, u32[]{:S(2)}, u32[]{:S(2)}) async-start(bf16[32,8,1024]{2,1,0:T(8,128)(2,1)} %bitcast.13), calls=%async_computation.1 | async-start | bytes 1048576 | tf_op jit(solution)/shard_map/all_to_all | solution.py:338
  45.0 0.0 copy-start.16
  45.0 2.9 %collective-permute-start = (bf16[128,512]{1,0:T(8,128)(2,1)S(1)}, bf16[128,512]{1,0:T(8,128)(2,1)S(1)}, u32[]{:S(2)}, u32[]{:S(2)}) collective-permute-start(bf16[128,512]{1,0:T(8,128)(2,1)S(1)} %broadcast_select_fusion.2), channel_id=1, source_target_pairs={{0,1},{1,0},{2,3},{3,2},{4,5},{5,4},{6,7},{7,6},{8,9},{9,8},{10,11... | collective-permute-start | bytes 393224 | tf_op jit(solution)/shard_map/ppermute | solution.py:342
  47.9 1.0 collective-permute-done
  48.9 4.8 %collective-permute-start.3 = (bf16[256,512]{1,0:T(8,128)(2,1)S(1)}, bf16[256,512]{1,0:T(8,128)(2,1)S(1)}, u32[]{:S(2)}, u32[]{:S(2)}) collective-permute-start(bf16[256,512]{1,0:T(8,128)(2,1)S(1)} %bitcast.79), channel_id=1, source_target_pairs={{0,6},{1,265},{2,0},{3,267},{4,2},{5,269},{6,4},{7,271},{8,14},{9,... | collective-permute-start | bytes 786440 | tf_op jit(solution)/shard_map/ppermute | solution.py:386
  53.7 1.9 %collective-permute-start.2 = (bf16[256,512]{1,0:T(8,128)(2,1)S(1)}, bf16[256,512]{1,0:T(8,128)(2,1)S(1)}, u32[]{:S(2)}, u32[]{:S(2)}) collective-permute-start(bf16[256,512]{1,0:T(8,128)(2,1)S(1)} %bitcast.80), channel_id=1, source_target_pairs={{0,2},{1,9},{2,4},{3,11},{4,6},{5,13},{6,0},{7,15},{8,10},{9,257},... | collective-permute-start | bytes 786440 | tf_op jit(solution)/shard_map/ppermute | solution.py:386
  55.6 3.5 %collective-permute-start.1 = (bf16[256,512]{1,0:T(8,128)(2,1)S(1)}, bf16[256,512]{1,0:T(8,128)(2,1)S(1)}, u32[]{:S(2)}, u32[]{:S(2)}) collective-permute-start(bf16[256,512]{1,0:T(8,128)(2,1)S(1)} %bitcast.81), channel_id=1, source_target_pairs={{0,4},{1,257},{2,6},{3,259},{4,0},{5,261},{6,2},{7,263},{8,12},{9,... | collective-permute-start | bytes 786440 | tf_op jit(solution)/shard_map/ppermute | solution.py:386
  59.2 0.0 collective-permute-done.3
  59.2 7.8 %collective-permute-done.2 = bf16[256,512]{1,0:T(8,128)(2,1)S(1)} collective-permute-done((bf16[256,512]{1,0:T(8,128)(2,1)S(1)}, bf16[256,512]{1,0:T(8,128)(2,1)S(1)}, u32[]{:S(2)}, u32[]{:S(2)}) %collective-permute-start.2) | collective-permute-done | bytes 262176 | tf_op jit(solution)/shard_map/ppermute | solution.py:386
  66.9 0.1 pad_maximum_fusion.refs_1_.refs_2_.refs_0_
  67.1 3.1 %collective-permute-start.4 = (bf16[4,256,512]{2,1,0:T(8,128)(2,1)S(1)}, bf16[4,256,512]{2,1,0:T(8,128)(2,1)S(1)}, u32[]{:S(2)}, u32[]{:S(2)}) collective-permute-start(bf16[4,256,512]{2,1,0:T(8,128)(2,1)S(1)} %pad_maximum_fusion.refs_1_.refs_2_.refs_0_), channel_id=1, source_target_pairs={{0,8},{1,3},{2,10},{3,5},{4,12},{5,7},{6,14},{7,1},{8,256},{9,11},... | collective-permute-start | bytes 3145736 | tf_op jit(solution)/shard_map/ppermute | solution.py:388
  70.2 3.4 %collective-permute-start.6 = (bf16[4,256,512]{2,1,0:T(8,128)(2,1)S(1)}, bf16[4,256,512]{2,1,0:T(8,128)(2,1)}, u32[]{:S(2)}, u32[]{:S(2)}) collective-permute-start(bf16[4,256,512]{2,1,0:T(8,128)(2,1)S(1)} %pad_maximum_fusion.refs_1_.refs_2_.refs_0_), channel_id=1, source_target_pairs={{0,264},{1,7},{2,266},{3,1},{4,268},{5,3},{6,270},{7,5},{8,0},{9,1... | collective-permute-start | bytes 3145736 | tf_op jit(solution)/shard_map/ppermute | solution.py:388
  73.6 3.4 %collective-permute-start.5 = (bf16[4,256,512]{2,1,0:T(8,128)(2,1)S(1)}, bf16[4,256,512]{2,1,0:T(8,128)(2,1)}, u32[]{:S(2)}, u32[]{:S(2)}) collective-permute-start(bf16[4,256,512]{2,1,0:T(8,128)(2,1)S(1)} %pad_maximum_fusion.refs_1_.refs_2_.refs_0_), channel_id=1, source_target_pairs={{0,256},{1,5},{2,258},{3,7},{4,260},{5,1},{6,262},{7,3},{8,264},{9... | collective-permute-start | bytes 3145736 | tf_op jit(solution)/shard_map/ppermute | solution.py:388
  77.0 0.1 all-to-all-done.1
  77.1 6.0 %all-to-all-start.2 = ((bf16[16,16,1024]{2,1,0:T(8,128)(2,1)}), bf16[16,16,1024]{2,1,0:T(8,128)(2,1)}, u32[]{:S(2)}, u32[]{:S(2)}) async-start(bf16[16,16,1024]{2,1,0:T(8,128)(2,1)} %bitcast.15), calls=%async_computation.2 | async-start | bytes 1048576 | tf_op jit(solution)/shard_map/all_to_all | solution.py:338
  83.1 2.1 %collective-permute-start.7 = (bf16[4,256,512]{2,1,0:T(8,128)(2,1)S(1)}, bf16[4,256,512]{2,1,0:T(8,128)(2,1)}, u32[]{:S(2)}, u32[]{:S(2)}) collective-permute-start(bf16[4,256,512]{2,1,0:T(8,128)(2,1)S(1)} %pad_maximum_fusion.refs_1_.refs_2_.refs_0_), channel_id=1, source_target_pairs={{0,1},{1,0},{2,3},{3,2},{4,5},{5,4},{6,7},{7,6},{8,9},{9,8},{10,11... | collective-permute-start | bytes 3145736 | tf_op jit(solution)/shard_map/ppermute | solution.py:342
  85.2 2.3 %collective-permute-start.8 = (bf16[4,256,512]{2,1,0:T(8,128)(2,1)S(1)}, bf16[4,256,512]{2,1,0:T(8,128)(2,1)}, u32[]{:S(2)}, u32[]{:S(2)}) collective-permute-start(bf16[4,256,512]{2,1,0:T(8,128)(2,1)S(1)} %collective-permute-done.4.refs_2_.refs_3_.refs_1_), channel_id=1, source_target_pairs={{0,1},{1,0},{2,3},{3,2},{4,5},{5,4},{6,7},{7,6},{8,9},{9,8},{10,11... | collective-permute-start | bytes 3145736 | tf_op jit(solution)/shard_map/ppermute | solution.py:342
  87.4 3.4 %collective-permute-done.6.refs_4_.refs_5_.refs_3_ = bf16[4,256,512]{2,1,0:T(8,128)(2,1)} collective-permute-done((bf16[4,256,512]{2,1,0:T(8,128)(2,1)S(1)}, bf16[4,256,512]{2,1,0:T(8,128)(2,1)}, u32[]{:S(2)}, u32[]{:S(2)}) %collective-permute-start.6) | collective-permute-done | bytes 1048608 | tf_op jit(solution)/shard_map/ppermute | solution.py:388
  90.9 1.9 %collective-permute-start.10 = (bf16[4,256,512]{2,1,0:T(8,128)(2,1)}, bf16[4,256,512]{2,1,0:T(8,128)(2,1)}, u32[]{:S(2)}, u32[]{:S(2)}) collective-permute-start(bf16[4,256,512]{2,1,0:T(8,128)(2,1)} %collective-permute-done.6.refs_4_.refs_5_.refs_3_), channel_id=1, source_target_pairs={{0,1},{1,0},{2,3},{3,2},{4,5},{5,4},{6,7},{7,6},{8,9},{9,8},{10,11... | collective-permute-start | bytes 3145736 | tf_op jit(solution)/shard_map/ppermute | solution.py:342
  92.8 6.5 %collective-permute-done.5.refs_3_.refs_4_.refs_2_ = bf16[4,256,512]{2,1,0:T(8,128)(2,1)} collective-permute-done((bf16[4,256,512]{2,1,0:T(8,128)(2,1)S(1)}, bf16[4,256,512]{2,1,0:T(8,128)(2,1)}, u32[]{:S(2)}, u32[]{:S(2)}) %collective-permute-start.5) | collective-permute-done | bytes 1048608 | tf_op jit(solution)/shard_map/ppermute | solution.py:388
  99.3 3.8 %all-to-all-done.2 = bf16[16,16,1024]{2,1,0:T(8,128)(2,1)} async-done(((bf16[16,16,1024]{2,1,0:T(8,128)(2,1)}), bf16[16,16,1024]{2,1,0:T(8,128)(2,1)}, u32[]{:S(2)}, u32[]{:S(2)}) %all-to-all-start.2) | async-done | bytes 524320 | tf_op jit(solution)/shard_map/all_to_all | solution.py:338
  103.1 2.3 %collective-permute-start.9 = (bf16[4,256,512]{2,1,0:T(8,128)(2,1)}, bf16[4,256,512]{2,1,0:T(8,128)(2,1)}, u32[]{:S(2)}, u32[]{:S(2)}) collective-permute-start(bf16[4,256,512]{2,1,0:T(8,128)(2,1)} %collective-permute-done.5.refs_3_.refs_4_.refs_2_), channel_id=1, source_target_pairs={{0,1},{1,0},{2,3},{3,2},{4,5},{5,4},{6,7},{7,6},{8,9},{9,8},{10,11... | collective-permute-start | bytes 3145736 | tf_op jit(solution)/shard_map/ppermute | solution.py:342
  105.4 0.7 concatenate.12.scalar_ref
  106.1 1.8 collective-permute-done.9.refs_7_.refs_8_.refs_6_
  108.0 14.8 %attend_2_3.1 = (bf16[256,1024]{1,0:T(8,128)(2,1)}, bf16[256,1024]{1,0:T(8,128)(2,1)}) custom-call(s32[13]{0:T(128)} %concatenate.12.scalar_ref, bf16[256,1024]{1,0:T(8,128)(2,1)} %bitcast.78, bf16[256,1024]{1,0:T(8,128)(2,1)} %bitcast.16.refs_1_, bf16[4,256,512]{2,1,0:T(8,128)(2,1)} %copy-done, bf16[4,256,512]{2,1,0:T(8,128)(2,1)} %copy-done.3, ...), custom_call_target="tpu_custom_call" | custom-call | flops 1000 | bytes 1000 | tf_op jit(solution)/shard_map/attend_2_3/pallas_call | solution.py:219
  122.8 14.0 %all-to-all-start.3 = ((bf16[32,8,1024]{2,1,0:T(8,128)(2,1)}), bf16[32,8,1024]{2,1,0:T(8,128)(2,1)}, u32[]{:S(2)}, u32[]{:S(2)}) async-start(bf16[32,8,1024]{2,1,0:T(8,128)(2,1)} %bitcast.83), calls=%async_computation.3 | async-start | bytes 1048576 | tf_op jit(solution)/shard_map/all_to_all | solution.py:338
  136.8 1.8 fusion.1
  138.6 2.2 %collective-permute-start.11 = (bf16[64,1024]{1,0:T(8,128)(2,1)}, bf16[64,1024]{1,0:T(8,128)(2,1)S(1)}, u32[]{:S(2)}, u32[]{:S(2)}) collective-permute-start(bf16[64,1024]{1,0:T(8,128)(2,1)} %get-tuple-element.28), channel_id=1, source_target_pairs={{0,2},{1,3},{2,4},{3,5},{4,6},{5,7},{6,0},{7,1},{8,10},{9,11},{10,... | collective-permute-start | bytes 393224 | tf_op jit(solution)/shard_map/ppermute | solution.py:406
  140.8 5.1 %collective-permute-start.12 = (bf16[64,1024]{1,0:T(8,128)(2,1)}, bf16[64,1024]{1,0:T(8,128)(2,1)S(1)}, u32[]{:S(2)}, u32[]{:S(2)}) collective-permute-start(bf16[64,1024]{1,0:T(8,128)(2,1)} %get-tuple-element.27), channel_id=1, source_target_pairs={{0,4},{1,5},{2,6},{3,7},{4,0},{5,1},{6,2},{7,3},{8,12},{9,13},{10,... | collective-permute-start | bytes 393224 | tf_op jit(solution)/shard_map/ppermute | solution.py:406
  146.0 2.2 %collective-permute-start.13 = (bf16[64,1024]{1,0:T(8,128)(2,1)}, bf16[64,1024]{1,0:T(8,128)(2,1)S(1)}, u32[]{:S(2)}, u32[]{:S(2)}) collective-permute-start(bf16[64,1024]{1,0:T(8,128)(2,1)} %get-tuple-element.26), channel_id=1, source_target_pairs={{0,6},{1,7},{2,0},{3,1},{4,2},{5,3},{6,4},{7,5},{8,14},{9,15},{10,... | collective-permute-start | bytes 393224 | tf_op jit(solution)/shard_map/ppermute | solution.py:406
  148.2 11.2 %attend_1.1.refs_8_.x_ref = bf16[256,1024]{1,0:T(8,128)(2,1)} custom-call(s32[13]{0:T(128)} %concatenate.12.scalar_ref, bf16[256,1024]{1,0:T(8,128)(2,1)} %norm.1.refs_0_, bf16[4,256,512]{2,1,0:T(8,128)(2,1)} %copy-done, bf16[4,256,512]{2,1,0:T(8,128)(2,1)} %copy-done.3, bf16[4,256,512]{2,1,0:T(8,128)(2,1)} %collective-permute-done.5.refs_3_.refs_4_.refs_2_, ...), custom_call_target="tpu_custom_call" | custom-call | flops 1000 | bytes 1000 | tf_op jit(solution)/shard_map/attend_1/pallas_call | solution.py:219
  159.4 1.2 copy-done.4
  160.6 1.0 copy-done.7
  161.7 2.7 %gather_out.1.w_ref = bf16[1024,1024]{1,0:T(8,128)(2,1)S(1)} custom-call(s32[13]{0:T(128)S(1)} %copy-done.11, bf16[4,256,512]{2,1,0:T(8,128)(2,1)S(1)} %copy-done.1, bf16[4,256,512]{2,1,0:T(8,128)(2,1)S(1)} %copy-done.4, bf16[4,256,512]{2,1,0:T(8,128)(2,1)} %collective-permute-done.5.refs_3_.refs_4_.refs_2_, ...), custom_call_target="tpu_custom_call" | custom-call | tf_op jit(solution)/shard_map/gather_out/pallas_call | solution.py:262
  164.4 0.8 constant_dynamic-update-slice_fusion.7
  165.2 0.8 constant_dynamic-update-slice_fusion.15
  166.0 2.9 %all-to-all-done.3 = bf16[32,8,1024]{2,1,0:T(8,128)(2,1)} async-done(((bf16[32,8,1024]{2,1,0:T(8,128)(2,1)}), bf16[32,8,1024]{2,1,0:T(8,128)(2,1)}, u32[]{:S(2)}, u32[]{:S(2)}) %all-to-all-start.3) | async-done | bytes 524320 | tf_op jit(solution)/shard_map/all_to_all | solution.py:338
  169.0 3.0 %collective-permute-start.14 = (bf16[8,16,1024]{2,1,0:T(8,128)(2,1)S(1)}, bf16[8,16,1024]{2,1,0:T(8,128)(2,1)S(1)}, u32[]{:S(2)}, u32[]{:S(2)}) collective-permute-start(bf16[8,16,1024]{2,1,0:T(8,128)(2,1)S(1)} %get-tuple-element.20), channel_id=1, source_target_pairs={{0,1},{1,0},{2,3},{3,2},{4,5},{5,4},{6,7},{7,6},{8,9},{9,8},{10,11... | collective-permute-start | bytes 786440 | tf_op jit(solution)/shard_map/ppermute | solution.py:342
  172.0 1.1 collective-permute-done.14
  173.2 1.9 %collective-permute-start.15 = (bf16[8,16,1024]{2,1,0:T(8,128)(2,1)S(1)}, bf16[8,16,1024]{2,1,0:T(8,128)(2,1)S(1)}, u32[]{:S(2)}, u32[]{:S(2)}) collective-permute-start(bf16[8,16,1024]{2,1,0:T(8,128)(2,1)S(1)} %get-tuple-element.32), channel_id=1, source_target_pairs={{0,8},{8,0},{1,9},{9,1},{2,10},{10,2},{3,11},{11,3},{4,12},{12,4},... | collective-permute-start | bytes 786440 | tf_op jit(solution)/shard_map/ppermute | solution.py:342
  175.1 1.0 copy-done.8
  176.2 1.0 copy-done.10
  177.2 1.5 mix_0.1.refs_0_
  178.7 3.9 %collective-permute-done.15.parts_ref = bf16[8,16,1024]{2,1,0:T(8,128)(2,1)S(1)} collective-permute-done((bf16[8,16,1024]{2,1,0:T(8,128)(2,1)S(1)}, bf16[8,16,1024]{2,1,0:T(8,128)(2,1)S(1)}, u32[]{:S(2)}, u32[]{:S(2)}) %collective-permute-start.15) | collective-permute-done | bytes 262176 | tf_op jit(solution)/shard_map/ppermute | solution.py:342
  182.6 1.5 mix_1.1
  184.1 1.0 reshape.51
  (48 shorter events, 0.2 us)
Async XLA Ops:
  0.0 20.3 %copy-start.13 = (f32[16,127]{1,0:T(8,128)S(1)}, f32[16,127]{1,0:T(8,128)}, u32[]{:S(2)}) copy-start(f32[16,127]{1,0:T(8,128)} %param.10) | copy-start | bytes 24388
  0.0 21.8 %copy-start.14 = (f32[16,63]{1,0:T(8,128)S(1)}, f32[16,63]{1,0:T(8,128)}, u32[]{:S(2)}) copy-start(f32[16,63]{1,0:T(8,128)} %param.11) | copy-start | bytes 12100
  2.2 28.9 %all-to-all-start = ((bf16[16,16,512]{2,1,0:T(8,128)(2,1)}), bf16[16,16,512]{2,1,0:T(8,128)(2,1)S(1)}, u32[]{:S(2)}, u32[]{:S(2)}) async-start(bf16[16,16,512]{2,1,0:T(8,128)(2,1)} %broadcast_in_dim.2), calls=%async_computation | async-start | bytes 524288 | tf_op jit(solution)/shard_map/all_to_all | solution.py:338
  17.9 5.2 %copy-start.15 = (f32[16,63]{1,0:T(8,128)S(1)}, f32[16,63]{1,0:T(8,128)}, u32[]{:S(2)}) copy-start(f32[16,63]{1,0:T(8,128)} %param.12) | copy-start | bytes 12100
  19.2 4.4 %copy-start.9 = (bf16[256,1024]{1,0:T(8,128)(2,1)}, bf16[256,1024]{1,0:T(8,128)(2,1)S(1)}, u32[]{:S(2)}) copy-start(bf16[256,1024]{1,0:T(8,128)(2,1)S(1)} %reshape.42.tokens_ref) | copy-start | bytes 1572868
  20.8 1.0 copy-start.2
  22.2 1.0 copy-start.5
  23.6 1.0 copy-start.6
  31.1 46.0 %all-to-all-start.1 = ((bf16[32,8,1024]{2,1,0:T(8,128)(2,1)}), bf16[32,8,1024]{2,1,0:T(8,128)(2,1)S(1)}, u32[]{:S(2)}, u32[]{:S(2)}) async-start(bf16[32,8,1024]{2,1,0:T(8,128)(2,1)} %bitcast.13), calls=%async_computation.1 | async-start | bytes 1048576 | tf_op jit(solution)/shard_map/all_to_all | solution.py:338
  45.0 60.4 %copy-start.16 = (s32[4]{0:T(128)S(1)}, s32[4]{0:T(128)}, u32[]{:S(2)}) copy-start(s32[4]{0:T(128)} %constant.81) | copy-start | bytes 52
  45.0 3.9 %collective-permute-start = (bf16[128,512]{1,0:T(8,128)(2,1)S(1)}, bf16[128,512]{1,0:T(8,128)(2,1)S(1)}, u32[]{:S(2)}, u32[]{:S(2)}) collective-permute-start(bf16[128,512]{1,0:T(8,128)(2,1)S(1)} %broadcast_select_fusion.2), channel_id=1, source_target_pairs={{0,1},{1,0},{2,3},{3,2},{4,5},{5,4},{6,7},{7,6},{8,9},{9,8},{10,11... | collective-permute-start | bytes 393224 | tf_op jit(solution)/shard_map/ppermute | solution.py:342
  48.9 10.2 %collective-permute-start.3 = (bf16[256,512]{1,0:T(8,128)(2,1)S(1)}, bf16[256,512]{1,0:T(8,128)(2,1)S(1)}, u32[]{:S(2)}, u32[]{:S(2)}) collective-permute-start(bf16[256,512]{1,0:T(8,128)(2,1)S(1)} %bitcast.79), channel_id=1, source_target_pairs={{0,6},{1,265},{2,0},{3,267},{4,2},{5,269},{6,4},{7,271},{8,14},{9,... | collective-permute-start | bytes 786440 | tf_op jit(solution)/shard_map/ppermute | solution.py:386
  53.7 13.2 %collective-permute-start.2 = (bf16[256,512]{1,0:T(8,128)(2,1)S(1)}, bf16[256,512]{1,0:T(8,128)(2,1)S(1)}, u32[]{:S(2)}, u32[]{:S(2)}) collective-permute-start(bf16[256,512]{1,0:T(8,128)(2,1)S(1)} %bitcast.80), channel_id=1, source_target_pairs={{0,2},{1,9},{2,4},{3,11},{4,6},{5,13},{6,0},{7,15},{8,10},{9,257},... | collective-permute-start | bytes 786440 | tf_op jit(solution)/shard_map/ppermute | solution.py:386
  55.6 11.3 %collective-permute-start.1 = (bf16[256,512]{1,0:T(8,128)(2,1)S(1)}, bf16[256,512]{1,0:T(8,128)(2,1)S(1)}, u32[]{:S(2)}, u32[]{:S(2)}) collective-permute-start(bf16[256,512]{1,0:T(8,128)(2,1)S(1)} %bitcast.81), channel_id=1, source_target_pairs={{0,4},{1,257},{2,6},{3,259},{4,0},{5,261},{6,2},{7,263},{8,12},{9,... | collective-permute-start | bytes 786440 | tf_op jit(solution)/shard_map/ppermute | solution.py:386
  67.1 40.9 %copy-start = (bf16[4,256,512]{2,1,0:T(8,128)(2,1)}, bf16[4,256,512]{2,1,0:T(8,128)(2,1)S(1)}, u32[]{:S(2)}) copy-start(bf16[4,256,512]{2,1,0:T(8,128)(2,1)S(1)} %pad_maximum_fusion.refs_1_.refs_2_.refs_0_) | copy-start | bytes 3145732
  67.1 18.1 %collective-permute-start.4 = (bf16[4,256,512]{2,1,0:T(8,128)(2,1)S(1)}, bf16[4,256,512]{2,1,0:T(8,128)(2,1)S(1)}, u32[]{:S(2)}, u32[]{:S(2)}) collective-permute-start(bf16[4,256,512]{2,1,0:T(8,128)(2,1)S(1)} %pad_maximum_fusion.refs_1_.refs_2_.refs_0_), channel_id=1, source_target_pairs={{0,8},{1,3},{2,10},{3,5},{4,12},{5,7},{6,14},{7,1},{8,256},{9,11},... | collective-permute-start | bytes 3145736 | tf_op jit(solution)/shard_map/ppermute | solution.py:388
  70.2 20.6 %collective-permute-start.6 = (bf16[4,256,512]{2,1,0:T(8,128)(2,1)S(1)}, bf16[4,256,512]{2,1,0:T(8,128)(2,1)}, u32[]{:S(2)}, u32[]{:S(2)}) collective-permute-start(bf16[4,256,512]{2,1,0:T(8,128)(2,1)S(1)} %pad_maximum_fusion.refs_1_.refs_2_.refs_0_), channel_id=1, source_target_pairs={{0,264},{1,7},{2,266},{3,1},{4,268},{5,3},{6,270},{7,5},{8,0},{9,1... | collective-permute-start | bytes 3145736 | tf_op jit(solution)/shard_map/ppermute | solution.py:388
  73.6 25.7 %collective-permute-start.5 = (bf16[4,256,512]{2,1,0:T(8,128)(2,1)S(1)}, bf16[4,256,512]{2,1,0:T(8,128)(2,1)}, u32[]{:S(2)}, u32[]{:S(2)}) collective-permute-start(bf16[4,256,512]{2,1,0:T(8,128)(2,1)S(1)} %pad_maximum_fusion.refs_1_.refs_2_.refs_0_), channel_id=1, source_target_pairs={{0,256},{1,5},{2,258},{3,7},{4,260},{5,1},{6,262},{7,3},{8,264},{9... | collective-permute-start | bytes 3145736 | tf_op jit(solution)/shard_map/ppermute | solution.py:388
  77.1 30.9 %copy-start.12 = (bf16[32,8,1024]{2,1,0:T(8,128)(2,1)}, bf16[32,8,1024]{2,1,0:T(8,128)(2,1)S(1)}, u32[]{:S(2)}) copy-start(bf16[32,8,1024]{2,1,0:T(8,128)(2,1)S(1)} %all-to-all-done.1) | copy-start | bytes 1572868
  77.1 26.0 %all-to-all-start.2 = ((bf16[16,16,1024]{2,1,0:T(8,128)(2,1)}), bf16[16,16,1024]{2,1,0:T(8,128)(2,1)}, u32[]{:S(2)}, u32[]{:S(2)}) async-start(bf16[16,16,1024]{2,1,0:T(8,128)(2,1)} %bitcast.15), calls=%async_computation.2 | async-start | bytes 1048576 | tf_op jit(solution)/shard_map/all_to_all | solution.py:338
  83.1 23.0 %collective-permute-start.7 = (bf16[4,256,512]{2,1,0:T(8,128)(2,1)S(1)}, bf16[4,256,512]{2,1,0:T(8,128)(2,1)}, u32[]{:S(2)}, u32[]{:S(2)}) collective-permute-start(bf16[4,256,512]{2,1,0:T(8,128)(2,1)S(1)} %pad_maximum_fusion.refs_1_.refs_2_.refs_0_), channel_id=1, source_target_pairs={{0,1},{1,0},{2,3},{3,2},{4,5},{5,4},{6,7},{7,6},{8,9},{9,8},{10,11... | collective-permute-start | bytes 3145736 | tf_op jit(solution)/shard_map/ppermute | solution.py:342
  85.2 22.8 %copy-start.3 = (bf16[4,256,512]{2,1,0:T(8,128)(2,1)}, bf16[4,256,512]{2,1,0:T(8,128)(2,1)S(1)}, u32[]{:S(2)}) copy-start(bf16[4,256,512]{2,1,0:T(8,128)(2,1)S(1)} %collective-permute-done.4.refs_2_.refs_3_.refs_1_) | copy-start | bytes 3145732
  85.2 21.0 %collective-permute-start.8 = (bf16[4,256,512]{2,1,0:T(8,128)(2,1)S(1)}, bf16[4,256,512]{2,1,0:T(8,128)(2,1)}, u32[]{:S(2)}, u32[]{:S(2)}) collective-permute-start(bf16[4,256,512]{2,1,0:T(8,128)(2,1)S(1)} %collective-permute-done.4.refs_2_.refs_3_.refs_1_), channel_id=1, source_target_pairs={{0,1},{1,0},{2,3},{3,2},{4,5},{5,4},{6,7},{7,6},{8,9},{9,8},{10,11... | collective-permute-start | bytes 3145736 | tf_op jit(solution)/shard_map/ppermute | solution.py:342
  90.9 15.3 %collective-permute-start.10 = (bf16[4,256,512]{2,1,0:T(8,128)(2,1)}, bf16[4,256,512]{2,1,0:T(8,128)(2,1)}, u32[]{:S(2)}, u32[]{:S(2)}) collective-permute-start(bf16[4,256,512]{2,1,0:T(8,128)(2,1)} %collective-permute-done.6.refs_4_.refs_5_.refs_3_), channel_id=1, source_target_pairs={{0,1},{1,0},{2,3},{3,2},{4,5},{5,4},{6,7},{7,6},{8,9},{9,8},{10,11... | collective-permute-start | bytes 3145736 | tf_op jit(solution)/shard_map/ppermute | solution.py:342
  103.1 4.9 %collective-permute-start.9 = (bf16[4,256,512]{2,1,0:T(8,128)(2,1)}, bf16[4,256,512]{2,1,0:T(8,128)(2,1)}, u32[]{:S(2)}, u32[]{:S(2)}) collective-permute-start(bf16[4,256,512]{2,1,0:T(8,128)(2,1)} %collective-permute-done.5.refs_3_.refs_4_.refs_2_), channel_id=1, source_target_pairs={{0,1},{1,0},{2,3},{3,2},{4,5},{5,4},{6,7},{7,6},{8,9},{9,8},{10,11... | collective-permute-start | bytes 3145736 | tf_op jit(solution)/shard_map/ppermute | solution.py:342
  122.8 46.2 %all-to-all-start.3 = ((bf16[32,8,1024]{2,1,0:T(8,128)(2,1)}), bf16[32,8,1024]{2,1,0:T(8,128)(2,1)}, u32[]{:S(2)}, u32[]{:S(2)}) async-start(bf16[32,8,1024]{2,1,0:T(8,128)(2,1)} %bitcast.83), calls=%async_computation.3 | async-start | bytes 1048576 | tf_op jit(solution)/shard_map/all_to_all | solution.py:338
  138.6 26.5 %collective-permute-start.11 = (bf16[64,1024]{1,0:T(8,128)(2,1)}, bf16[64,1024]{1,0:T(8,128)(2,1)S(1)}, u32[]{:S(2)}, u32[]{:S(2)}) collective-permute-start(bf16[64,1024]{1,0:T(8,128)(2,1)} %get-tuple-element.28), channel_id=1, source_target_pairs={{0,2},{1,3},{2,4},{3,5},{4,6},{5,7},{6,0},{7,1},{8,10},{9,11},{10,... | collective-permute-start | bytes 393224 | tf_op jit(solution)/shard_map/ppermute | solution.py:406
  140.8 24.3 %collective-permute-start.12 = (bf16[64,1024]{1,0:T(8,128)(2,1)}, bf16[64,1024]{1,0:T(8,128)(2,1)S(1)}, u32[]{:S(2)}, u32[]{:S(2)}) collective-permute-start(bf16[64,1024]{1,0:T(8,128)(2,1)} %get-tuple-element.27), channel_id=1, source_target_pairs={{0,4},{1,5},{2,6},{3,7},{4,0},{5,1},{6,2},{7,3},{8,12},{9,13},{10,... | collective-permute-start | bytes 393224 | tf_op jit(solution)/shard_map/ppermute | solution.py:406
  145.9 13.4 %copy-start.1 = (bf16[4,256,512]{2,1,0:T(8,128)(2,1)S(1)}, bf16[4,256,512]{2,1,0:T(8,128)(2,1)}, u32[]{:S(2)}) copy-start(bf16[4,256,512]{2,1,0:T(8,128)(2,1)} %copy-done) | copy-start | bytes 3145732
  145.9 13.4 %copy-start.11 = (s32[13]{0:T(128)S(1)}, s32[13]{0:T(128)}, u32[]{:S(2)}) copy-start(s32[13]{0:T(128)} %concatenate.12.scalar_ref) | copy-start | bytes 160
  146.0 19.2 %collective-permute-start.13 = (bf16[64,1024]{1,0:T(8,128)(2,1)}, bf16[64,1024]{1,0:T(8,128)(2,1)S(1)}, u32[]{:S(2)}, u32[]{:S(2)}) collective-permute-start(bf16[64,1024]{1,0:T(8,128)(2,1)} %get-tuple-element.26), channel_id=1, source_target_pairs={{0,6},{1,7},{2,0},{3,1},{4,2},{5,3},{6,4},{7,5},{8,14},{9,15},{10,... | collective-permute-start | bytes 393224 | tf_op jit(solution)/shard_map/ppermute | solution.py:406
  159.4 1.2 copy-start.4
  160.6 1.0 copy-start.7
  169.0 4.2 %collective-permute-start.14 = (bf16[8,16,1024]{2,1,0:T(8,128)(2,1)S(1)}, bf16[8,16,1024]{2,1,0:T(8,128)(2,1)S(1)}, u32[]{:S(2)}, u32[]{:S(2)}) collective-permute-start(bf16[8,16,1024]{2,1,0:T(8,128)(2,1)S(1)} %get-tuple-element.20), channel_id=1, source_target_pairs={{0,1},{1,0},{2,3},{3,2},{4,5},{5,4},{6,7},{7,6},{8,9},{9,8},{10,11... | collective-permute-start | bytes 786440 | tf_op jit(solution)/shard_map/ppermute | solution.py:342
  173.2 9.4 %collective-permute-start.15 = (bf16[8,16,1024]{2,1,0:T(8,128)(2,1)S(1)}, bf16[8,16,1024]{2,1,0:T(8,128)(2,1)S(1)}, u32[]{:S(2)}, u32[]{:S(2)}) collective-permute-start(bf16[8,16,1024]{2,1,0:T(8,128)(2,1)S(1)} %get-tuple-element.32), channel_id=1, source_target_pairs={{0,8},{8,0},{1,9},{9,1},{2,10},{10,2},{3,11},{11,3},{4,12},{12,4},... | collective-permute-start | bytes 786440 | tf_op jit(solution)/shard_map/ppermute | solution.py:342
  175.1 1.0 copy-start.8
  176.2 1.0 copy-start.10

commit v5 on v4

--- a/solution.py
+++ b/solution.py
@@ -269,6 +269,7 @@
             out_specs=pl.BlockSpec((size, size), lambda i, p: (0, 0)),
         ),
         compiler_params=pltpu.CompilerParams(vmem_limit_bytes=24 * 2**20),
+        cost_estimate=pl.CostEstimate(flops=1000, bytes_accessed=1000, transcendentals=0),
         name="gather_out",
     )(scalars, *weights, after)
 
@@ -406,11 +407,11 @@
     back = [z[0]] + [lax.ppermute(z[k], ALL, hop_x(k)) for k in range(1, 4)]
     (along_x,) = attend((1,), (normed,), every, (blocks_x,), scalars)
     w_whole = gather_out(scalars, every, along_x)
-    back_c = jnp.stack([b[r : r + 16] for r in (16, 48) for b in back])
-    back_c = swap(together(back_c, (along_y, w_whole)), "c")
-    back_y = jnp.concatenate([jnp.stack([b[32:48] for b in back]), back_c[4:]], axis=0)
+    far_c = swap(jnp.stack([b[48:] for b in back]), "c")
+    back_y = jnp.concatenate([jnp.stack([b[32:48] for b in back]), far_c], axis=0)
     back_y = swap(back_y, "yl")
-    near_z = jnp.concatenate([jnp.stack([b[:16] for b in back]), back_c[:4]], axis=0)
+    near_c = swap(jnp.stack([b[16:32] for b in back]), "c")
+    near_z = jnp.concatenate([jnp.stack([b[:16] for b in back]), near_c], axis=0)
     mixed = mix(0, (rows // 2, features), scalars, flat, along_x, along_y, near_z, w_whole)
     mixed = mix(1, flat.shape, scalars, flat, along_x, along_y, back_y, w_whole, mixed)
     return mixed.reshape(shape)

time: 188 us -> 190 us (1.011)
  waiting for transfers between devices: 38.8 us -> 35.5 us
  local copies, waits for them, and re-layouts: 16 us -> 19.2 us
  starting transfers between devices: 95.7 us -> 98.6 us
    ppermute x7 -> x8, waiting for transfers between devices: 7.82 us -> 2.88 us  [swap(): return lax.ppermute(array, axis, [(0, 1), (1, 0)])]
    ppermute x3, waiting for transfers between devices: 0.01 us -> 4.59 us  [shards(): back = [z[0]] + [lax.ppermute(z[k], ALL, hop_x(k)) for k in range(1, 4)]]
    ppermute x7 -> x8, starting transfers between devices: 16.4 us -> 19.7 us  [swap(): return lax.ppermute(array, axis, [(0, 1), (1, 0)])]
    all_to_all x4, waiting for transfers between devices: 13.3 us -> 10.3 us  [exchange(): return lax.all_to_all(array, axes, split_axis=0, concat_axis=0, tiled=True)]
    unnamed x42 -> x38, local copies, waits for them, and re-layouts: 8.89 us -> 10.5 us
  transfers between devices with their start and end apart: 20 -> 21, of which waited for: 11 -> 9; matrix products, arithmetic and copies ran while one was open for 3% -> 3% of each run, Pallas kernels for 9% -> 9%
where the time goes in v5:
time: 190 us; the launch traced here: 188 us
  starting transfers between devices  98.6 us (52%)
  waiting for transfers between devices  35.5 us (19%)
  Pallas kernels  34 us (18%)
  local copies, waits for them, and re-layouts  19.2 us (10%)
    all_to_all x4, starting transfers between devices, exchange(): return lax.all_to_all(array, axes, split_axis=0, concat_axis=0, tiled=True)  49.6 us
    pallas_call x2, Pallas kernels, attend(): pl.pallas_call(functools.partial(attend_kernel, axes), out_shape=[jax.Sha...  26 us
    ppermute x8, starting transfers between devices, swap(): return lax.ppermute(array, axis, [(0, 1), (1, 0)])  19.7 us
    unnamed x38, local copies, waits for them, and re-layouts  10.5 us
    all_to_all x4, waiting for transfers between devices, exchange(): return lax.all_to_all(array, axes, split_axis=0, concat_axis=0, tiled=True)  10.3 us
    ppermute x3, starting transfers between devices, shards(): lax.ppermute(piece, ALL, hop_plane(k, 0))  10.2 us
    ppermute x3, starting transfers between devices, shards(): lax.ppermute(first, ALL, hop_plane(k, 1))  9.94 us
    ppermute x3, waiting for transfers between devices, shards(): lax.ppermute(first, ALL, hop_plane(k, 1))  9.92 us
  transfers between devices with their start and end apart: 21, of which 9 were waited for; matrix products, arithmetic and copies ran while one was open for 3% of the time, Pallas kernels for 9%

profile of v5, /device:TPU:1, one launch (start us, length us, event | category | flops | bytes accessed | tf_op | source)
XLA Modules:
  0.0 188.1 jit_solution(9061589941672800006)
XLA Ops:
  0.0 0.7 dynamic_slice.15
  0.7 0.7 fusion.8
  1.4 0.7 broadcast_in_dim.2
  2.2 15.7 %all-to-all-start = ((bf16[16,16,512]{2,1,0:T(8,128)(2,1)}), bf16[16,16,512]{2,1,0:T(8,128)(2,1)S(1)}, u32[]{:S(2)}, u32[]{:S(2)}) async-start(bf16[16,16,512]{2,1,0:T(8,128)(2,1)} %broadcast_in_dim.2), calls=%async_computation | async-start | bytes 524288 | tf_op jit(solution)/shard_map/all_to_all | solution.py:339
  17.9 1.2 reshape.42.tokens_ref
  19.2 1.2 norm.1.refs_0_
  20.4 0.1 rev.9
  20.5 0.3 bias_64.1.refs_9_.refs_10_
  20.8 1.0 copy-done.2
  21.8 0.1 rev.10
  21.9 0.3 bias_32.2.refs_10_.refs_11_
  22.2 1.0 copy-done.5
  23.2 0.1 rev.11
  23.3 0.3 bias_32.3.refs_12_.refs_13_
  23.6 1.0 copy-done.6
  24.6 6.5 %all-to-all-done = bf16[16,16,512]{2,1,0:T(8,128)(2,1)S(1)} async-done(((bf16[16,16,512]{2,1,0:T(8,128)(2,1)}), bf16[16,16,512]{2,1,0:T(8,128)(2,1)S(1)}, u32[]{:S(2)}, u32[]{:S(2)}) %all-to-all-start) | async-done | bytes 262176 | tf_op jit(solution)/shard_map/all_to_all | solution.py:339
  31.1 13.9 %all-to-all-start.1 = ((bf16[32,8,1024]{2,1,0:T(8,128)(2,1)}), bf16[32,8,1024]{2,1,0:T(8,128)(2,1)S(1)}, u32[]{:S(2)}, u32[]{:S(2)}) async-start(bf16[32,8,1024]{2,1,0:T(8,128)(2,1)} %bitcast.13), calls=%async_computation.1 | async-start | bytes 1048576 | tf_op jit(solution)/shard_map/all_to_all | solution.py:339
  45.0 2.9 %collective-permute-start = (bf16[128,512]{1,0:T(8,128)(2,1)S(1)}, bf16[128,512]{1,0:T(8,128)(2,1)S(1)}, u32[]{:S(2)}, u32[]{:S(2)}) collective-permute-start(bf16[128,512]{1,0:T(8,128)(2,1)S(1)} %broadcast_select_fusion.2), channel_id=1, source_target_pairs={{0,1},{1,0},{2,3},{3,2},{4,5},{5,4},{6,7},{7,6},{8,9},{9,8},{10,11... | collective-permute-start | bytes 393224 | tf_op jit(solution)/shard_map/ppermute | solution.py:343
  47.9 1.0 collective-permute-done
  49.0 4.8 %collective-permute-start.3 = (bf16[256,512]{1,0:T(8,128)(2,1)S(1)}, bf16[256,512]{1,0:T(8,128)(2,1)S(1)}, u32[]{:S(2)}, u32[]{:S(2)}) collective-permute-start(bf16[256,512]{1,0:T(8,128)(2,1)S(1)} %bitcast.67), channel_id=1, source_target_pairs={{0,6},{1,265},{2,0},{3,267},{4,2},{5,269},{6,4},{7,271},{8,14},{9,... | collective-permute-start | bytes 786440 | tf_op jit(solution)/shard_map/ppermute | solution.py:387
  53.7 1.9 %collective-permute-start.2 = (bf16[256,512]{1,0:T(8,128)(2,1)S(1)}, bf16[256,512]{1,0:T(8,128)(2,1)S(1)}, u32[]{:S(2)}, u32[]{:S(2)}) collective-permute-start(bf16[256,512]{1,0:T(8,128)(2,1)S(1)} %bitcast.68), channel_id=1, source_target_pairs={{0,2},{1,9},{2,4},{3,11},{4,6},{5,13},{6,0},{7,15},{8,10},{9,257},... | collective-permute-start | bytes 786440 | tf_op jit(solution)/shard_map/ppermute | solution.py:387
  55.6 3.5 %collective-permute-start.1 = (bf16[256,512]{1,0:T(8,128)(2,1)S(1)}, bf16[256,512]{1,0:T(8,128)(2,1)S(1)}, u32[]{:S(2)}, u32[]{:S(2)}) collective-permute-start(bf16[256,512]{1,0:T(8,128)(2,1)S(1)} %bitcast.69), channel_id=1, source_target_pairs={{0,4},{1,257},{2,6},{3,259},{4,0},{5,261},{6,2},{7,263},{8,12},{9,... | collective-permute-start | bytes 786440 | tf_op jit(solution)/shard_map/ppermute | solution.py:387
  59.2 7.8 %collective-permute-done.2 = bf16[256,512]{1,0:T(8,128)(2,1)S(1)} collective-permute-done((bf16[256,512]{1,0:T(8,128)(2,1)S(1)}, bf16[256,512]{1,0:T(8,128)(2,1)S(1)}, u32[]{:S(2)}, u32[]{:S(2)}) %collective-permute-start.2) | collective-permute-done | bytes 262176 | tf_op jit(solution)/shard_map/ppermute | solution.py:387
  67.0 0.1 pad_maximum_fusion.refs_1_.refs_2_.refs_0_
  67.1 3.1 %collective-permute-start.4 = (bf16[4,256,512]{2,1,0:T(8,128)(2,1)S(1)}, bf16[4,256,512]{2,1,0:T(8,128)(2,1)S(1)}, u32[]{:S(2)}, u32[]{:S(2)}) collective-permute-start(bf16[4,256,512]{2,1,0:T(8,128)(2,1)S(1)} %pad_maximum_fusion.refs_1_.refs_2_.refs_0_), channel_id=1, source_target_pairs={{0,8},{1,3},{2,10},{3,5},{4,12},{5,7},{6,14},{7,1},{8,256},{9,11},... | collective-permute-start | bytes 3145736 | tf_op jit(solution)/shard_map/ppermute | solution.py:389
  70.2 3.4 %collective-permute-start.6 = (bf16[4,256,512]{2,1,0:T(8,128)(2,1)S(1)}, bf16[4,256,512]{2,1,0:T(8,128)(2,1)}, u32[]{:S(2)}, u32[]{:S(2)}) collective-permute-start(bf16[4,256,512]{2,1,0:T(8,128)(2,1)S(1)} %pad_maximum_fusion.refs_1_.refs_2_.refs_0_), channel_id=1, source_target_pairs={{0,264},{1,7},{2,266},{3,1},{4,268},{5,3},{6,270},{7,5},{8,0},{9,1... | collective-permute-start | bytes 3145736 | tf_op jit(solution)/shard_map/ppermute | solution.py:389
  73.6 3.4 %collective-permute-start.5 = (bf16[4,256,512]{2,1,0:T(8,128)(2,1)S(1)}, bf16[4,256,512]{2,1,0:T(8,128)(2,1)}, u32[]{:S(2)}, u32[]{:S(2)}) collective-permute-start(bf16[4,256,512]{2,1,0:T(8,128)(2,1)S(1)} %pad_maximum_fusion.refs_1_.refs_2_.refs_0_), channel_id=1, source_target_pairs={{0,256},{1,5},{2,258},{3,7},{4,260},{5,1},{6,262},{7,3},{8,264},{9... | collective-permute-start | bytes 3145736 | tf_op jit(solution)/shard_map/ppermute | solution.py:389
  77.1 0.1 all-to-all-done.1
  77.1 6.0 %all-to-all-start.2 = ((bf16[16,16,1024]{2,1,0:T(8,128)(2,1)}), bf16[16,16,1024]{2,1,0:T(8,128)(2,1)}, u32[]{:S(2)}, u32[]{:S(2)}) async-start(bf16[16,16,1024]{2,1,0:T(8,128)(2,1)} %bitcast.15), calls=%async_computation.2 | async-start | bytes 1048576 | tf_op jit(solution)/shard_map/all_to_all | solution.py:339
  83.1 2.1 %collective-permute-start.7 = (bf16[4,256,512]{2,1,0:T(8,128)(2,1)S(1)}, bf16[4,256,512]{2,1,0:T(8,128)(2,1)}, u32[]{:S(2)}, u32[]{:S(2)}) collective-permute-start(bf16[4,256,512]{2,1,0:T(8,128)(2,1)S(1)} %pad_maximum_fusion.refs_1_.refs_2_.refs_0_), channel_id=1, source_target_pairs={{0,1},{1,0},{2,3},{3,2},{4,5},{5,4},{6,7},{7,6},{8,9},{9,8},{10,11... | collective-permute-start | bytes 3145736 | tf_op jit(solution)/shard_map/ppermute | solution.py:343
  85.2 2.3 %collective-permute-start.8 = (bf16[4,256,512]{2,1,0:T(8,128)(2,1)S(1)}, bf16[4,256,512]{2,1,0:T(8,128)(2,1)}, u32[]{:S(2)}, u32[]{:S(2)}) collective-permute-start(bf16[4,256,512]{2,1,0:T(8,128)(2,1)S(1)} %collective-permute-done.4.refs_2_.refs_3_.refs_1_), channel_id=1, source_target_pairs={{0,1},{1,0},{2,3},{3,2},{4,5},{5,4},{6,7},{7,6},{8,9},{9,8},{10,11... | collective-permute-start | bytes 3145736 | tf_op jit(solution)/shard_map/ppermute | solution.py:343
  87.5 3.4 %collective-permute-done.6.refs_4_.refs_5_.refs_3_ = bf16[4,256,512]{2,1,0:T(8,128)(2,1)} collective-permute-done((bf16[4,256,512]{2,1,0:T(8,128)(2,1)S(1)}, bf16[4,256,512]{2,1,0:T(8,128)(2,1)}, u32[]{:S(2)}, u32[]{:S(2)}) %collective-permute-start.6) | collective-permute-done | bytes 1048608 | tf_op jit(solution)/shard_map/ppermute | solution.py:389
  90.9 1.9 %collective-permute-start.10 = (bf16[4,256,512]{2,1,0:T(8,128)(2,1)}, bf16[4,256,512]{2,1,0:T(8,128)(2,1)}, u32[]{:S(2)}, u32[]{:S(2)}) collective-permute-start(bf16[4,256,512]{2,1,0:T(8,128)(2,1)} %collective-permute-done.6.refs_4_.refs_5_.refs_3_), channel_id=1, source_target_pairs={{0,1},{1,0},{2,3},{3,2},{4,5},{5,4},{6,7},{7,6},{8,9},{9,8},{10,11... | collective-permute-start | bytes 3145736 | tf_op jit(solution)/shard_map/ppermute | solution.py:343
  92.8 6.5 %collective-permute-done.5.refs_3_.refs_4_.refs_2_ = bf16[4,256,512]{2,1,0:T(8,128)(2,1)} collective-permute-done((bf16[4,256,512]{2,1,0:T(8,128)(2,1)S(1)}, bf16[4,256,512]{2,1,0:T(8,128)(2,1)}, u32[]{:S(2)}, u32[]{:S(2)}) %collective-permute-start.5) | collective-permute-done | bytes 1048608 | tf_op jit(solution)/shard_map/ppermute | solution.py:389
  99.3 3.8 %all-to-all-done.2 = bf16[16,16,1024]{2,1,0:T(8,128)(2,1)} async-done(((bf16[16,16,1024]{2,1,0:T(8,128)(2,1)}), bf16[16,16,1024]{2,1,0:T(8,128)(2,1)}, u32[]{:S(2)}, u32[]{:S(2)}) %all-to-all-start.2) | async-done | bytes 524320 | tf_op jit(solution)/shard_map/all_to_all | solution.py:339
  103.1 2.3 %collective-permute-start.9 = (bf16[4,256,512]{2,1,0:T(8,128)(2,1)}, bf16[4,256,512]{2,1,0:T(8,128)(2,1)}, u32[]{:S(2)}, u32[]{:S(2)}) collective-permute-start(bf16[4,256,512]{2,1,0:T(8,128)(2,1)} %collective-permute-done.5.refs_3_.refs_4_.refs_2_), channel_id=1, source_target_pairs={{0,1},{1,0},{2,3},{3,2},{4,5},{5,4},{6,7},{7,6},{8,9},{9,8},{10,11... | collective-permute-start | bytes 3145736 | tf_op jit(solution)/shard_map/ppermute | solution.py:343
  105.5 0.6 concatenate.12.scalar_ref
  106.1 1.9 %collective-permute-done.9.refs_7_.refs_8_.refs_6_ = bf16[4,256,512]{2,1,0:T(8,128)(2,1)} collective-permute-done((bf16[4,256,512]{2,1,0:T(8,128)(2,1)}, bf16[4,256,512]{2,1,0:T(8,128)(2,1)}, u32[]{:S(2)}, u32[]{:S(2)}) %collective-permute-start.9) | collective-permute-done | bytes 1048608 | tf_op jit(solution)/shard_map/ppermute | solution.py:343
  108.0 14.8 %attend_2_3.1 = (bf16[256,1024]{1,0:T(8,128)(2,1)}, bf16[256,1024]{1,0:T(8,128)(2,1)}) custom-call(s32[13]{0:T(128)} %concatenate.12.scalar_ref, bf16[256,1024]{1,0:T(8,128)(2,1)} %bitcast.66, bf16[256,1024]{1,0:T(8,128)(2,1)} %bitcast.16.refs_1_, bf16[4,256,512]{2,1,0:T(8,128)(2,1)} %copy-done, bf16[4,256,512]{2,1,0:T(8,128)(2,1)} %copy-done.3, ...), custom_call_target="tpu_custom_call" | custom-call | flops 1000 | bytes 1000 | tf_op jit(solution)/shard_map/attend_2_3/pallas_call | solution.py:219
  122.8 1.4 bitcast_dynamic-update-slice_fusion
  124.2 1.1 fusion.7
  125.2 14.0 %all-to-all-start.3 = ((bf16[32,8,1024]{2,1,0:T(8,128)(2,1)}), bf16[32,8,1024]{2,1,0:T(8,128)(2,1)}, u32[]{:S(2)}, u32[]{:S(2)}) async-start(bf16[32,8,1024]{2,1,0:T(8,128)(2,1)} %bitcast.71), calls=%async_computation.3 | async-start | bytes 1048576 | tf_op jit(solution)/shard_map/all_to_all | solution.py:339
  139.2 4.3 %collective-permute-start.13 = (bf16[64,1024]{1,0:T(8,128)(2,1)S(1)}, bf16[64,1024]{1,0:T(8,128)(2,1)S(1)}, u32[]{:S(2)}, u32[]{:S(2)}) collective-permute-start(bf16[64,1024]{1,0:T(8,128)(2,1)S(1)} %get-tuple-element.25), channel_id=1, source_target_pairs={{0,6},{1,7},{2,0},{3,1},{4,2},{5,3},{6,4},{7,5},{8,14},{9,15},{10,... | collective-permute-start | bytes 393224 | tf_op jit(solution)/shard_map/ppermute | solution.py:407
  143.5 0.8 slice_bitcast_fusion.12
  144.3 1.9 %collective-permute-start.11 = (bf16[64,1024]{1,0:T(8,128)(2,1)S(1)}, bf16[64,1024]{1,0:T(8,128)(2,1)S(1)}, u32[]{:S(2)}, u32[]{:S(2)}) collective-permute-start(bf16[64,1024]{1,0:T(8,128)(2,1)S(1)} %get-tuple-element.27), channel_id=1, source_target_pairs={{0,2},{1,3},{2,4},{3,5},{4,6},{5,7},{6,0},{7,1},{8,10},{9,11},{10,... | collective-permute-start | bytes 393224 | tf_op jit(solution)/shard_map/ppermute | solution.py:407
  146.2 3.1 %collective-permute-start.12 = (bf16[64,1024]{1,0:T(8,128)(2,1)S(1)}, bf16[64,1024]{1,0:T(8,128)(2,1)S(1)}, u32[]{:S(2)}, u32[]{:S(2)}) collective-permute-start(bf16[64,1024]{1,0:T(8,128)(2,1)S(1)} %get-tuple-element.26), channel_id=1, source_target_pairs={{0,4},{1,5},{2,6},{3,7},{4,0},{5,1},{6,2},{7,3},{8,12},{9,13},{10,... | collective-permute-start | bytes 393224 | tf_op jit(solution)/shard_map/ppermute | solution.py:407
  149.3 4.6 %collective-permute-done.12 = bf16[64,1024]{1,0:T(8,128)(2,1)S(1)} collective-permute-done((bf16[64,1024]{1,0:T(8,128)(2,1)S(1)}, bf16[64,1024]{1,0:T(8,128)(2,1)S(1)}, u32[]{:S(2)}, u32[]{:S(2)}) %collective-permute-start.12) | collective-permute-done | bytes 131104 | tf_op jit(solution)/shard_map/ppermute | solution.py:407
  154.0 4.1 %collective-permute-start.14 = (bf16[4,16,1024]{2,1,0:T(8,128)(2,1)S(1)}, bf16[4,16,1024]{2,1,0:T(8,128)(2,1)S(1)}, u32[]{:S(2)}, u32[]{:S(2)}) collective-permute-start(bf16[4,16,1024]{2,1,0:T(8,128)(2,1)S(1)} %pad_maximum_fusion.2), channel_id=1, source_target_pairs={{0,1},{1,0},{2,3},{3,2},{4,5},{5,4},{6,7},{7,6},{8,9},{9,8},{10,11... | collective-permute-start | bytes 393224 | tf_op jit(solution)/shard_map/ppermute | solution.py:343
  158.0 0.6 fusion.2
  158.7 0.6 fusion.1
  159.3 0.6 fusion
  159.9 0.7 constant_dynamic-update-slice_fusion
  160.5 1.9 %collective-permute-start.15 = (bf16[8,16,1024]{2,1,0:T(8,128)(2,1)}, bf16[8,16,1024]{2,1,0:T(8,128)(2,1)}, u32[]{:S(2)}, u32[]{:S(2)}) collective-permute-start(bf16[8,16,1024]{2,1,0:T(8,128)(2,1)} %constant_dynamic-update-slice_fusion), channel_id=1, source_target_pairs={{0,8},{8,0},{1,9},{9,1},{2,10},{10,2},{3,11},{11,3},{4,12},{12,4},... | collective-permute-start | bytes 786440 | tf_op jit(solution)/shard_map/ppermute | solution.py:343
  162.5 2.2 %collective-permute-start.16 = (bf16[4,16,1024]{2,1,0:T(8,128)(2,1)S(1)}, bf16[4,16,1024]{2,1,0:T(8,128)(2,1)}, u32[]{:S(2)}, u32[]{:S(2)}) collective-permute-start(bf16[4,16,1024]{2,1,0:T(8,128)(2,1)S(1)} %pad_maximum_fusion.3), channel_id=1, source_target_pairs={{0,1},{1,0},{2,3},{3,2},{4,5},{5,4},{6,7},{7,6},{8,9},{9,8},{10,11... | collective-permute-start | bytes 393224 | tf_op jit(solution)/shard_map/ppermute | solution.py:343
  164.8 11.2 %attend_1.1.refs_8_.x_ref = bf16[256,1024]{1,0:T(8,128)(2,1)} custom-call(s32[13]{0:T(128)} %concatenate.12.scalar_ref, bf16[256,1024]{1,0:T(8,128)(2,1)} %norm.1.refs_0_, bf16[4,256,512]{2,1,0:T(8,128)(2,1)} %copy-done, bf16[4,256,512]{2,1,0:T(8,128)(2,1)} %copy-done.3, bf16[4,256,512]{2,1,0:T(8,128)(2,1)} %collective-permute-done.5.refs_3_.refs_4_.refs_2_, ...), custom_call_target="tpu_custom_call" | custom-call | flops 1000 | bytes 1000 | tf_op jit(solution)/shard_map/attend_1/pallas_call | solution.py:219
  176.0 1.2 copy-done.4
  177.2 1.0 copy-done.7
  178.2 2.7 %gather_out.1.w_ref = bf16[1024,1024]{1,0:T(8,128)(2,1)S(1)} custom-call(s32[13]{0:T(128)S(1)} %copy-done.11, bf16[4,256,512]{2,1,0:T(8,128)(2,1)S(1)} %copy-done.1, bf16[4,256,512]{2,1,0:T(8,128)(2,1)S(1)} %copy-done.4, bf16[4,256,512]{2,1,0:T(8,128)(2,1)} %collective-permute-done.5.refs_3_.refs_4_.refs_2_, ...), custom_call_target="tpu_custom_call" | custom-call | flops 1000 | bytes 1000 | tf_op jit(solution)/shard_map/gather_out/pallas_call | solution.py:262
  180.9 0.9 constant_dynamic-update-slice_fusion.1.parts_ref
  181.9 1.0 copy-done.8
  182.9 1.0 copy-done.10
  183.9 1.5 mix_0.1.refs_0_
  185.5 1.6 mix_1.1
  187.1 1.0 reshape.51
  (53 shorter events, 0.3 us)
Async XLA Ops:
  0.0 20.4 %copy-start.13 = (f32[16,127]{1,0:T(8,128)S(1)}, f32[16,127]{1,0:T(8,128)}, u32[]{:S(2)}) copy-start(f32[16,127]{1,0:T(8,128)} %param.10) | copy-start | bytes 24388
  0.0 21.8 %copy-start.14 = (f32[16,63]{1,0:T(8,128)S(1)}, f32[16,63]{1,0:T(8,128)}, u32[]{:S(2)}) copy-start(f32[16,63]{1,0:T(8,128)} %param.11) | copy-start | bytes 12100
  2.2 28.9 %all-to-all-start = ((bf16[16,16,512]{2,1,0:T(8,128)(2,1)}), bf16[16,16,512]{2,1,0:T(8,128)(2,1)S(1)}, u32[]{:S(2)}, u32[]{:S(2)}) async-start(bf16[16,16,512]{2,1,0:T(8,128)(2,1)} %broadcast_in_dim.2), calls=%async_computation | async-start | bytes 524288 | tf_op jit(solution)/shard_map/all_to_all | solution.py:339
  17.9 5.3 %copy-start.15 = (f32[16,63]{1,0:T(8,128)S(1)}, f32[16,63]{1,0:T(8,128)}, u32[]{:S(2)}) copy-start(f32[16,63]{1,0:T(8,128)} %param.12) | copy-start | bytes 12100
  19.2 4.4 %copy-start.9 = (bf16[256,1024]{1,0:T(8,128)(2,1)}, bf16[256,1024]{1,0:T(8,128)(2,1)S(1)}, u32[]{:S(2)}) copy-start(bf16[256,1024]{1,0:T(8,128)(2,1)S(1)} %reshape.42.tokens_ref) | copy-start | bytes 1572868
  20.8 1.0 copy-start.2
  22.2 1.0 copy-start.5
  23.6 1.0 copy-start.6
  31.1 46.0 %all-to-all-start.1 = ((bf16[32,8,1024]{2,1,0:T(8,128)(2,1)}), bf16[32,8,1024]{2,1,0:T(8,128)(2,1)S(1)}, u32[]{:S(2)}, u32[]{:S(2)}) async-start(bf16[32,8,1024]{2,1,0:T(8,128)(2,1)} %bitcast.13), calls=%async_computation.1 | async-start | bytes 1048576 | tf_op jit(solution)/shard_map/all_to_all | solution.py:339
  45.0 60.4 %copy-start.16 = (s32[4]{0:T(128)S(1)}, s32[4]{0:T(128)}, u32[]{:S(2)}) copy-start(s32[4]{0:T(128)} %constant.81) | copy-start | bytes 52
  45.0 3.9 %collective-permute-start = (bf16[128,512]{1,0:T(8,128)(2,1)S(1)}, bf16[128,512]{1,0:T(8,128)(2,1)S(1)}, u32[]{:S(2)}, u32[]{:S(2)}) collective-permute-start(bf16[128,512]{1,0:T(8,128)(2,1)S(1)} %broadcast_select_fusion.2), channel_id=1, source_target_pairs={{0,1},{1,0},{2,3},{3,2},{4,5},{5,4},{6,7},{7,6},{8,9},{9,8},{10,11... | collective-permute-start | bytes 393224 | tf_op jit(solution)/shard_map/ppermute | solution.py:343
  49.0 10.2 %collective-permute-start.3 = (bf16[256,512]{1,0:T(8,128)(2,1)S(1)}, bf16[256,512]{1,0:T(8,128)(2,1)S(1)}, u32[]{:S(2)}, u32[]{:S(2)}) collective-permute-start(bf16[256,512]{1,0:T(8,128)(2,1)S(1)} %bitcast.67), channel_id=1, source_target_pairs={{0,6},{1,265},{2,0},{3,267},{4,2},{5,269},{6,4},{7,271},{8,14},{9,... | collective-permute-start | bytes 786440 | tf_op jit(solution)/shard_map/ppermute | solution.py:387
  53.7 13.2 %collective-permute-start.2 = (bf16[256,512]{1,0:T(8,128)(2,1)S(1)}, bf16[256,512]{1,0:T(8,128)(2,1)S(1)}, u32[]{:S(2)}, u32[]{:S(2)}) collective-permute-start(bf16[256,512]{1,0:T(8,128)(2,1)S(1)} %bitcast.68), channel_id=1, source_target_pairs={{0,2},{1,9},{2,4},{3,11},{4,6},{5,13},{6,0},{7,15},{8,10},{9,257},... | collective-permute-start | bytes 786440 | tf_op jit(solution)/shard_map/ppermute | solution.py:387
  55.6 11.3 %collective-permute-start.1 = (bf16[256,512]{1,0:T(8,128)(2,1)S(1)}, bf16[256,512]{1,0:T(8,128)(2,1)S(1)}, u32[]{:S(2)}, u32[]{:S(2)}) collective-permute-start(bf16[256,512]{1,0:T(8,128)(2,1)S(1)} %bitcast.69), channel_id=1, source_target_pairs={{0,4},{1,257},{2,6},{3,259},{4,0},{5,261},{6,2},{7,263},{8,12},{9,... | collective-permute-start | bytes 786440 | tf_op jit(solution)/shard_map/ppermute | solution.py:387
  67.1 40.9 %copy-start = (bf16[4,256,512]{2,1,0:T(8,128)(2,1)}, bf16[4,256,512]{2,1,0:T(8,128)(2,1)S(1)}, u32[]{:S(2)}) copy-start(bf16[4,256,512]{2,1,0:T(8,128)(2,1)S(1)} %pad_maximum_fusion.refs_1_.refs_2_.refs_0_) | copy-start | bytes 3145732
  67.1 18.1 %collective-permute-start.4 = (bf16[4,256,512]{2,1,0:T(8,128)(2,1)S(1)}, bf16[4,256,512]{2,1,0:T(8,128)(2,1)S(1)}, u32[]{:S(2)}, u32[]{:S(2)}) collective-permute-start(bf16[4,256,512]{2,1,0:T(8,128)(2,1)S(1)} %pad_maximum_fusion.refs_1_.refs_2_.refs_0_), channel_id=1, source_target_pairs={{0,8},{1,3},{2,10},{3,5},{4,12},{5,7},{6,14},{7,1},{8,256},{9,11},... | collective-permute-start | bytes 3145736 | tf_op jit(solution)/shard_map/ppermute | solution.py:389
  70.2 20.6 %collective-permute-start.6 = (bf16[4,256,512]{2,1,0:T(8,128)(2,1)S(1)}, bf16[4,256,512]{2,1,0:T(8,128)(2,1)}, u32[]{:S(2)}, u32[]{:S(2)}) collective-permute-start(bf16[4,256,512]{2,1,0:T(8,128)(2,1)S(1)} %pad_maximum_fusion.refs_1_.refs_2_.refs_0_), channel_id=1, source_target_pairs={{0,264},{1,7},{2,266},{3,1},{4,268},{5,3},{6,270},{7,5},{8,0},{9,1... | collective-permute-start | bytes 3145736 | tf_op jit(solution)/shard_map/ppermute | solution.py:389
  73.6 25.7 %collective-permute-start.5 = (bf16[4,256,512]{2,1,0:T(8,128)(2,1)S(1)}, bf16[4,256,512]{2,1,0:T(8,128)(2,1)}, u32[]{:S(2)}, u32[]{:S(2)}) collective-permute-start(bf16[4,256,512]{2,1,0:T(8,128)(2,1)S(1)} %pad_maximum_fusion.refs_1_.refs_2_.refs_0_), channel_id=1, source_target_pairs={{0,256},{1,5},{2,258},{3,7},{4,260},{5,1},{6,262},{7,3},{8,264},{9... | collective-permute-start | bytes 3145736 | tf_op jit(solution)/shard_map/ppermute | solution.py:389
  77.1 30.9 %copy-start.12 = (bf16[32,8,1024]{2,1,0:T(8,128)(2,1)}, bf16[32,8,1024]{2,1,0:T(8,128)(2,1)S(1)}, u32[]{:S(2)}) copy-start(bf16[32,8,1024]{2,1,0:T(8,128)(2,1)S(1)} %all-to-all-done.1) | copy-start | bytes 1572868
  77.1 26.0 %all-to-all-start.2 = ((bf16[16,16,1024]{2,1,0:T(8,128)(2,1)}), bf16[16,16,1024]{2,1,0:T(8,128)(2,1)}, u32[]{:S(2)}, u32[]{:S(2)}) async-start(bf16[16,16,1024]{2,1,0:T(8,128)(2,1)} %bitcast.15), calls=%async_computation.2 | async-start | bytes 1048576 | tf_op jit(solution)/shard_map/all_to_all | solution.py:339
  83.1 23.0 %collective-permute-start.7 = (bf16[4,256,512]{2,1,0:T(8,128)(2,1)S(1)}, bf16[4,256,512]{2,1,0:T(8,128)(2,1)}, u32[]{:S(2)}, u32[]{:S(2)}) collective-permute-start(bf16[4,256,512]{2,1,0:T(8,128)(2,1)S(1)} %pad_maximum_fusion.refs_1_.refs_2_.refs_0_), channel_id=1, source_target_pairs={{0,1},{1,0},{2,3},{3,2},{4,5},{5,4},{6,7},{7,6},{8,9},{9,8},{10,11... | collective-permute-start | bytes 3145736 | tf_op jit(solution)/shard_map/ppermute | solution.py:343
  85.2 22.8 %copy-start.3 = (bf16[4,256,512]{2,1,0:T(8,128)(2,1)}, bf16[4,256,512]{2,1,0:T(8,128)(2,1)S(1)}, u32[]{:S(2)}) copy-start(bf16[4,256,512]{2,1,0:T(8,128)(2,1)S(1)} %collective-permute-done.4.refs_2_.refs_3_.refs_1_) | copy-start | bytes 3145732
  85.2 20.9 %collective-permute-start.8 = (bf16[4,256,512]{2,1,0:T(8,128)(2,1)S(1)}, bf16[4,256,512]{2,1,0:T(8,128)(2,1)}, u32[]{:S(2)}, u32[]{:S(2)}) collective-permute-start(bf16[4,256,512]{2,1,0:T(8,128)(2,1)S(1)} %collective-permute-done.4.refs_2_.refs_3_.refs_1_), channel_id=1, source_target_pairs={{0,1},{1,0},{2,3},{3,2},{4,5},{5,4},{6,7},{7,6},{8,9},{9,8},{10,11... | collective-permute-start | bytes 3145736 | tf_op jit(solution)/shard_map/ppermute | solution.py:343
  90.9 15.2 %collective-permute-start.10 = (bf16[4,256,512]{2,1,0:T(8,128)(2,1)}, bf16[4,256,512]{2,1,0:T(8,128)(2,1)}, u32[]{:S(2)}, u32[]{:S(2)}) collective-permute-start(bf16[4,256,512]{2,1,0:T(8,128)(2,1)} %collective-permute-done.6.refs_4_.refs_5_.refs_3_), channel_id=1, source_target_pairs={{0,1},{1,0},{2,3},{3,2},{4,5},{5,4},{6,7},{7,6},{8,9},{9,8},{10,11... | collective-permute-start | bytes 3145736 | tf_op jit(solution)/shard_map/ppermute | solution.py:343
  103.1 4.9 %collective-permute-start.9 = (bf16[4,256,512]{2,1,0:T(8,128)(2,1)}, bf16[4,256,512]{2,1,0:T(8,128)(2,1)}, u32[]{:S(2)}, u32[]{:S(2)}) collective-permute-start(bf16[4,256,512]{2,1,0:T(8,128)(2,1)} %collective-permute-done.5.refs_3_.refs_4_.refs_2_), channel_id=1, source_target_pairs={{0,1},{1,0},{2,3},{3,2},{4,5},{5,4},{6,7},{7,6},{8,9},{9,8},{10,11... | collective-permute-start | bytes 3145736 | tf_op jit(solution)/shard_map/ppermute | solution.py:343
  125.2 56.6 %all-to-all-start.3 = ((bf16[32,8,1024]{2,1,0:T(8,128)(2,1)}), bf16[32,8,1024]{2,1,0:T(8,128)(2,1)}, u32[]{:S(2)}, u32[]{:S(2)}) async-start(bf16[32,8,1024]{2,1,0:T(8,128)(2,1)} %bitcast.71), calls=%async_computation.3 | async-start | bytes 1048576 | tf_op jit(solution)/shard_map/all_to_all | solution.py:339
  139.2 10.1 %collective-permute-start.13 = (bf16[64,1024]{1,0:T(8,128)(2,1)S(1)}, bf16[64,1024]{1,0:T(8,128)(2,1)S(1)}, u32[]{:S(2)}, u32[]{:S(2)}) collective-permute-start(bf16[64,1024]{1,0:T(8,128)(2,1)S(1)} %get-tuple-element.25), channel_id=1, source_target_pairs={{0,6},{1,7},{2,0},{3,1},{4,2},{5,3},{6,4},{7,5},{8,14},{9,15},{10,... | collective-permute-start | bytes 393224 | tf_op jit(solution)/shard_map/ppermute | solution.py:407
  144.3 9.6 %collective-permute-start.11 = (bf16[64,1024]{1,0:T(8,128)(2,1)S(1)}, bf16[64,1024]{1,0:T(8,128)(2,1)S(1)}, u32[]{:S(2)}, u32[]{:S(2)}) collective-permute-start(bf16[64,1024]{1,0:T(8,128)(2,1)S(1)} %get-tuple-element.27), channel_id=1, source_target_pairs={{0,2},{1,3},{2,4},{3,5},{4,6},{5,7},{6,0},{7,1},{8,10},{9,11},{10,... | collective-permute-start | bytes 393224 | tf_op jit(solution)/shard_map/ppermute | solution.py:407
  146.2 7.7 %collective-permute-start.12 = (bf16[64,1024]{1,0:T(8,128)(2,1)S(1)}, bf16[64,1024]{1,0:T(8,128)(2,1)S(1)}, u32[]{:S(2)}, u32[]{:S(2)}) collective-permute-start(bf16[64,1024]{1,0:T(8,128)(2,1)S(1)} %get-tuple-element.26), channel_id=1, source_target_pairs={{0,4},{1,5},{2,6},{3,7},{4,0},{5,1},{6,2},{7,3},{8,12},{9,13},{10,... | collective-permute-start | bytes 393224 | tf_op jit(solution)/shard_map/ppermute | solution.py:407
  154.0 5.9 %collective-permute-start.14 = (bf16[4,16,1024]{2,1,0:T(8,128)(2,1)S(1)}, bf16[4,16,1024]{2,1,0:T(8,128)(2,1)S(1)}, u32[]{:S(2)}, u32[]{:S(2)}) collective-permute-start(bf16[4,16,1024]{2,1,0:T(8,128)(2,1)S(1)} %pad_maximum_fusion.2), channel_id=1, source_target_pairs={{0,1},{1,0},{2,3},{3,2},{4,5},{5,4},{6,7},{7,6},{8,9},{9,8},{10,11... | collective-permute-start | bytes 393224 | tf_op jit(solution)/shard_map/ppermute | solution.py:343
  160.5 24.9 %collective-permute-start.15 = (bf16[8,16,1024]{2,1,0:T(8,128)(2,1)}, bf16[8,16,1024]{2,1,0:T(8,128)(2,1)}, u32[]{:S(2)}, u32[]{:S(2)}) collective-permute-start(bf16[8,16,1024]{2,1,0:T(8,128)(2,1)} %constant_dynamic-update-slice_fusion), channel_id=1, source_target_pairs={{0,8},{8,0},{1,9},{9,1},{2,10},{10,2},{3,11},{11,3},{4,12},{12,4},... | collective-permute-start | bytes 786440 | tf_op jit(solution)/shard_map/ppermute | solution.py:343
  162.5 13.4 %copy-start.1 = (bf16[4,256,512]{2,1,0:T(8,128)(2,1)S(1)}, bf16[4,256,512]{2,1,0:T(8,128)(2,1)}, u32[]{:S(2)}) copy-start(bf16[4,256,512]{2,1,0:T(8,128)(2,1)} %copy-done) | copy-start | bytes 3145732
  162.5 13.4 %copy-start.11 = (s32[13]{0:T(128)S(1)}, s32[13]{0:T(128)}, u32[]{:S(2)}) copy-start(s32[13]{0:T(128)} %concatenate.12.scalar_ref) | copy-start | bytes 160
  162.5 18.4 %collective-permute-start.16 = (bf16[4,16,1024]{2,1,0:T(8,128)(2,1)S(1)}, bf16[4,16,1024]{2,1,0:T(8,128)(2,1)}, u32[]{:S(2)}, u32[]{:S(2)}) collective-permute-start(bf16[4,16,1024]{2,1,0:T(8,128)(2,1)S(1)} %pad_maximum_fusion.3), channel_id=1, source_target_pairs={{0,1},{1,0},{2,3},{3,2},{4,5},{5,4},{6,7},{7,6},{8,9},{9,8},{10,11... | collective-permute-start | bytes 393224 | tf_op jit(solution)/shard_map/ppermute | solution.py:343
  176.0 1.2 copy-start.4
  177.2 1.0 copy-start.7
  181.9 1.0 copy-start.8
  182.9 1.0 copy-start.10

commit v6 on v5

--- a/solution.py
+++ b/solution.py
@@ -232,7 +232,9 @@
             ],
         ),
         compiler_params=pltpu.CompilerParams(vmem_limit_bytes=61 * 2**20),
-        cost_estimate=pl.CostEstimate(flops=1000, bytes_accessed=1000, transcendentals=0),
+        cost_estimate=pl.CostEstimate(
+            flops=10**10 if axes == (1,) else 1000, bytes_accessed=1000, transcendentals=0
+        ),
         name="attend_" + "_".join(map(str, axes)),
     )(scalars, *tokens, *weights, *bias_args, *after)
 
@@ -268,8 +270,8 @@
             in_specs=specs,
             out_specs=pl.BlockSpec((size, size), lambda i, p: (0, 0)),
         ),
-        compiler_params=pltpu.CompilerParams(vmem_limit_bytes=24 * 2**20),
-        cost_estimate=pl.CostEstimate(flops=1000, bytes_accessed=1000, transcendentals=0),
+        compiler_params=pltpu.CompilerParams(vmem_limit_bytes=61 * 2**20),
+        cost_estimate=pl.CostEstimate(flops=3 * 10**9, bytes_accessed=1000, transcendentals=0),
         name="gather_out",
     )(scalars, *weights, after)
 
@@ -403,10 +405,11 @@
     along_y, z = attend((2, 3), (y_lines, z_lines), every, (blocks_y, blocks_z), scalars)
     along_y = exchange(along_y.reshape(peers, -1, features), GY).reshape(rows, features)
 
+    made = z
     z = z.reshape(4, rows // 4, features)
     back = [z[0]] + [lax.ppermute(z[k], ALL, hop_x(k)) for k in range(1, 4)]
     (along_x,) = attend((1,), (normed,), every, (blocks_x,), scalars)
-    w_whole = gather_out(scalars, every, along_x)
+    w_whole = gather_out(scalars, every, made)
     far_c = swap(jnp.stack([b[48:] for b in back]), "c")
     back_y = jnp.concatenate([jnp.stack([b[32:48] for b in back]), far_c], axis=0)
     back_y = swap(back_y, "yl")

time: 190 us -> 178 us (0.937)
  local copies, waits for them, and re-layouts: 19.2 us -> 12.6 us
  waiting for transfers between devices: 35.5 us -> 30.9 us
    unnamed x38 -> x30, local copies, waits for them, and re-layouts: 10.5 us -> 5.36 us
    ppermute x3, waiting for transfers between devices: 4.59 us -> 0.01 us  [shards(): back = [z[0]] + [lax.ppermute(z[k], ALL, hop_x(k)) for k in range(1, 4)]]
  transfers between devices with their start and end apart: 21 -> 21, of which waited for: 9 -> 8; matrix products, arithmetic and copies ran while one was open for 3% -> 2% of each run, Pallas kernels for 9% -> 11%
where the time goes in v6:
time: 178 us; the launch traced here: 177 us
  starting transfers between devices  98 us (55%)
  Pallas kernels  34.5 us (19%)
  waiting for transfers between devices  30.9 us (17%)
  local copies, waits for them, and re-layouts  12.6 us (7%)
    all_to_all x4, starting transfers between devices, exchange(): return lax.all_to_all(array, axes, split_axis=0, concat_axis=0, tiled=True)  49.4 us
    pallas_call x2, Pallas kernels, attend(): pl.pallas_call(functools.partial(attend_kernel, axes), out_shape=[jax.Sha...  26 us
    ppermute x8, starting transfers between devices, swap(): return lax.ppermute(array, axis, [(0, 1), (1, 0)])  19 us
    all_to_all x4, waiting for transfers between devices, exchange(): return lax.all_to_all(array, axes, split_axis=0, concat_axis=0, tiled=True)  10.2 us
    ppermute x3, starting transfers between devices, shards(): lax.ppermute(piece, ALL, hop_plane(k, 0))  10.2 us
    ppermute x3, waiting for transfers between devices, shards(): lax.ppermute(first, ALL, hop_plane(k, 1))  9.96 us
    ppermute x3, starting transfers between devices, shards(): lax.ppermute(first, ALL, hop_plane(k, 1))  9.94 us
    ppermute x3, starting transfers between devices, shards(): back = [z[0]] + [lax.ppermute(z[k], ALL, hop_x(k)) for k in range(1, 4)]  9.45 us
  transfers between devices with their start and end apart: 21, of which 8 were waited for; matrix products, arithmetic and copies ran while one was open for 2% of the time, Pallas kernels for 11%

profile of v6, /device:TPU:1, one launch (start us, length us, event | category | flops | bytes accessed | tf_op | source)
XLA Modules:
  0.0 176.8 jit_solution(587809632651145517)
XLA Ops:
  0.0 0.7 dynamic_slice.15
  0.7 0.7 fusion.8
  1.4 0.8 broadcast_in_dim.2
  2.2 15.7 %all-to-all-start = ((bf16[16,16,512]{2,1,0:T(8,128)(2,1)}), bf16[16,16,512]{2,1,0:T(8,128)(2,1)S(1)}, u32[]{:S(2)}, u32[]{:S(2)}) async-start(bf16[16,16,512]{2,1,0:T(8,128)(2,1)} %broadcast_in_dim.2), calls=%async_computation | async-start | bytes 524288 | tf_op jit(solution)/shard_map/all_to_all | solution.py:341
  18.0 0.0 copy-start.11
  18.0 1.2 reshape.42.tokens_ref
  19.2 1.1 norm.1.refs_0_
  20.3 0.1 rev.9
  20.4 0.3 bias_64.1.refs_9_.refs_10_
  20.8 1.0 copy-done.4
  21.8 0.1 rev.10
  21.8 0.3 bias_32.2.refs_10_.refs_11_
  22.2 1.0 copy-done
  23.2 0.1 rev.11
  23.3 0.3 bias_32.3.refs_12_.refs_13_
  23.6 1.0 copy-done.1
  24.6 6.5 %all-to-all-done = bf16[16,16,512]{2,1,0:T(8,128)(2,1)S(1)} async-done(((bf16[16,16,512]{2,1,0:T(8,128)(2,1)}), bf16[16,16,512]{2,1,0:T(8,128)(2,1)S(1)}, u32[]{:S(2)}, u32[]{:S(2)}) %all-to-all-start) | async-done | bytes 262176 | tf_op jit(solution)/shard_map/all_to_all | solution.py:341
  31.1 13.9 %all-to-all-start.1 = ((bf16[32,8,1024]{2,1,0:T(8,128)(2,1)}), bf16[32,8,1024]{2,1,0:T(8,128)(2,1)S(1)}, u32[]{:S(2)}, u32[]{:S(2)}) async-start(bf16[32,8,1024]{2,1,0:T(8,128)(2,1)} %bitcast.13), calls=%async_computation.1 | async-start | bytes 1048576 | tf_op jit(solution)/shard_map/all_to_all | solution.py:341
  45.0 0.0 copy-start.12
  45.0 2.9 %collective-permute-start = (bf16[128,512]{1,0:T(8,128)(2,1)S(1)}, bf16[128,512]{1,0:T(8,128)(2,1)S(1)}, u32[]{:S(2)}, u32[]{:S(2)}) collective-permute-start(bf16[128,512]{1,0:T(8,128)(2,1)S(1)} %broadcast_select_fusion.2), channel_id=1, source_target_pairs={{0,1},{1,0},{2,3},{3,2},{4,5},{5,4},{6,7},{7,6},{8,9},{9,8},{10,11... | collective-permute-start | bytes 393224 | tf_op jit(solution)/shard_map/ppermute | solution.py:345
  47.9 1.0 collective-permute-done
  49.0 4.8 %collective-permute-start.3 = (bf16[256,512]{1,0:T(8,128)(2,1)S(1)}, bf16[256,512]{1,0:T(8,128)(2,1)S(1)}, u32[]{:S(2)}, u32[]{:S(2)}) collective-permute-start(bf16[256,512]{1,0:T(8,128)(2,1)S(1)} %bitcast.70), channel_id=1, source_target_pairs={{0,6},{1,265},{2,0},{3,267},{4,2},{5,269},{6,4},{7,271},{8,14},{9,... | collective-permute-start | bytes 786440 | tf_op jit(solution)/shard_map/ppermute | solution.py:389
  53.7 1.9 %collective-permute-start.2 = (bf16[256,512]{1,0:T(8,128)(2,1)S(1)}, bf16[256,512]{1,0:T(8,128)(2,1)S(1)}, u32[]{:S(2)}, u32[]{:S(2)}) collective-permute-start(bf16[256,512]{1,0:T(8,128)(2,1)S(1)} %bitcast.71), channel_id=1, source_target_pairs={{0,2},{1,9},{2,4},{3,11},{4,6},{5,13},{6,0},{7,15},{8,10},{9,257},... | collective-permute-start | bytes 786440 | tf_op jit(solution)/shard_map/ppermute | solution.py:389
  55.7 3.5 %collective-permute-start.1 = (bf16[256,512]{1,0:T(8,128)(2,1)S(1)}, bf16[256,512]{1,0:T(8,128)(2,1)S(1)}, u32[]{:S(2)}, u32[]{:S(2)}) collective-permute-start(bf16[256,512]{1,0:T(8,128)(2,1)S(1)} %bitcast.72), channel_id=1, source_target_pairs={{0,4},{1,257},{2,6},{3,259},{4,0},{5,261},{6,2},{7,263},{8,12},{9,... | collective-permute-start | bytes 786440 | tf_op jit(solution)/shard_map/ppermute | solution.py:389
  59.2 0.0 collective-permute-done.3
  59.2 7.8 %collective-permute-done.2 = bf16[256,512]{1,0:T(8,128)(2,1)S(1)} collective-permute-done((bf16[256,512]{1,0:T(8,128)(2,1)S(1)}, bf16[256,512]{1,0:T(8,128)(2,1)S(1)}, u32[]{:S(2)}, u32[]{:S(2)}) %collective-permute-start.2) | collective-permute-done | bytes 262176 | tf_op jit(solution)/shard_map/ppermute | solution.py:389
  67.0 0.0 collective-permute-done.1
  67.0 0.1 pad_maximum_fusion.refs_1_.refs_2_.refs_0_
  67.1 3.1 %collective-permute-start.4 = (bf16[4,256,512]{2,1,0:T(8,128)(2,1)S(1)}, bf16[4,256,512]{2,1,0:T(8,128)(2,1)}, u32[]{:S(2)}, u32[]{:S(2)}) collective-permute-start(bf16[4,256,512]{2,1,0:T(8,128)(2,1)S(1)} %pad_maximum_fusion.refs_1_.refs_2_.refs_0_), channel_id=1, source_target_pairs={{0,8},{1,3},{2,10},{3,5},{4,12},{5,7},{6,14},{7,1},{8,256},{9,11},... | collective-permute-start | bytes 3145736 | tf_op jit(solution)/shard_map/ppermute | solution.py:391
  70.3 3.4 %collective-permute-start.6 = (bf16[4,256,512]{2,1,0:T(8,128)(2,1)S(1)}, bf16[4,256,512]{2,1,0:T(8,128)(2,1)}, u32[]{:S(2)}, u32[]{:S(2)}) collective-permute-start(bf16[4,256,512]{2,1,0:T(8,128)(2,1)S(1)} %pad_maximum_fusion.refs_1_.refs_2_.refs_0_), channel_id=1, source_target_pairs={{0,264},{1,7},{2,266},{3,1},{4,268},{5,3},{6,270},{7,5},{8,0},{9,1... | collective-permute-start | bytes 3145736 | tf_op jit(solution)/shard_map/ppermute | solution.py:391
  73.7 3.4 %collective-permute-start.5 = (bf16[4,256,512]{2,1,0:T(8,128)(2,1)S(1)}, bf16[4,256,512]{2,1,0:T(8,128)(2,1)}, u32[]{:S(2)}, u32[]{:S(2)}) collective-permute-start(bf16[4,256,512]{2,1,0:T(8,128)(2,1)S(1)} %pad_maximum_fusion.refs_1_.refs_2_.refs_0_), channel_id=1, source_target_pairs={{0,256},{1,5},{2,258},{3,7},{4,260},{5,1},{6,262},{7,3},{8,264},{9... | collective-permute-start | bytes 3145736 | tf_op jit(solution)/shard_map/ppermute | solution.py:391
  77.1 0.0 all-to-all-done.1
  77.1 6.0 %all-to-all-start.2 = ((bf16[16,16,1024]{2,1,0:T(8,128)(2,1)}), bf16[16,16,1024]{2,1,0:T(8,128)(2,1)S(1)}, u32[]{:S(2)}, u32[]{:S(2)}) async-start(bf16[16,16,1024]{2,1,0:T(8,128)(2,1)} %bitcast.15), calls=%async_computation.2 | async-start | bytes 1048576 | tf_op jit(solution)/shard_map/all_to_all | solution.py:341
  83.1 2.0 %collective-permute-start.7 = (bf16[4,256,512]{2,1,0:T(8,128)(2,1)S(1)}, bf16[4,256,512]{2,1,0:T(8,128)(2,1)}, u32[]{:S(2)}, u32[]{:S(2)}) collective-permute-start(bf16[4,256,512]{2,1,0:T(8,128)(2,1)S(1)} %pad_maximum_fusion.refs_1_.refs_2_.refs_0_), channel_id=1, source_target_pairs={{0,1},{1,0},{2,3},{3,2},{4,5},{5,4},{6,7},{7,6},{8,9},{9,8},{10,11... | collective-permute-start | bytes 3145736 | tf_op jit(solution)/shard_map/ppermute | solution.py:345
  85.1 2.3 %collective-permute-start.8 = (bf16[4,256,512]{2,1,0:T(8,128)(2,1)}, bf16[4,256,512]{2,1,0:T(8,128)(2,1)}, u32[]{:S(2)}, u32[]{:S(2)}) collective-permute-start(bf16[4,256,512]{2,1,0:T(8,128)(2,1)} %collective-permute-done.4.refs_2_.refs_3_.refs_1_), channel_id=1, source_target_pairs={{0,1},{1,0},{2,3},{3,2},{4,5},{5,4},{6,7},{7,6},{8,9},{9,8},{10,11... | collective-permute-start | bytes 3145736 | tf_op jit(solution)/shard_map/ppermute | solution.py:345
  87.5 3.5 %collective-permute-done.6.refs_4_.refs_5_.refs_3_ = bf16[4,256,512]{2,1,0:T(8,128)(2,1)} collective-permute-done((bf16[4,256,512]{2,1,0:T(8,128)(2,1)S(1)}, bf16[4,256,512]{2,1,0:T(8,128)(2,1)}, u32[]{:S(2)}, u32[]{:S(2)}) %collective-permute-start.6) | collective-permute-done | bytes 1048608 | tf_op jit(solution)/shard_map/ppermute | solution.py:391
  90.9 1.9 %collective-permute-start.10 = (bf16[4,256,512]{2,1,0:T(8,128)(2,1)}, bf16[4,256,512]{2,1,0:T(8,128)(2,1)}, u32[]{:S(2)}, u32[]{:S(2)}) collective-permute-start(bf16[4,256,512]{2,1,0:T(8,128)(2,1)} %collective-permute-done.6.refs_4_.refs_5_.refs_3_), channel_id=1, source_target_pairs={{0,1},{1,0},{2,3},{3,2},{4,5},{5,4},{6,7},{7,6},{8,9},{9,8},{10,11... | collective-permute-start | bytes 3145736 | tf_op jit(solution)/shard_map/ppermute | solution.py:345
  92.9 6.5 %collective-permute-done.5.refs_3_.refs_4_.refs_2_ = bf16[4,256,512]{2,1,0:T(8,128)(2,1)} collective-permute-done((bf16[4,256,512]{2,1,0:T(8,128)(2,1)S(1)}, bf16[4,256,512]{2,1,0:T(8,128)(2,1)}, u32[]{:S(2)}, u32[]{:S(2)}) %collective-permute-start.5) | collective-permute-done | bytes 1048608 | tf_op jit(solution)/shard_map/ppermute | solution.py:391
  99.3 3.7 %all-to-all-done.2 = bf16[16,16,1024]{2,1,0:T(8,128)(2,1)S(1)} async-done(((bf16[16,16,1024]{2,1,0:T(8,128)(2,1)}), bf16[16,16,1024]{2,1,0:T(8,128)(2,1)S(1)}, u32[]{:S(2)}, u32[]{:S(2)}) %all-to-all-start.2) | async-done | bytes 524320 | tf_op jit(solution)/shard_map/all_to_all | solution.py:341
  103.0 2.3 %collective-permute-start.9 = (bf16[4,256,512]{2,1,0:T(8,128)(2,1)}, bf16[4,256,512]{2,1,0:T(8,128)(2,1)}, u32[]{:S(2)}, u32[]{:S(2)}) collective-permute-start(bf16[4,256,512]{2,1,0:T(8,128)(2,1)} %collective-permute-done.5.refs_3_.refs_4_.refs_2_), channel_id=1, source_target_pairs={{0,1},{1,0},{2,3},{3,2},{4,5},{5,4},{6,7},{7,6},{8,9},{9,8},{10,11... | collective-permute-start | bytes 3145736 | tf_op jit(solution)/shard_map/ppermute | solution.py:345
  105.4 0.7 concatenate.12.scalar_ref
  106.1 1.8 %collective-permute-done.9.refs_7_.refs_8_.refs_6_ = bf16[4,256,512]{2,1,0:T(8,128)(2,1)} collective-permute-done((bf16[4,256,512]{2,1,0:T(8,128)(2,1)}, bf16[4,256,512]{2,1,0:T(8,128)(2,1)}, u32[]{:S(2)}, u32[]{:S(2)}) %collective-permute-start.9) | collective-permute-done | bytes 1048608 | tf_op jit(solution)/shard_map/ppermute | solution.py:345
  107.9 14.8 %attend_2_3.1 = (bf16[256,1024]{1,0:T(8,128)(2,1)}, bf16[256,1024]{1,0:T(8,128)(2,1)}) custom-call(s32[13]{0:T(128)} %concatenate.12.scalar_ref, bf16[256,1024]{1,0:T(8,128)(2,1)} %bitcast.68, bf16[256,1024]{1,0:T(8,128)(2,1)} %bitcast.69, bf16[4,256,512]{2,1,0:T(8,128)(2,1)} %copy-done.6, ...), custom_call_target="tpu_custom_call" | custom-call | flops 1000 | bytes 1000 | tf_op jit(solution)/shard_map/attend_2_3/pallas_call | solution.py:219
  122.8 0.8 bitcast_dynamic-update-slice_fusion
  123.5 1.1 fusion.7
  124.6 13.8 %all-to-all-start.3 = ((bf16[32,8,1024]{2,1,0:T(8,128)(2,1)}), bf16[32,8,1024]{2,1,0:T(8,128)(2,1)S(1)}, u32[]{:S(2)}, u32[]{:S(2)}) async-start(bf16[32,8,1024]{2,1,0:T(8,128)(2,1)} %bitcast.74), calls=%async_computation.3 | async-start | bytes 1048576 | tf_op jit(solution)/shard_map/all_to_all | solution.py:341
  138.4 2.2 %collective-permute-start.11 = (bf16[64,1024]{1,0:T(8,128)(2,1)S(1)}, bf16[64,1024]{1,0:T(8,128)(2,1)S(1)}, u32[]{:S(2)}, u32[]{:S(2)}) collective-permute-start(bf16[64,1024]{1,0:T(8,128)(2,1)S(1)} %get-tuple-element.27), channel_id=1, source_target_pairs={{0,2},{1,3},{2,4},{3,5},{4,6},{5,7},{6,0},{7,1},{8,10},{9,11},{10,... | collective-permute-start | bytes 393224 | tf_op jit(solution)/shard_map/ppermute | solution.py:410
  140.7 5.1 %collective-permute-start.12 = (bf16[64,1024]{1,0:T(8,128)(2,1)S(1)}, bf16[64,1024]{1,0:T(8,128)(2,1)S(1)}, u32[]{:S(2)}, u32[]{:S(2)}) collective-permute-start(bf16[64,1024]{1,0:T(8,128)(2,1)S(1)} %get-tuple-element.26), channel_id=1, source_target_pairs={{0,4},{1,5},{2,6},{3,7},{4,0},{5,1},{6,2},{7,3},{8,12},{9,13},{10,... | collective-permute-start | bytes 393224 | tf_op jit(solution)/shard_map/ppermute | solution.py:410
  145.8 2.1 %collective-permute-start.13 = (bf16[64,1024]{1,0:T(8,128)(2,1)S(1)}, bf16[64,1024]{1,0:T(8,128)(2,1)S(1)}, u32[]{:S(2)}, u32[]{:S(2)}) collective-permute-start(bf16[64,1024]{1,0:T(8,128)(2,1)S(1)} %get-tuple-element.25), channel_id=1, source_target_pairs={{0,6},{1,7},{2,0},{3,1},{4,2},{5,3},{6,4},{7,5},{8,14},{9,15},{10,... | collective-permute-start | bytes 393224 | tf_op jit(solution)/shard_map/ppermute | solution.py:410
  147.9 11.2 %attend_1.1.x_ref = bf16[256,1024]{1,0:T(8,128)(2,1)} custom-call(s32[13]{0:T(128)} %concatenate.12.scalar_ref, bf16[256,1024]{1,0:T(8,128)(2,1)} %norm.1.refs_0_, bf16[4,256,512]{2,1,0:T(8,128)(2,1)} %copy-done.6, bf16[4,256,512]{2,1,0:T(8,128)(2,1)} %collective-permute-done.4.refs_2_.refs_3_.refs_1_, ...), custom_call_target="tpu_custom_call" | custom-call | flops 10000000000 | bytes 1000 | tf_op jit(solution)/shard_map/attend_1/pallas_call | solution.py:219
  159.1 0.8 slice_bitcast_fusion.12
  159.9 0.0 collective-permute-done.13
  159.9 0.0 collective-permute-done.12
  159.9 0.0 collective-permute-done.11
  160.0 3.3 %collective-permute-start.14 = (bf16[4,16,1024]{2,1,0:T(8,128)(2,1)S(1)}, bf16[4,16,1024]{2,1,0:T(8,128)(2,1)S(1)}, u32[]{:S(2)}, u32[]{:S(2)}) collective-permute-start(bf16[4,16,1024]{2,1,0:T(8,128)(2,1)S(1)} %pad_maximum_fusion.2), channel_id=1, source_target_pairs={{0,1},{1,0},{2,3},{3,2},{4,5},{5,4},{6,7},{7,6},{8,9},{9,8},{10,11... | collective-permute-start | bytes 393224 | tf_op jit(solution)/shard_map/ppermute | solution.py:345
  163.3 1.9 %collective-permute-start.16 = (bf16[4,16,1024]{2,1,0:T(8,128)(2,1)S(1)}, bf16[4,16,1024]{2,1,0:T(8,128)(2,1)S(1)}, u32[]{:S(2)}, u32[]{:S(2)}) collective-permute-start(bf16[4,16,1024]{2,1,0:T(8,128)(2,1)S(1)} %pad_maximum_fusion.3), channel_id=1, source_target_pairs={{0,1},{1,0},{2,3},{3,2},{4,5},{5,4},{6,7},{7,6},{8,9},{9,8},{10,11... | collective-permute-start | bytes 393224 | tf_op jit(solution)/shard_map/ppermute | solution.py:345
  165.3 0.0 collective-permute-done.14
  165.3 2.3 %collective-permute-start.15 = (bf16[8,16,1024]{2,1,0:T(8,128)(2,1)S(1)}, bf16[8,16,1024]{2,1,0:T(8,128)(2,1)S(1)}, u32[]{:S(2)}, u32[]{:S(2)}) collective-permute-start(bf16[8,16,1024]{2,1,0:T(8,128)(2,1)S(1)} %constant_dynamic-update-slice_fusion), channel_id=1, source_target_pairs={{0,8},{8,0},{1,9},{9,1},{2,10},{10,2},{3,11},{11,3},{4,12},{12,4},... | collective-permute-start | bytes 786440 | tf_op jit(solution)/shard_map/ppermute | solution.py:345
  167.7 4.3 %gather_out.1.w_ref = bf16[1024,1024]{1,0:T(8,128)(2,1)} custom-call(s32[13]{0:T(128)} %concatenate.12.scalar_ref, bf16[4,256,512]{2,1,0:T(8,128)(2,1)} %copy-done.6, bf16[4,256,512]{2,1,0:T(8,128)(2,1)} %collective-permute-done.4.refs_2_.refs_3_.refs_1_, bf16[4,256,512]{2,1,0:T(8,128)(2,1)} %collective-permute-done.5.refs_3_.refs_4_.refs_2_, ...), custom_call_target="tpu_custom_call" | custom-call | flops 3000000000 | bytes 1000 | tf_op jit(solution)/shard_map/gather_out/pallas_call | solution.py:264
  172.0 1.6 copy-done.2
  173.6 1.0 mix_0.1.refs_0_
  174.6 0.1 collective-permute-done.15.parts_ref
  174.7 1.0 mix_1.1
  175.8 1.0 reshape.51
  (45 shorter events, 0.3 us)
Async XLA Ops:
  0.0 20.3 %copy-start.9 = (f32[16,127]{1,0:T(8,128)S(1)}, f32[16,127]{1,0:T(8,128)}, u32[]{:S(2)}) copy-start(f32[16,127]{1,0:T(8,128)} %param.10) | copy-start | bytes 24388
  0.0 21.8 %copy-start.10 = (f32[16,63]{1,0:T(8,128)S(1)}, f32[16,63]{1,0:T(8,128)}, u32[]{:S(2)}) copy-start(f32[16,63]{1,0:T(8,128)} %param.11) | copy-start | bytes 12100
  2.2 28.9 %all-to-all-start = ((bf16[16,16,512]{2,1,0:T(8,128)(2,1)}), bf16[16,16,512]{2,1,0:T(8,128)(2,1)S(1)}, u32[]{:S(2)}, u32[]{:S(2)}) async-start(bf16[16,16,512]{2,1,0:T(8,128)(2,1)} %broadcast_in_dim.2), calls=%async_computation | async-start | bytes 524288 | tf_op jit(solution)/shard_map/all_to_all | solution.py:341
  18.0 5.2 %copy-start.11 = (f32[16,63]{1,0:T(8,128)S(1)}, f32[16,63]{1,0:T(8,128)}, u32[]{:S(2)}) copy-start(f32[16,63]{1,0:T(8,128)} %param.12) | copy-start | bytes 12100
  20.8 1.0 copy-start.4
  22.2 1.0 copy-start
  23.6 1.0 copy-start.1
  31.1 46.0 %all-to-all-start.1 = ((bf16[32,8,1024]{2,1,0:T(8,128)(2,1)}), bf16[32,8,1024]{2,1,0:T(8,128)(2,1)S(1)}, u32[]{:S(2)}, u32[]{:S(2)}) async-start(bf16[32,8,1024]{2,1,0:T(8,128)(2,1)} %bitcast.13), calls=%async_computation.1 | async-start | bytes 1048576 | tf_op jit(solution)/shard_map/all_to_all | solution.py:341
  45.0 60.4 %copy-start.12 = (s32[4]{0:T(128)S(1)}, s32[4]{0:T(128)}, u32[]{:S(2)}) copy-start(s32[4]{0:T(128)} %constant.81) | copy-start | bytes 52
  45.0 3.9 %collective-permute-start = (bf16[128,512]{1,0:T(8,128)(2,1)S(1)}, bf16[128,512]{1,0:T(8,128)(2,1)S(1)}, u32[]{:S(2)}, u32[]{:S(2)}) collective-permute-start(bf16[128,512]{1,0:T(8,128)(2,1)S(1)} %broadcast_select_fusion.2), channel_id=1, source_target_pairs={{0,1},{1,0},{2,3},{3,2},{4,5},{5,4},{6,7},{7,6},{8,9},{9,8},{10,11... | collective-permute-start | bytes 393224 | tf_op jit(solution)/shard_map/ppermute | solution.py:345
  49.0 10.2 %collective-permute-start.3 = (bf16[256,512]{1,0:T(8,128)(2,1)S(1)}, bf16[256,512]{1,0:T(8,128)(2,1)S(1)}, u32[]{:S(2)}, u32[]{:S(2)}) collective-permute-start(bf16[256,512]{1,0:T(8,128)(2,1)S(1)} %bitcast.70), channel_id=1, source_target_pairs={{0,6},{1,265},{2,0},{3,267},{4,2},{5,269},{6,4},{7,271},{8,14},{9,... | collective-permute-start | bytes 786440 | tf_op jit(solution)/shard_map/ppermute | solution.py:389
  53.7 13.3 %collective-permute-start.2 = (bf16[256,512]{1,0:T(8,128)(2,1)S(1)}, bf16[256,512]{1,0:T(8,128)(2,1)S(1)}, u32[]{:S(2)}, u32[]{:S(2)}) collective-permute-start(bf16[256,512]{1,0:T(8,128)(2,1)S(1)} %bitcast.71), channel_id=1, source_target_pairs={{0,2},{1,9},{2,4},{3,11},{4,6},{5,13},{6,0},{7,15},{8,10},{9,257},... | collective-permute-start | bytes 786440 | tf_op jit(solution)/shard_map/ppermute | solution.py:389
  55.7 11.3 %collective-permute-start.1 = (bf16[256,512]{1,0:T(8,128)(2,1)S(1)}, bf16[256,512]{1,0:T(8,128)(2,1)S(1)}, u32[]{:S(2)}, u32[]{:S(2)}) collective-permute-start(bf16[256,512]{1,0:T(8,128)(2,1)S(1)} %bitcast.72), channel_id=1, source_target_pairs={{0,4},{1,257},{2,6},{3,259},{4,0},{5,261},{6,2},{7,263},{8,12},{9,... | collective-permute-start | bytes 786440 | tf_op jit(solution)/shard_map/ppermute | solution.py:389
  67.1 40.8 %copy-start.6 = (bf16[4,256,512]{2,1,0:T(8,128)(2,1)}, bf16[4,256,512]{2,1,0:T(8,128)(2,1)S(1)}, u32[]{:S(2)}) copy-start(bf16[4,256,512]{2,1,0:T(8,128)(2,1)S(1)} %pad_maximum_fusion.refs_1_.refs_2_.refs_0_) | copy-start | bytes 3145732
  67.1 18.0 %collective-permute-start.4 = (bf16[4,256,512]{2,1,0:T(8,128)(2,1)S(1)}, bf16[4,256,512]{2,1,0:T(8,128)(2,1)}, u32[]{:S(2)}, u32[]{:S(2)}) collective-permute-start(bf16[4,256,512]{2,1,0:T(8,128)(2,1)S(1)} %pad_maximum_fusion.refs_1_.refs_2_.refs_0_), channel_id=1, source_target_pairs={{0,8},{1,3},{2,10},{3,5},{4,12},{5,7},{6,14},{7,1},{8,256},{9,11},... | collective-permute-start | bytes 3145736 | tf_op jit(solution)/shard_map/ppermute | solution.py:391
  70.3 20.7 %collective-permute-start.6 = (bf16[4,256,512]{2,1,0:T(8,128)(2,1)S(1)}, bf16[4,256,512]{2,1,0:T(8,128)(2,1)}, u32[]{:S(2)}, u32[]{:S(2)}) collective-permute-start(bf16[4,256,512]{2,1,0:T(8,128)(2,1)S(1)} %pad_maximum_fusion.refs_1_.refs_2_.refs_0_), channel_id=1, source_target_pairs={{0,264},{1,7},{2,266},{3,1},{4,268},{5,3},{6,270},{7,5},{8,0},{9,1... | collective-permute-start | bytes 3145736 | tf_op jit(solution)/shard_map/ppermute | solution.py:391
  73.7 25.7 %collective-permute-start.5 = (bf16[4,256,512]{2,1,0:T(8,128)(2,1)S(1)}, bf16[4,256,512]{2,1,0:T(8,128)(2,1)}, u32[]{:S(2)}, u32[]{:S(2)}) collective-permute-start(bf16[4,256,512]{2,1,0:T(8,128)(2,1)S(1)} %pad_maximum_fusion.refs_1_.refs_2_.refs_0_), channel_id=1, source_target_pairs={{0,256},{1,5},{2,258},{3,7},{4,260},{5,1},{6,262},{7,3},{8,264},{9... | collective-permute-start | bytes 3145736 | tf_op jit(solution)/shard_map/ppermute | solution.py:391
  77.1 30.8 %copy-start.7 = (bf16[32,8,1024]{2,1,0:T(8,128)(2,1)}, bf16[32,8,1024]{2,1,0:T(8,128)(2,1)S(1)}, u32[]{:S(2)}) copy-start(bf16[32,8,1024]{2,1,0:T(8,128)(2,1)S(1)} %all-to-all-done.1) | copy-start | bytes 1572868
  77.1 25.9 %all-to-all-start.2 = ((bf16[16,16,1024]{2,1,0:T(8,128)(2,1)}), bf16[16,16,1024]{2,1,0:T(8,128)(2,1)S(1)}, u32[]{:S(2)}, u32[]{:S(2)}) async-start(bf16[16,16,1024]{2,1,0:T(8,128)(2,1)} %bitcast.15), calls=%async_computation.2 | async-start | bytes 1048576 | tf_op jit(solution)/shard_map/all_to_all | solution.py:341
  83.1 23.0 %collective-permute-start.7 = (bf16[4,256,512]{2,1,0:T(8,128)(2,1)S(1)}, bf16[4,256,512]{2,1,0:T(8,128)(2,1)}, u32[]{:S(2)}, u32[]{:S(2)}) collective-permute-start(bf16[4,256,512]{2,1,0:T(8,128)(2,1)S(1)} %pad_maximum_fusion.refs_1_.refs_2_.refs_0_), channel_id=1, source_target_pairs={{0,1},{1,0},{2,3},{3,2},{4,5},{5,4},{6,7},{7,6},{8,9},{9,8},{10,11... | collective-permute-start | bytes 3145736 | tf_op jit(solution)/shard_map/ppermute | solution.py:345
  85.1 20.9 %collective-permute-start.8 = (bf16[4,256,512]{2,1,0:T(8,128)(2,1)}, bf16[4,256,512]{2,1,0:T(8,128)(2,1)}, u32[]{:S(2)}, u32[]{:S(2)}) collective-permute-start(bf16[4,256,512]{2,1,0:T(8,128)(2,1)} %collective-permute-done.4.refs_2_.refs_3_.refs_1_), channel_id=1, source_target_pairs={{0,1},{1,0},{2,3},{3,2},{4,5},{5,4},{6,7},{7,6},{8,9},{9,8},{10,11... | collective-permute-start | bytes 3145736 | tf_op jit(solution)/shard_map/ppermute | solution.py:345
  90.9 15.1 %collective-permute-start.10 = (bf16[4,256,512]{2,1,0:T(8,128)(2,1)}, bf16[4,256,512]{2,1,0:T(8,128)(2,1)}, u32[]{:S(2)}, u32[]{:S(2)}) collective-permute-start(bf16[4,256,512]{2,1,0:T(8,128)(2,1)} %collective-permute-done.6.refs_4_.refs_5_.refs_3_), channel_id=1, source_target_pairs={{0,1},{1,0},{2,3},{3,2},{4,5},{5,4},{6,7},{7,6},{8,9},{9,8},{10,11... | collective-permute-start | bytes 3145736 | tf_op jit(solution)/shard_map/ppermute | solution.py:345
  103.0 4.9 %copy-start.8 = (bf16[16,16,1024]{2,1,0:T(8,128)(2,1)}, bf16[16,16,1024]{2,1,0:T(8,128)(2,1)S(1)}, u32[]{:S(2)}) copy-start(bf16[16,16,1024]{2,1,0:T(8,128)(2,1)S(1)} %all-to-all-done.2) | copy-start | bytes 1572868
  103.0 4.9 %collective-permute-start.9 = (bf16[4,256,512]{2,1,0:T(8,128)(2,1)}, bf16[4,256,512]{2,1,0:T(8,128)(2,1)}, u32[]{:S(2)}, u32[]{:S(2)}) collective-permute-start(bf16[4,256,512]{2,1,0:T(8,128)(2,1)} %collective-permute-done.5.refs_3_.refs_4_.refs_2_), channel_id=1, source_target_pairs={{0,1},{1,0},{2,3},{3,2},{4,5},{5,4},{6,7},{7,6},{8,9},{9,8},{10,11... | collective-permute-start | bytes 3145736 | tf_op jit(solution)/shard_map/ppermute | solution.py:345
  124.6 47.4 %all-to-all-start.3 = ((bf16[32,8,1024]{2,1,0:T(8,128)(2,1)}), bf16[32,8,1024]{2,1,0:T(8,128)(2,1)S(1)}, u32[]{:S(2)}, u32[]{:S(2)}) async-start(bf16[32,8,1024]{2,1,0:T(8,128)(2,1)} %bitcast.74), calls=%async_computation.3 | async-start | bytes 1048576 | tf_op jit(solution)/shard_map/all_to_all | solution.py:341
  138.4 21.5 %collective-permute-start.11 = (bf16[64,1024]{1,0:T(8,128)(2,1)S(1)}, bf16[64,1024]{1,0:T(8,128)(2,1)S(1)}, u32[]{:S(2)}, u32[]{:S(2)}) collective-permute-start(bf16[64,1024]{1,0:T(8,128)(2,1)S(1)} %get-tuple-element.27), channel_id=1, source_target_pairs={{0,2},{1,3},{2,4},{3,5},{4,6},{5,7},{6,0},{7,1},{8,10},{9,11},{10,... | collective-permute-start | bytes 393224 | tf_op jit(solution)/shard_map/ppermute | solution.py:410
  140.7 19.2 %collective-permute-start.12 = (bf16[64,1024]{1,0:T(8,128)(2,1)S(1)}, bf16[64,1024]{1,0:T(8,128)(2,1)S(1)}, u32[]{:S(2)}, u32[]{:S(2)}) collective-permute-start(bf16[64,1024]{1,0:T(8,128)(2,1)S(1)} %get-tuple-element.26), channel_id=1, source_target_pairs={{0,4},{1,5},{2,6},{3,7},{4,0},{5,1},{6,2},{7,3},{8,12},{9,13},{10,... | collective-permute-start | bytes 393224 | tf_op jit(solution)/shard_map/ppermute | solution.py:410
  145.8 14.1 %collective-permute-start.13 = (bf16[64,1024]{1,0:T(8,128)(2,1)S(1)}, bf16[64,1024]{1,0:T(8,128)(2,1)S(1)}, u32[]{:S(2)}, u32[]{:S(2)}) collective-permute-start(bf16[64,1024]{1,0:T(8,128)(2,1)S(1)} %get-tuple-element.25), channel_id=1, source_target_pairs={{0,6},{1,7},{2,0},{3,1},{4,2},{5,3},{6,4},{7,5},{8,14},{9,15},{10,... | collective-permute-start | bytes 393224 | tf_op jit(solution)/shard_map/ppermute | solution.py:410
  160.0 5.3 %collective-permute-start.14 = (bf16[4,16,1024]{2,1,0:T(8,128)(2,1)S(1)}, bf16[4,16,1024]{2,1,0:T(8,128)(2,1)S(1)}, u32[]{:S(2)}, u32[]{:S(2)}) collective-permute-start(bf16[4,16,1024]{2,1,0:T(8,128)(2,1)S(1)} %pad_maximum_fusion.2), channel_id=1, source_target_pairs={{0,1},{1,0},{2,3},{3,2},{4,5},{5,4},{6,7},{7,6},{8,9},{9,8},{10,11... | collective-permute-start | bytes 393224 | tf_op jit(solution)/shard_map/ppermute | solution.py:345
  163.3 8.7 %collective-permute-start.16 = (bf16[4,16,1024]{2,1,0:T(8,128)(2,1)S(1)}, bf16[4,16,1024]{2,1,0:T(8,128)(2,1)S(1)}, u32[]{:S(2)}, u32[]{:S(2)}) collective-permute-start(bf16[4,16,1024]{2,1,0:T(8,128)(2,1)S(1)} %pad_maximum_fusion.3), channel_id=1, source_target_pairs={{0,1},{1,0},{2,3},{3,2},{4,5},{5,4},{6,7},{7,6},{8,9},{9,8},{10,11... | collective-permute-start | bytes 393224 | tf_op jit(solution)/shard_map/ppermute | solution.py:345
  165.3 6.7 %copy-start.3 = (bf16[256,1024]{1,0:T(8,128)(2,1)S(1)}, bf16[256,1024]{1,0:T(8,128)(2,1)}, u32[]{:S(2)}) copy-start(bf16[256,1024]{1,0:T(8,128)(2,1)} %attend_1.1.x_ref) | copy-start | bytes 1572868
  165.3 6.7 %copy-start.5 = (s32[13]{0:T(128)S(1)}, s32[13]{0:T(128)}, u32[]{:S(2)}) copy-start(s32[13]{0:T(128)} %concatenate.12.scalar_ref) | copy-start | bytes 160
  165.3 9.4 %collective-permute-start.15 = (bf16[8,16,1024]{2,1,0:T(8,128)(2,1)S(1)}, bf16[8,16,1024]{2,1,0:T(8,128)(2,1)S(1)}, u32[]{:S(2)}, u32[]{:S(2)}) collective-permute-start(bf16[8,16,1024]{2,1,0:T(8,128)(2,1)S(1)} %constant_dynamic-update-slice_fusion), channel_id=1, source_target_pairs={{0,8},{8,0},{1,9},{9,1},{2,10},{10,2},{3,11},{11,3},{4,12},{12,4},... | collective-permute-start | bytes 786440 | tf_op jit(solution)/shard_map/ppermute | solution.py:345
  172.0 1.6 copy-start.2

commit v7 on v6

--- a/solution.py
+++ b/solution.py
@@ -92,9 +92,10 @@
     token_refs, refs = refs[:count], refs[count:]
     weight_refs, refs = refs[:8], refs[8:]
     bias_refs = refs[: 2 * count]
-    refs = refs[-(count * 2 + 3) :]
-    out_refs, back_refs = refs[:count], refs[count : 2 * count]
-    lines_ref, qkv_ref, mixed_ref = refs[2 * count :]
+    outs = sum(4 if axis == 3 else 1 for axis in axes)
+    refs = refs[-(outs + count + 3) :]
+    out_refs, back_refs = refs[:outs], refs[outs : outs + count]
+    lines_ref, qkv_ref, mixed_ref = refs[outs + count :]
     step = pl.program_id(0)
     rows = token_refs[0].shape[0]
     core, turned_a, turned_b, yl, x = [scalar_ref[8 + n] for n in range(5)]
@@ -187,7 +188,11 @@
         for a in range(count):
             mixed = mixed_ref[a * rows : (a + 1) * rows]
             out = jnp.dot(back_refs[a][...], mixed, preferred_element_type=F32)
-            out_refs[a][...] = out.astype(BF)
+            if axes[a] == 3:
+                for k in range(4):
+                    out_refs[a + k][...] = out[k * (rows // 4) : (k + 1) * (rows // 4)].astype(BF)
+            else:
+                out_refs[a][...] = out.astype(BF)
 
 
 def attend(axes, tokens, weights, biases, scalars, after=()):
@@ -215,15 +220,16 @@
 
             specs.append(pl.BlockSpec((1, BLOCK, 2 * BLOCK), pair))
     specs.extend([pl.BlockSpec(memory_space=pl.ANY)] * len(after))
+    heights = [n for axis in axes for n in ([rows // 4] * 4 if axis == 3 else [rows])]
     bias_args = [b for bias in biases for b in (bias, bias)]
     return pl.pallas_call(
         functools.partial(attend_kernel, axes),
-        out_shape=[jax.ShapeDtypeStruct((rows, HEADS * HEAD), BF)] * count,
+        out_shape=[jax.ShapeDtypeStruct((n, features), BF) for n in heights],
         grid_spec=pltpu.PrefetchScalarGridSpec(
             num_scalar_prefetch=1,
             grid=(5,),
             in_specs=specs,
-            out_specs=[pl.BlockSpec((rows, features), lambda s, p: (0, 0))] * count,
+            out_specs=[pl.BlockSpec((n, features), lambda s, p: (0, 0)) for n in heights],
             scratch_shapes=[pltpu.VMEM((rows, rows), BF)] * count
             + [
                 pltpu.VMEM((count * rows, features), BF),
@@ -402,11 +408,10 @@
     ).astype(jnp.int32)
 
     every = (*second, *others)
-    along_y, z = attend((2, 3), (y_lines, z_lines), every, (blocks_y, blocks_z), scalars)
+    along_y, *z = attend((2, 3), (y_lines, z_lines), every, (blocks_y, blocks_z), scalars)
     along_y = exchange(along_y.reshape(peers, -1, features), GY).reshape(rows, features)
 
-    made = z
-    z = z.reshape(4, rows // 4, features)
+    made = z[0]
     back = [z[0]] + [lax.ppermute(z[k], ALL, hop_x(k)) for k in range(1, 4)]
     (along_x,) = attend((1,), (normed,), every, (blocks_x,), scalars)
     w_whole = gather_out(scalars, every, made)

time: 178 us -> 177 us (level)
  local copies, waits for them, and re-layouts: 12.6 us -> 10.7 us
    unnamed x30 -> x32, local copies, waits for them, and re-layouts: 5.36 us -> 5.36 us
where the time goes in v7:
time: 177 us; the launch traced here: 175 us
  starting transfers between devices  98.1 us (55%)
  Pallas kernels  34.5 us (19%)
  waiting for transfers between devices  30.9 us (17%)
  local copies, waits for them, and re-layouts  10.7 us (6%)
    all_to_all x4, starting transfers between devices, exchange(): return lax.all_to_all(array, axes, split_axis=0, concat_axis=0, tiled=True)  49.4 us
    pallas_call x2, Pallas kernels, attend(): pl.pallas_call(functools.partial(attend_kernel, axes), out_shape=[jax.Sha...  26 us
    ppermute x8, starting transfers between devices, swap(): return lax.ppermute(array, axis, [(0, 1), (1, 0)])  19 us
    all_to_all x4, waiting for transfers between devices, exchange(): return lax.all_to_all(array, axes, split_axis=0, concat_axis=0, tiled=True)  10.2 us
    ppermute x3, starting transfers between devices, shards(): lax.ppermute(piece, ALL, hop_plane(k, 0))  10.2 us
    ppermute x3, waiting for transfers between devices, shards(): lax.ppermute(first, ALL, hop_plane(k, 1))  9.96 us
    ppermute x3, starting transfers between devices, shards(): lax.ppermute(first, ALL, hop_plane(k, 1))  9.94 us
    ppermute x3, starting transfers between devices, shards(): back = [z[0]] + [lax.ppermute(z[k], ALL, hop_x(k)) for k in range(1, 4)]  9.57 us
  transfers between devices with their start and end apart: 21, of which 8 were waited for; matrix products, arithmetic and copies ran while one was open for 2% of the time, Pallas kernels for 11%

profile of v7, /device:TPU:1, one launch (start us, length us, event | category | flops | bytes accessed | tf_op | source)
XLA Modules:
  0.0 175.1 jit_solution(12587250244395168594)
XLA Ops:
  0.0 0.7 dynamic_slice.15
  0.7 0.7 fusion.7
  1.4 0.8 broadcast_in_dim.2
  2.2 15.7 %all-to-all-start = ((bf16[16,16,512]{2,1,0:T(8,128)(2,1)}), bf16[16,16,512]{2,1,0:T(8,128)(2,1)S(1)}, u32[]{:S(2)}, u32[]{:S(2)}) async-start(bf16[16,16,512]{2,1,0:T(8,128)(2,1)} %broadcast_in_dim.2), calls=%async_computation | async-start | bytes 524288 | tf_op jit(solution)/shard_map/all_to_all | solution.py:347
  18.0 0.0 copy-start.12
  18.0 1.2 reshape.31.tokens_ref
  19.2 1.1 norm.1.refs_0_
  20.3 0.1 rev.9
  20.4 0.3 bias_64.1.refs_9_.refs_10_
  20.8 1.0 copy-done.4
  21.8 0.1 rev.10
  21.8 0.3 bias_32.2.refs_10_.refs_11_
  22.2 1.0 copy-done
  23.2 0.1 rev.11
  23.3 0.3 bias_32.3.refs_12_.refs_13_
  23.6 1.0 copy-done.1
  24.6 6.5 %all-to-all-done = bf16[16,16,512]{2,1,0:T(8,128)(2,1)S(1)} async-done(((bf16[16,16,512]{2,1,0:T(8,128)(2,1)}), bf16[16,16,512]{2,1,0:T(8,128)(2,1)S(1)}, u32[]{:S(2)}, u32[]{:S(2)}) %all-to-all-start) | async-done | bytes 262176 | tf_op jit(solution)/shard_map/all_to_all | solution.py:347
  31.1 13.9 %all-to-all-start.1 = ((bf16[32,8,1024]{2,1,0:T(8,128)(2,1)}), bf16[32,8,1024]{2,1,0:T(8,128)(2,1)S(1)}, u32[]{:S(2)}, u32[]{:S(2)}) async-start(bf16[32,8,1024]{2,1,0:T(8,128)(2,1)} %bitcast.13), calls=%async_computation.1 | async-start | bytes 1048576 | tf_op jit(solution)/shard_map/all_to_all | solution.py:347
  45.0 0.0 copy-start.13
  45.0 2.9 %collective-permute-start = (bf16[128,512]{1,0:T(8,128)(2,1)S(1)}, bf16[128,512]{1,0:T(8,128)(2,1)S(1)}, u32[]{:S(2)}, u32[]{:S(2)}) collective-permute-start(bf16[128,512]{1,0:T(8,128)(2,1)S(1)} %broadcast_select_fusion.2), channel_id=1, source_target_pairs={{0,1},{1,0},{2,3},{3,2},{4,5},{5,4},{6,7},{7,6},{8,9},{9,8},{10,11... | collective-permute-start | bytes 393224 | tf_op jit(solution)/shard_map/ppermute | solution.py:351
  47.9 1.0 collective-permute-done
  49.0 4.8 %collective-permute-start.3 = (bf16[256,512]{1,0:T(8,128)(2,1)S(1)}, bf16[256,512]{1,0:T(8,128)(2,1)S(1)}, u32[]{:S(2)}, u32[]{:S(2)}) collective-permute-start(bf16[256,512]{1,0:T(8,128)(2,1)S(1)} %bitcast.70), channel_id=1, source_target_pairs={{0,6},{1,265},{2,0},{3,267},{4,2},{5,269},{6,4},{7,271},{8,14},{9,... | collective-permute-start | bytes 786440 | tf_op jit(solution)/shard_map/ppermute | solution.py:395
  53.7 1.9 %collective-permute-start.2 = (bf16[256,512]{1,0:T(8,128)(2,1)S(1)}, bf16[256,512]{1,0:T(8,128)(2,1)S(1)}, u32[]{:S(2)}, u32[]{:S(2)}) collective-permute-start(bf16[256,512]{1,0:T(8,128)(2,1)S(1)} %bitcast.71), channel_id=1, source_target_pairs={{0,2},{1,9},{2,4},{3,11},{4,6},{5,13},{6,0},{7,15},{8,10},{9,257},... | collective-permute-start | bytes 786440 | tf_op jit(solution)/shard_map/ppermute | solution.py:395
  55.7 3.5 %collective-permute-start.1 = (bf16[256,512]{1,0:T(8,128)(2,1)S(1)}, bf16[256,512]{1,0:T(8,128)(2,1)S(1)}, u32[]{:S(2)}, u32[]{:S(2)}) collective-permute-start(bf16[256,512]{1,0:T(8,128)(2,1)S(1)} %bitcast.72), channel_id=1, source_target_pairs={{0,4},{1,257},{2,6},{3,259},{4,0},{5,261},{6,2},{7,263},{8,12},{9,... | collective-permute-start | bytes 786440 | tf_op jit(solution)/shard_map/ppermute | solution.py:395
  59.2 0.0 collective-permute-done.3
  59.2 7.8 %collective-permute-done.2 = bf16[256,512]{1,0:T(8,128)(2,1)S(1)} collective-permute-done((bf16[256,512]{1,0:T(8,128)(2,1)S(1)}, bf16[256,512]{1,0:T(8,128)(2,1)S(1)}, u32[]{:S(2)}, u32[]{:S(2)}) %collective-permute-start.2) | collective-permute-done | bytes 262176 | tf_op jit(solution)/shard_map/ppermute | solution.py:395
  67.0 0.0 collective-permute-done.1
  67.0 0.1 pad_maximum_fusion.refs_1_.refs_2_.refs_0_
  67.1 3.1 %collective-permute-start.4 = (bf16[4,256,512]{2,1,0:T(8,128)(2,1)S(1)}, bf16[4,256,512]{2,1,0:T(8,128)(2,1)}, u32[]{:S(2)}, u32[]{:S(2)}) collective-permute-start(bf16[4,256,512]{2,1,0:T(8,128)(2,1)S(1)} %pad_maximum_fusion.refs_1_.refs_2_.refs_0_), channel_id=1, source_target_pairs={{0,8},{1,3},{2,10},{3,5},{4,12},{5,7},{6,14},{7,1},{8,256},{9,11},... | collective-permute-start | bytes 3145736 | tf_op jit(solution)/shard_map/ppermute | solution.py:397
  70.3 3.4 %collective-permute-start.6 = (bf16[4,256,512]{2,1,0:T(8,128)(2,1)S(1)}, bf16[4,256,512]{2,1,0:T(8,128)(2,1)}, u32[]{:S(2)}, u32[]{:S(2)}) collective-permute-start(bf16[4,256,512]{2,1,0:T(8,128)(2,1)S(1)} %pad_maximum_fusion.refs_1_.refs_2_.refs_0_), channel_id=1, source_target_pairs={{0,264},{1,7},{2,266},{3,1},{4,268},{5,3},{6,270},{7,5},{8,0},{9,1... | collective-permute-start | bytes 3145736 | tf_op jit(solution)/shard_map/ppermute | solution.py:397
  73.7 3.4 %collective-permute-start.5 = (bf16[4,256,512]{2,1,0:T(8,128)(2,1)S(1)}, bf16[4,256,512]{2,1,0:T(8,128)(2,1)}, u32[]{:S(2)}, u32[]{:S(2)}) collective-permute-start(bf16[4,256,512]{2,1,0:T(8,128)(2,1)S(1)} %pad_maximum_fusion.refs_1_.refs_2_.refs_0_), channel_id=1, source_target_pairs={{0,256},{1,5},{2,258},{3,7},{4,260},{5,1},{6,262},{7,3},{8,264},{9... | collective-permute-start | bytes 3145736 | tf_op jit(solution)/shard_map/ppermute | solution.py:397
  77.1 0.0 all-to-all-done.1
  77.1 6.0 %all-to-all-start.2 = ((bf16[16,16,1024]{2,1,0:T(8,128)(2,1)}), bf16[16,16,1024]{2,1,0:T(8,128)(2,1)S(1)}, u32[]{:S(2)}, u32[]{:S(2)}) async-start(bf16[16,16,1024]{2,1,0:T(8,128)(2,1)} %bitcast.15), calls=%async_computation.2 | async-start | bytes 1048576 | tf_op jit(solution)/shard_map/all_to_all | solution.py:347
  83.1 2.0 %collective-permute-start.7 = (bf16[4,256,512]{2,1,0:T(8,128)(2,1)S(1)}, bf16[4,256,512]{2,1,0:T(8,128)(2,1)}, u32[]{:S(2)}, u32[]{:S(2)}) collective-permute-start(bf16[4,256,512]{2,1,0:T(8,128)(2,1)S(1)} %pad_maximum_fusion.refs_1_.refs_2_.refs_0_), channel_id=1, source_target_pairs={{0,1},{1,0},{2,3},{3,2},{4,5},{5,4},{6,7},{7,6},{8,9},{9,8},{10,11... | collective-permute-start | bytes 3145736 | tf_op jit(solution)/shard_map/ppermute | solution.py:351
  85.1 0.0 collective-permute-done.4.refs_2_.refs_3_.refs_1_
  85.1 2.3 %collective-permute-start.8 = (bf16[4,256,512]{2,1,0:T(8,128)(2,1)}, bf16[4,256,512]{2,1,0:T(8,128)(2,1)}, u32[]{:S(2)}, u32[]{:S(2)}) collective-permute-start(bf16[4,256,512]{2,1,0:T(8,128)(2,1)} %collective-permute-done.4.refs_2_.refs_3_.refs_1_), channel_id=1, source_target_pairs={{0,1},{1,0},{2,3},{3,2},{4,5},{5,4},{6,7},{7,6},{8,9},{9,8},{10,11... | collective-permute-start | bytes 3145736 | tf_op jit(solution)/shard_map/ppermute | solution.py:351
  87.5 3.5 %collective-permute-done.6.refs_4_.refs_5_.refs_3_ = bf16[4,256,512]{2,1,0:T(8,128)(2,1)} collective-permute-done((bf16[4,256,512]{2,1,0:T(8,128)(2,1)S(1)}, bf16[4,256,512]{2,1,0:T(8,128)(2,1)}, u32[]{:S(2)}, u32[]{:S(2)}) %collective-permute-start.6) | collective-permute-done | bytes 1048608 | tf_op jit(solution)/shard_map/ppermute | solution.py:397
  90.9 1.9 %collective-permute-start.10 = (bf16[4,256,512]{2,1,0:T(8,128)(2,1)}, bf16[4,256,512]{2,1,0:T(8,128)(2,1)}, u32[]{:S(2)}, u32[]{:S(2)}) collective-permute-start(bf16[4,256,512]{2,1,0:T(8,128)(2,1)} %collective-permute-done.6.refs_4_.refs_5_.refs_3_), channel_id=1, source_target_pairs={{0,1},{1,0},{2,3},{3,2},{4,5},{5,4},{6,7},{7,6},{8,9},{9,8},{10,11... | collective-permute-start | bytes 3145736 | tf_op jit(solution)/shard_map/ppermute | solution.py:351
  92.9 6.5 %collective-permute-done.5.refs_3_.refs_4_.refs_2_ = bf16[4,256,512]{2,1,0:T(8,128)(2,1)} collective-permute-done((bf16[4,256,512]{2,1,0:T(8,128)(2,1)S(1)}, bf16[4,256,512]{2,1,0:T(8,128)(2,1)}, u32[]{:S(2)}, u32[]{:S(2)}) %collective-permute-start.5) | collective-permute-done | bytes 1048608 | tf_op jit(solution)/shard_map/ppermute | solution.py:397
  99.3 3.7 %all-to-all-done.2 = bf16[16,16,1024]{2,1,0:T(8,128)(2,1)S(1)} async-done(((bf16[16,16,1024]{2,1,0:T(8,128)(2,1)}), bf16[16,16,1024]{2,1,0:T(8,128)(2,1)S(1)}, u32[]{:S(2)}, u32[]{:S(2)}) %all-to-all-start.2) | async-done | bytes 524320 | tf_op jit(solution)/shard_map/all_to_all | solution.py:347
  103.0 2.3 %collective-permute-start.9 = (bf16[4,256,512]{2,1,0:T(8,128)(2,1)}, bf16[4,256,512]{2,1,0:T(8,128)(2,1)}, u32[]{:S(2)}, u32[]{:S(2)}) collective-permute-start(bf16[4,256,512]{2,1,0:T(8,128)(2,1)} %collective-permute-done.5.refs_3_.refs_4_.refs_2_), channel_id=1, source_target_pairs={{0,1},{1,0},{2,3},{3,2},{4,5},{5,4},{6,7},{7,6},{8,9},{9,8},{10,11... | collective-permute-start | bytes 3145736 | tf_op jit(solution)/shard_map/ppermute | solution.py:351
  105.4 0.7 concatenate.12.scalar_ref
  106.1 0.0 collective-permute-done.7.refs_5_.refs_6_.refs_4_
  106.1 0.0 collective-permute-done.8.refs_6_.refs_7_.refs_5_
  106.1 0.0 collective-permute-done.10.refs_8_.refs_9_.refs_7_
  106.1 1.8 %collective-permute-done.9.refs_7_.refs_8_.refs_6_ = bf16[4,256,512]{2,1,0:T(8,128)(2,1)} collective-permute-done((bf16[4,256,512]{2,1,0:T(8,128)(2,1)}, bf16[4,256,512]{2,1,0:T(8,128)(2,1)}, u32[]{:S(2)}, u32[]{:S(2)}) %collective-permute-start.9) | collective-permute-done | bytes 1048608 | tf_op jit(solution)/shard_map/ppermute | solution.py:351
  107.9 14.8 %attend_2_3.1 = (bf16[256,1024]{1,0:T(8,128)(2,1)}, bf16[64,1024]{1,0:T(8,128)(2,1)}, bf16[64,1024]{1,0:T(8,128)(2,1)}, bf16[64,1024]{1,0:T(8,128)(2,1)}, bf16[64,1024]{1,0:T(8,128)(2,1)}) custom-call(s32[13]{0:T(128)} %concatenate.12.scalar_ref, bf16[256,1024]{1,0:T(8,128)(2,1)} %bitcast.68, bf16[256,1024]{1,0:T(8,128)(2,1)} %bitcast.69, ...), custom_call_target="tpu_custom_call" | custom-call | flops 1000 | bytes 1000 | tf_op jit(solution)/shard_map/attend_2_3/pallas_call | solution.py:225
  122.8 13.8 %all-to-all-start.3 = ((bf16[32,8,1024]{2,1,0:T(8,128)(2,1)}), bf16[32,8,1024]{2,1,0:T(8,128)(2,1)S(1)}, u32[]{:S(2)}, u32[]{:S(2)}) async-start(bf16[32,8,1024]{2,1,0:T(8,128)(2,1)} %bitcast.74), calls=%async_computation.3 | async-start | bytes 1048576 | tf_op jit(solution)/shard_map/all_to_all | solution.py:347
  136.6 0.8 bitcast_dynamic-update-slice_fusion
  137.4 2.2 %collective-permute-start.11 = (bf16[64,1024]{1,0:T(8,128)(2,1)}, bf16[64,1024]{1,0:T(8,128)(2,1)S(1)}, u32[]{:S(2)}, u32[]{:S(2)}) collective-permute-start(bf16[64,1024]{1,0:T(8,128)(2,1)} %get-tuple-element.22), channel_id=1, source_target_pairs={{0,2},{1,3},{2,4},{3,5},{4,6},{5,7},{6,0},{7,1},{8,10},{9,11},{10,... | collective-permute-start | bytes 393224 | tf_op jit(solution)/shard_map/ppermute | solution.py:415
  139.6 5.1 %collective-permute-start.12 = (bf16[64,1024]{1,0:T(8,128)(2,1)}, bf16[64,1024]{1,0:T(8,128)(2,1)S(1)}, u32[]{:S(2)}, u32[]{:S(2)}) collective-permute-start(bf16[64,1024]{1,0:T(8,128)(2,1)} %get-tuple-element.23), channel_id=1, source_target_pairs={{0,4},{1,5},{2,6},{3,7},{4,0},{5,1},{6,2},{7,3},{8,12},{9,13},{10,... | collective-permute-start | bytes 393224 | tf_op jit(solution)/shard_map/ppermute | solution.py:415
  144.8 2.2 %collective-permute-start.13 = (bf16[64,1024]{1,0:T(8,128)(2,1)}, bf16[64,1024]{1,0:T(8,128)(2,1)S(1)}, u32[]{:S(2)}, u32[]{:S(2)}) collective-permute-start(bf16[64,1024]{1,0:T(8,128)(2,1)} %get-tuple-element.24), channel_id=1, source_target_pairs={{0,6},{1,7},{2,0},{3,1},{4,2},{5,3},{6,4},{7,5},{8,14},{9,15},{10,... | collective-permute-start | bytes 393224 | tf_op jit(solution)/shard_map/ppermute | solution.py:415
  147.0 11.2 %attend_1.1.x_ref = bf16[256,1024]{1,0:T(8,128)(2,1)} custom-call(s32[13]{0:T(128)} %concatenate.12.scalar_ref, bf16[256,1024]{1,0:T(8,128)(2,1)} %norm.1.refs_0_, bf16[4,256,512]{2,1,0:T(8,128)(2,1)} %copy-done.6, bf16[4,256,512]{2,1,0:T(8,128)(2,1)} %collective-permute-done.4.refs_2_.refs_3_.refs_1_, ...), custom_call_target="tpu_custom_call" | custom-call | flops 10000000000 | bytes 1000 | tf_op jit(solution)/shard_map/attend_1/pallas_call | solution.py:225
  158.2 0.0 collective-permute-done.13
  158.2 0.0 collective-permute-done.11
  158.3 3.3 %collective-permute-start.14 = (bf16[4,16,1024]{2,1,0:T(8,128)(2,1)S(1)}, bf16[4,16,1024]{2,1,0:T(8,128)(2,1)S(1)}, u32[]{:S(2)}, u32[]{:S(2)}) collective-permute-start(bf16[4,16,1024]{2,1,0:T(8,128)(2,1)S(1)} %pad_maximum_fusion.2), channel_id=1, source_target_pairs={{0,1},{1,0},{2,3},{3,2},{4,5},{5,4},{6,7},{7,6},{8,9},{9,8},{10,11... | collective-permute-start | bytes 393224 | tf_op jit(solution)/shard_map/ppermute | solution.py:351
  161.6 1.9 %collective-permute-start.16 = (bf16[4,16,1024]{2,1,0:T(8,128)(2,1)S(1)}, bf16[4,16,1024]{2,1,0:T(8,128)(2,1)S(1)}, u32[]{:S(2)}, u32[]{:S(2)}) collective-permute-start(bf16[4,16,1024]{2,1,0:T(8,128)(2,1)S(1)} %pad_maximum_fusion.3), channel_id=1, source_target_pairs={{0,1},{1,0},{2,3},{3,2},{4,5},{5,4},{6,7},{7,6},{8,9},{9,8},{10,11... | collective-permute-start | bytes 393224 | tf_op jit(solution)/shard_map/ppermute | solution.py:351
  163.7 2.3 %collective-permute-start.15 = (bf16[8,16,1024]{2,1,0:T(8,128)(2,1)S(1)}, bf16[8,16,1024]{2,1,0:T(8,128)(2,1)S(1)}, u32[]{:S(2)}, u32[]{:S(2)}) collective-permute-start(bf16[8,16,1024]{2,1,0:T(8,128)(2,1)S(1)} %constant_dynamic-update-slice_fusion), channel_id=1, source_target_pairs={{0,8},{8,0},{1,9},{9,1},{2,10},{10,2},{3,11},{11,3},{4,12},{12,4},... | collective-permute-start | bytes 786440 | tf_op jit(solution)/shard_map/ppermute | solution.py:351
  166.0 4.3 %gather_out.1.w_ref = bf16[1024,1024]{1,0:T(8,128)(2,1)} custom-call(s32[13]{0:T(128)} %concatenate.12.scalar_ref, bf16[4,256,512]{2,1,0:T(8,128)(2,1)} %copy-done.6, bf16[4,256,512]{2,1,0:T(8,128)(2,1)} %collective-permute-done.4.refs_2_.refs_3_.refs_1_, bf16[4,256,512]{2,1,0:T(8,128)(2,1)} %collective-permute-done.5.refs_3_.refs_4_.refs_2_, ...), custom_call_target="tpu_custom_call" | custom-call | flops 3000000000 | bytes 1000 | tf_op jit(solution)/shard_map/gather_out/pallas_call | solution.py:270
  170.4 1.6 copy-done.2
  171.9 1.0 mix_0.1.refs_0_
  172.9 0.1 collective-permute-done.15.parts_ref
  173.1 1.0 mix_1.1
  174.1 1.0 reshape.40
  (46 shorter events, 0.3 us)
Async XLA Ops:
  0.0 20.3 %copy-start.10 = (f32[16,127]{1,0:T(8,128)S(1)}, f32[16,127]{1,0:T(8,128)}, u32[]{:S(2)}) copy-start(f32[16,127]{1,0:T(8,128)} %param.10) | copy-start | bytes 24388
  0.0 21.8 %copy-start.11 = (f32[16,63]{1,0:T(8,128)S(1)}, f32[16,63]{1,0:T(8,128)}, u32[]{:S(2)}) copy-start(f32[16,63]{1,0:T(8,128)} %param.11) | copy-start | bytes 12100
  2.2 28.9 %all-to-all-start = ((bf16[16,16,512]{2,1,0:T(8,128)(2,1)}), bf16[16,16,512]{2,1,0:T(8,128)(2,1)S(1)}, u32[]{:S(2)}, u32[]{:S(2)}) async-start(bf16[16,16,512]{2,1,0:T(8,128)(2,1)} %broadcast_in_dim.2), calls=%async_computation | async-start | bytes 524288 | tf_op jit(solution)/shard_map/all_to_all | solution.py:347
  18.0 5.2 %copy-start.12 = (f32[16,63]{1,0:T(8,128)S(1)}, f32[16,63]{1,0:T(8,128)}, u32[]{:S(2)}) copy-start(f32[16,63]{1,0:T(8,128)} %param.12) | copy-start | bytes 12100
  20.8 1.0 copy-start.4
  22.2 1.0 copy-start
  23.6 1.0 copy-start.1
  31.1 46.0 %all-to-all-start.1 = ((bf16[32,8,1024]{2,1,0:T(8,128)(2,1)}), bf16[32,8,1024]{2,1,0:T(8,128)(2,1)S(1)}, u32[]{:S(2)}, u32[]{:S(2)}) async-start(bf16[32,8,1024]{2,1,0:T(8,128)(2,1)} %bitcast.13), calls=%async_computation.1 | async-start | bytes 1048576 | tf_op jit(solution)/shard_map/all_to_all | solution.py:347
  45.0 60.4 %copy-start.13 = (s32[4]{0:T(128)S(1)}, s32[4]{0:T(128)}, u32[]{:S(2)}) copy-start(s32[4]{0:T(128)} %constant.81) | copy-start | bytes 52
  45.0 3.9 %collective-permute-start = (bf16[128,512]{1,0:T(8,128)(2,1)S(1)}, bf16[128,512]{1,0:T(8,128)(2,1)S(1)}, u32[]{:S(2)}, u32[]{:S(2)}) collective-permute-start(bf16[128,512]{1,0:T(8,128)(2,1)S(1)} %broadcast_select_fusion.2), channel_id=1, source_target_pairs={{0,1},{1,0},{2,3},{3,2},{4,5},{5,4},{6,7},{7,6},{8,9},{9,8},{10,11... | collective-permute-start | bytes 393224 | tf_op jit(solution)/shard_map/ppermute | solution.py:351
  49.0 10.2 %collective-permute-start.3 = (bf16[256,512]{1,0:T(8,128)(2,1)S(1)}, bf16[256,512]{1,0:T(8,128)(2,1)S(1)}, u32[]{:S(2)}, u32[]{:S(2)}) collective-permute-start(bf16[256,512]{1,0:T(8,128)(2,1)S(1)} %bitcast.70), channel_id=1, source_target_pairs={{0,6},{1,265},{2,0},{3,267},{4,2},{5,269},{6,4},{7,271},{8,14},{9,... | collective-permute-start | bytes 786440 | tf_op jit(solution)/shard_map/ppermute | solution.py:395
  53.7 13.3 %collective-permute-start.2 = (bf16[256,512]{1,0:T(8,128)(2,1)S(1)}, bf16[256,512]{1,0:T(8,128)(2,1)S(1)}, u32[]{:S(2)}, u32[]{:S(2)}) collective-permute-start(bf16[256,512]{1,0:T(8,128)(2,1)S(1)} %bitcast.71), channel_id=1, source_target_pairs={{0,2},{1,9},{2,4},{3,11},{4,6},{5,13},{6,0},{7,15},{8,10},{9,257},... | collective-permute-start | bytes 786440 | tf_op jit(solution)/shard_map/ppermute | solution.py:395
  55.7 11.3 %collective-permute-start.1 = (bf16[256,512]{1,0:T(8,128)(2,1)S(1)}, bf16[256,512]{1,0:T(8,128)(2,1)S(1)}, u32[]{:S(2)}, u32[]{:S(2)}) collective-permute-start(bf16[256,512]{1,0:T(8,128)(2,1)S(1)} %bitcast.72), channel_id=1, source_target_pairs={{0,4},{1,257},{2,6},{3,259},{4,0},{5,261},{6,2},{7,263},{8,12},{9,... | collective-permute-start | bytes 786440 | tf_op jit(solution)/shard_map/ppermute | solution.py:395
  67.1 40.8 %copy-start.6 = (bf16[4,256,512]{2,1,0:T(8,128)(2,1)}, bf16[4,256,512]{2,1,0:T(8,128)(2,1)S(1)}, u32[]{:S(2)}) copy-start(bf16[4,256,512]{2,1,0:T(8,128)(2,1)S(1)} %pad_maximum_fusion.refs_1_.refs_2_.refs_0_) | copy-start | bytes 3145732
  67.1 18.0 %collective-permute-start.4 = (bf16[4,256,512]{2,1,0:T(8,128)(2,1)S(1)}, bf16[4,256,512]{2,1,0:T(8,128)(2,1)}, u32[]{:S(2)}, u32[]{:S(2)}) collective-permute-start(bf16[4,256,512]{2,1,0:T(8,128)(2,1)S(1)} %pad_maximum_fusion.refs_1_.refs_2_.refs_0_), channel_id=1, source_target_pairs={{0,8},{1,3},{2,10},{3,5},{4,12},{5,7},{6,14},{7,1},{8,256},{9,11},... | collective-permute-start | bytes 3145736 | tf_op jit(solution)/shard_map/ppermute | solution.py:397
  70.3 20.7 %collective-permute-start.6 = (bf16[4,256,512]{2,1,0:T(8,128)(2,1)S(1)}, bf16[4,256,512]{2,1,0:T(8,128)(2,1)}, u32[]{:S(2)}, u32[]{:S(2)}) collective-permute-start(bf16[4,256,512]{2,1,0:T(8,128)(2,1)S(1)} %pad_maximum_fusion.refs_1_.refs_2_.refs_0_), channel_id=1, source_target_pairs={{0,264},{1,7},{2,266},{3,1},{4,268},{5,3},{6,270},{7,5},{8,0},{9,1... | collective-permute-start | bytes 3145736 | tf_op jit(solution)/shard_map/ppermute | solution.py:397
  73.7 25.7 %collective-permute-start.5 = (bf16[4,256,512]{2,1,0:T(8,128)(2,1)S(1)}, bf16[4,256,512]{2,1,0:T(8,128)(2,1)}, u32[]{:S(2)}, u32[]{:S(2)}) collective-permute-start(bf16[4,256,512]{2,1,0:T(8,128)(2,1)S(1)} %pad_maximum_fusion.refs_1_.refs_2_.refs_0_), channel_id=1, source_target_pairs={{0,256},{1,5},{2,258},{3,7},{4,260},{5,1},{6,262},{7,3},{8,264},{9... | collective-permute-start | bytes 3145736 | tf_op jit(solution)/shard_map/ppermute | solution.py:397
  77.1 30.8 %copy-start.7 = (bf16[32,8,1024]{2,1,0:T(8,128)(2,1)}, bf16[32,8,1024]{2,1,0:T(8,128)(2,1)S(1)}, u32[]{:S(2)}) copy-start(bf16[32,8,1024]{2,1,0:T(8,128)(2,1)S(1)} %all-to-all-done.1) | copy-start | bytes 1572868
  77.1 25.9 %all-to-all-start.2 = ((bf16[16,16,1024]{2,1,0:T(8,128)(2,1)}), bf16[16,16,1024]{2,1,0:T(8,128)(2,1)S(1)}, u32[]{:S(2)}, u32[]{:S(2)}) async-start(bf16[16,16,1024]{2,1,0:T(8,128)(2,1)} %bitcast.15), calls=%async_computation.2 | async-start | bytes 1048576 | tf_op jit(solution)/shard_map/all_to_all | solution.py:347
  83.1 23.0 %collective-permute-start.7 = (bf16[4,256,512]{2,1,0:T(8,128)(2,1)S(1)}, bf16[4,256,512]{2,1,0:T(8,128)(2,1)}, u32[]{:S(2)}, u32[]{:S(2)}) collective-permute-start(bf16[4,256,512]{2,1,0:T(8,128)(2,1)S(1)} %pad_maximum_fusion.refs_1_.refs_2_.refs_0_), channel_id=1, source_target_pairs={{0,1},{1,0},{2,3},{3,2},{4,5},{5,4},{6,7},{7,6},{8,9},{9,8},{10,11... | collective-permute-start | bytes 3145736 | tf_op jit(solution)/shard_map/ppermute | solution.py:351
  85.1 20.9 %collective-permute-start.8 = (bf16[4,256,512]{2,1,0:T(8,128)(2,1)}, bf16[4,256,512]{2,1,0:T(8,128)(2,1)}, u32[]{:S(2)}, u32[]{:S(2)}) collective-permute-start(bf16[4,256,512]{2,1,0:T(8,128)(2,1)} %collective-permute-done.4.refs_2_.refs_3_.refs_1_), channel_id=1, source_target_pairs={{0,1},{1,0},{2,3},{3,2},{4,5},{5,4},{6,7},{7,6},{8,9},{9,8},{10,11... | collective-permute-start | bytes 3145736 | tf_op jit(solution)/shard_map/ppermute | solution.py:351
  90.9 15.1 %collective-permute-start.10 = (bf16[4,256,512]{2,1,0:T(8,128)(2,1)}, bf16[4,256,512]{2,1,0:T(8,128)(2,1)}, u32[]{:S(2)}, u32[]{:S(2)}) collective-permute-start(bf16[4,256,512]{2,1,0:T(8,128)(2,1)} %collective-permute-done.6.refs_4_.refs_5_.refs_3_), channel_id=1, source_target_pairs={{0,1},{1,0},{2,3},{3,2},{4,5},{5,4},{6,7},{7,6},{8,9},{9,8},{10,11... | collective-permute-start | bytes 3145736 | tf_op jit(solution)/shard_map/ppermute | solution.py:351
  103.0 4.9 %copy-start.8 = (bf16[16,16,1024]{2,1,0:T(8,128)(2,1)}, bf16[16,16,1024]{2,1,0:T(8,128)(2,1)S(1)}, u32[]{:S(2)}) copy-start(bf16[16,16,1024]{2,1,0:T(8,128)(2,1)S(1)} %all-to-all-done.2) | copy-start | bytes 1572868
  103.0 4.9 %collective-permute-start.9 = (bf16[4,256,512]{2,1,0:T(8,128)(2,1)}, bf16[4,256,512]{2,1,0:T(8,128)(2,1)}, u32[]{:S(2)}, u32[]{:S(2)}) collective-permute-start(bf16[4,256,512]{2,1,0:T(8,128)(2,1)} %collective-permute-done.5.refs_3_.refs_4_.refs_2_), channel_id=1, source_target_pairs={{0,1},{1,0},{2,3},{3,2},{4,5},{5,4},{6,7},{7,6},{8,9},{9,8},{10,11... | collective-permute-start | bytes 3145736 | tf_op jit(solution)/shard_map/ppermute | solution.py:351
  122.8 47.6 %all-to-all-start.3 = ((bf16[32,8,1024]{2,1,0:T(8,128)(2,1)}), bf16[32,8,1024]{2,1,0:T(8,128)(2,1)S(1)}, u32[]{:S(2)}, u32[]{:S(2)}) async-start(bf16[32,8,1024]{2,1,0:T(8,128)(2,1)} %bitcast.74), calls=%async_computation.3 | async-start | bytes 1048576 | tf_op jit(solution)/shard_map/all_to_all | solution.py:347
  137.4 20.9 %collective-permute-start.11 = (bf16[64,1024]{1,0:T(8,128)(2,1)}, bf16[64,1024]{1,0:T(8,128)(2,1)S(1)}, u32[]{:S(2)}, u32[]{:S(2)}) collective-permute-start(bf16[64,1024]{1,0:T(8,128)(2,1)} %get-tuple-element.22), channel_id=1, source_target_pairs={{0,2},{1,3},{2,4},{3,5},{4,6},{5,7},{6,0},{7,1},{8,10},{9,11},{10,... | collective-permute-start | bytes 393224 | tf_op jit(solution)/shard_map/ppermute | solution.py:415
  139.6 18.6 %collective-permute-start.12 = (bf16[64,1024]{1,0:T(8,128)(2,1)}, bf16[64,1024]{1,0:T(8,128)(2,1)S(1)}, u32[]{:S(2)}, u32[]{:S(2)}) collective-permute-start(bf16[64,1024]{1,0:T(8,128)(2,1)} %get-tuple-element.23), channel_id=1, source_target_pairs={{0,4},{1,5},{2,6},{3,7},{4,0},{5,1},{6,2},{7,3},{8,12},{9,13},{10,... | collective-permute-start | bytes 393224 | tf_op jit(solution)/shard_map/ppermute | solution.py:415
  144.7 13.4 %copy-start.9 = (bf16[64,1024]{1,0:T(8,128)(2,1)S(1)}, bf16[64,1024]{1,0:T(8,128)(2,1)}, u32[]{:S(2)}) copy-start(bf16[64,1024]{1,0:T(8,128)(2,1)} %get-tuple-element.21.refs_8_) | copy-start | bytes 393220
  144.8 13.4 %collective-permute-start.13 = (bf16[64,1024]{1,0:T(8,128)(2,1)}, bf16[64,1024]{1,0:T(8,128)(2,1)S(1)}, u32[]{:S(2)}, u32[]{:S(2)}) collective-permute-start(bf16[64,1024]{1,0:T(8,128)(2,1)} %get-tuple-element.24), channel_id=1, source_target_pairs={{0,6},{1,7},{2,0},{3,1},{4,2},{5,3},{6,4},{7,5},{8,14},{9,15},{10,... | collective-permute-start | bytes 393224 | tf_op jit(solution)/shard_map/ppermute | solution.py:415
  158.3 5.3 %collective-permute-start.14 = (bf16[4,16,1024]{2,1,0:T(8,128)(2,1)S(1)}, bf16[4,16,1024]{2,1,0:T(8,128)(2,1)S(1)}, u32[]{:S(2)}, u32[]{:S(2)}) collective-permute-start(bf16[4,16,1024]{2,1,0:T(8,128)(2,1)S(1)} %pad_maximum_fusion.2), channel_id=1, source_target_pairs={{0,1},{1,0},{2,3},{3,2},{4,5},{5,4},{6,7},{7,6},{8,9},{9,8},{10,11... | collective-permute-start | bytes 393224 | tf_op jit(solution)/shard_map/ppermute | solution.py:351
  161.6 8.7 %collective-permute-start.16 = (bf16[4,16,1024]{2,1,0:T(8,128)(2,1)S(1)}, bf16[4,16,1024]{2,1,0:T(8,128)(2,1)S(1)}, u32[]{:S(2)}, u32[]{:S(2)}) collective-permute-start(bf16[4,16,1024]{2,1,0:T(8,128)(2,1)S(1)} %pad_maximum_fusion.3), channel_id=1, source_target_pairs={{0,1},{1,0},{2,3},{3,2},{4,5},{5,4},{6,7},{7,6},{8,9},{9,8},{10,11... | collective-permute-start | bytes 393224 | tf_op jit(solution)/shard_map/ppermute | solution.py:351
  163.6 6.7 %copy-start.3 = (bf16[256,1024]{1,0:T(8,128)(2,1)S(1)}, bf16[256,1024]{1,0:T(8,128)(2,1)}, u32[]{:S(2)}) copy-start(bf16[256,1024]{1,0:T(8,128)(2,1)} %attend_1.1.x_ref) | copy-start | bytes 1572868
  163.6 6.7 %copy-start.5 = (s32[13]{0:T(128)S(1)}, s32[13]{0:T(128)}, u32[]{:S(2)}) copy-start(s32[13]{0:T(128)} %concatenate.12.scalar_ref) | copy-start | bytes 160
  163.7 9.4 %collective-permute-start.15 = (bf16[8,16,1024]{2,1,0:T(8,128)(2,1)S(1)}, bf16[8,16,1024]{2,1,0:T(8,128)(2,1)S(1)}, u32[]{:S(2)}, u32[]{:S(2)}) collective-permute-start(bf16[8,16,1024]{2,1,0:T(8,128)(2,1)S(1)} %constant_dynamic-update-slice_fusion), channel_id=1, source_target_pairs={{0,8},{8,0},{1,9},{9,1},{2,10},{10,2},{3,11},{11,3},{4,12},{12,4},... | collective-permute-start | bytes 786440 | tf_op jit(solution)/shard_map/ppermute | solution.py:351
  170.3 1.6 copy-start.2
